TPU v7x, 32 devices: a whole 2x2x4 slice. The times are simulated.
32 devices in a mesh: img: 16 (over z, y, x), rep: 2 (over core).
Axes of the slice: x: 2, y: 2, z: 4, core: 2. Of those that a mesh axis runs over, the one named last changes fastest.
Arguments:
- panels: float32 [32, 512, 128], P('img', 'rep'), may hold values from -6 to 6
- blocks: bfloat16 [768, 512, 512], P('img', None, 'rep'), may hold values from -0.25 to 0.25
- pairs: int32 [768, 2], P('img'), may hold values from 0 to 31, as said below
- counts: int32 [16], P('img'), may hold values from 12 to 48, as said below
Outputs:
- basis: float32 [32, 512, 128], P('img', 'rep')
Inputs may be any that keep to these rules, and one draw needn't show every extreme that they name: `pairs`: row d * 48 + s is slot s of index d of img: its first image is one of d * 2 to d * 2 + 1, its second image lies on one of the indices d + 1 to d + 8 modulo 16. At most 6 slots of one index name second images on one other index, and that many is reached. `counts`: some index of img has all 48 slots live.
All inputs are finite; a program needn't handle non-finite values.
Results may differ from a plain program's by a relative error of at most 0.0025.
The roundings to bfloat16 on the way count: a program that leaves them out, or rounds other values in their place, can miss the bound.
Values may be sent and summed in bfloat16 or wider, within the bound.
No kernel may reach another device: no remote copies, remote signals or barrier semaphores. Data moves between devices by JAX's collectives and lax.ppermute only.
A program may use at most 128 MiB of HBM per device.

v0:
```python
import jax
import jax.numpy as jnp
from jax import lax
from jax.sharding import PartitionSpec as P

BAND = 8


def passed_along(value, axis, steps):
    count = lax.axis_size(axis)
    pairs = [(source, (source + steps) % count) for source in range(count)]
    return lax.ppermute(value, axis, pairs)


def shards(panels, blocks, pairs, counts):
    devices = lax.axis_size("img")
    own_index = lax.axis_index("img")
    img_dev = panels.shape[0]
    half_rows = panels.shape[1]
    univ_cols = panels.shape[2]
    pair_dev = blocks.shape[0]
    keypts = blocks.shape[1]
    band_width = BAND
    capacity = pair_dev // band_width
    buffer_rows = band_width * capacity
    rounded = panels.astype(jnp.bfloat16)
    own_full = lax.all_gather(rounded, "rep", axis=1, tiled=True)
    live_count = counts[0]
    slot_ids = jnp.arange(pair_dev)
    alive = slot_ids < live_count
    first_local = jnp.clip(pairs[:, 0] - own_index * img_dev, 0, img_dev - 1)
    peers = pairs[:, 1] // img_dev
    second_local = pairs[:, 1] - peers * img_dev
    offsets = (peers - own_index - 1) % devices
    peer_hits = ((offsets[:, None] == jnp.arange(band_width)[None, :]) & alive[:, None]).astype(
        jnp.int32
    )
    ranks = jnp.sum(jnp.cumsum(peer_hits, axis=0) * peer_hits, axis=1) - 1
    targets = jnp.where(alive, offsets * capacity + ranks, buffer_rows)
    slot_hits = (targets[:, None] == jnp.arange(buffer_rows)[None, :]).astype(jnp.int32)
    asking = (jnp.sum(slot_hits * (second_local + 1)[:, None], axis=0) - 1).reshape(
        band_width, capacity
    )
    incoming = jnp.stack(
        [passed_along(asking[step], "img", step + 1) for step in range(band_width)]
    )
    incoming_flat = incoming.reshape(buffer_rows)
    every_panel = lax.all_gather(rounded, "img", axis=0, tiled=True)
    second_panels = every_panel[pairs[:, 1]]
    first_panels = own_full[first_local]
    group_width = 8

    def one_group(group, carry):
        forward, reverse = carry
        start = group * group_width
        block_rows = lax.dynamic_slice_in_dim(blocks, start, group_width, 0)
        far_rows = lax.dynamic_slice_in_dim(second_panels, start, group_width, 0)
        near_rows = lax.dynamic_slice_in_dim(first_panels, start, group_width, 0)
        alive_rows = lax.dynamic_slice_in_dim(alive, start, group_width, 0)
        owners = lax.dynamic_slice_in_dim(first_local, start, group_width, 0)
        products = jnp.einsum(
            "skh,shn->skn", block_rows, far_rows, preferred_element_type=jnp.float32
        )
        weights = ((owners[None, :] == jnp.arange(img_dev)[:, None]) & alive_rows[None, :]).astype(
            jnp.float32
        )
        forward = forward + jnp.sum(weights[:, :, None, None] * products[None], axis=1)
        turned = jnp.einsum(
            "skh,skn->shn", block_rows, near_rows, preferred_element_type=jnp.float32
        ).astype(jnp.bfloat16)
        reverse = lax.dynamic_update_slice_in_dim(reverse, turned, start, 0)
        return (forward, reverse)

    initial = (
        jnp.zeros((img_dev, keypts, univ_cols), jnp.float32),
        jnp.zeros((pair_dev, half_rows, univ_cols), jnp.bfloat16),
    )
    forward, reverse = lax.fori_loop(
        0, (live_count + group_width - 1) // group_width, one_group, initial
    )
    outgoing = (
        jnp.zeros((buffer_rows, half_rows, univ_cols), jnp.bfloat16)
        .at[targets]
        .set(reverse, mode="drop")
    )
    outgoing = outgoing.reshape(band_width, capacity, half_rows, univ_cols)
    received = jnp.concatenate(
        [passed_along(outgoing[step], "img", step + 1) for step in range(band_width)], axis=0
    )
    image_pick = (incoming_flat[None, :] == jnp.arange(img_dev)[:, None]).astype(jnp.bfloat16)
    returned_sum = jnp.einsum(
        "ir,rkn->ikn", image_pick, received, preferred_element_type=jnp.float32
    )
    forward_half = lax.psum_scatter(forward, "rep", scatter_dimension=1, tiled=True)
    field = panels + forward_half + returned_sum
    gram_local = jnp.einsum(
        "ikn,ikm->nm",
        field,
        field,
        precision=lax.Precision.HIGHEST,
        preferred_element_type=jnp.float32,
    )
    gram_matrix = lax.psum(gram_local, ("img", "rep"))
    gram_matrix = gram_matrix / (devices * img_dev * keypts)
    factor = jnp.linalg.cholesky(gram_matrix)
    stacked = field.reshape(img_dev * half_rows, univ_cols)
    basis = lax.linalg.triangular_solve(
        factor, stacked, left_side=False, lower=True, transpose_a=True
    )
    return basis.reshape(img_dev, half_rows, univ_cols)


def solution(mesh):
    in_specs = (P("img", "rep", None), P("img", None, "rep"), P("img", None), P("img"))
    out_specs = P("img", "rep", None)
    return jax.shard_map(shards, mesh=mesh, in_specs=in_specs, out_specs=out_specs, check_vma=False)
```

profile of v0, /device:TPU:0, one launch (start us, length us, event | category | flops | bytes accessed | tf_op | source)
XLA Modules:
  0.0 474.5 jit_solution(9418180184608264308)
XLA Ops:
  9.9 2.4 all_gather.7
  12.2 4.8 %gather_fusion.1 = bf16[48,512,128]{2,1,0:T(8,128)(2,1)} fusion(bf16[2,512,128]{2,1,0:T(8,128)(2,1)S(1)} %all_gather.7, s32[1024]{0:T(1024)S(1)} %get-tuple-element.106), kind=kCustom, calls=%fused_computation.1 | custom fusion | bytes 12583104 | tf_op jit(solution)/shard_map/gather | solution.py:50
  17.4 56.2 %all-gather.2.cloned.1.call-done = bf16[32,256,128]{2,1,0:T(8,128)(2,1)} async-done(((bf16[2,256,128]{2,1,0:T(8,128)(2,1)}), bf16[32,256,128]{2,1,0:T(8,128)(2,1)}) %all-gather.2.cloned.1.call-update) | async-done | bytes 2097168 | tf_op jit(solution)/shard_map/all_gather | solution.py:48
  73.6 4.3 gather_fusion
  77.9 2.4 broadcast.186.clone
  80.3 13.0 %while.12 = (s32[]{:T(128)}, f32[2,512,128]{2,1,0:T(8,128)S(1)}, bf16[48,256,128]{2,1,0:T(8,128)(2,1)}, s32[]{:T(128)}, s32[48]{0:T(128)S(1)}, /*index=5*/pred[4...) while((s32[]{:T(128)}, f32[2,512,128]{2,1,0:T(8,128)S(1)}, ...), condition=%wide.region_2.3_spmd, body=%wide.region_0.2_spmd.sunk | while | flops 539230272 | bytes 12585899 | solution.py:78
  80.5 2.4 fusion.44
  83.4 3.5 fusion.45
  87.0 2.4 fusion.44
  89.9 3.5 fusion.45
  94.9 5.7 %scatter_fusion = bf16[48,256,128]{2,1,0:T(8,128)(2,1)S(1)} fusion(bf16[48,256,128]{2,1,0:T(8,128)(2,1)S(1)} %broadcast.186, s32[48]{0:T(128)S(1)} %get-tuple-element.85, bf16[48,256,128]{2,1,0:T(8,128)(2,1)} %get-tuple-element.55), kind=kCustom, calls=%fused_computation.2 | custom fusion | bytes 9437376 | tf_op jit(solution)/shard_map/scatter | solution.py:84
  101.3 27.5 %collective-permute-start.10 = (bf16[6,256,128]{2,0,1:T(8,128)(2,1)S(1)}, bf16[6,256,128]{2,0,1:T(8,128)(2,1)}, u32[]{:S(2)}, u32[]{:S(2)}) collective-permute-start(bf16[6,256,128]{2,0,1:T(8,128)(2,1)S(1)} %copy.91), channel_id=1, source_target_pairs={{0,6},{2,8},{4,10},{6,12},{8,14},{10,16},{12,18},{14,20},{16,22},{... | collective-permute-start | bytes 1179656 | tf_op jit(solution)/shard_map/ppermute | solution.py:12
  129.7 3.1 collective-permute-start.2
  132.8 3.5 collective-permute-start.3
  140.1 15.8 %collective-permute-done.2 = s32[6]{0:T(128)S(1)} collective-permute-done((s32[6]{0:T(128)S(1)}, s32[6]{0:T(128)S(1)}, u32[]{:S(2)}, u32[]{:S(2)}) %collective-permute-start.2) | collective-permute-done | bytes 56 | tf_op jit(solution)/shard_map/ppermute | solution.py:12
  155.9 4.5 collective-permute-start.4
  160.4 3.9 collective-permute-start.5
  164.3 4.7 collective-permute-done.4
  168.9 11.5 %collective-permute-start.6 = (s32[6]{0:T(128)S(1)}, s32[6]{0:T(128)S(1)}, u32[]{:S(2)}, u32[]{:S(2)}) collective-permute-start(s32[6]{0:T(128)S(1)} %get-tuple-element.99), channel_id=1, source_target_pairs={{0,14},{2,16},{4,18},{6,20},{8,22},{10,24},{12,26},{14,28},{16,30}... | collective-permute-start | bytes 80 | tf_op jit(solution)/shard_map/ppermute | solution.py:12
  180.5 2.7 collective-permute-start.7
  183.2 3.0 collective-permute-start
  187.3 3.2 collective-permute-done
  190.4 2.2 collective-permute-done.1
  192.8 19.8 %collective-permute-start.15 = (bf16[6,256,128]{2,0,1:T(8,128)(2,1)}, bf16[6,256,128]{2,0,1:T(8,128)(2,1)S(1)}, u32[]{:S(2)}, u32[]{:S(2)}) collective-permute-start(bf16[6,256,128]{2,0,1:T(8,128)(2,1)} %copy.96), channel_id=1, source_target_pairs={{0,16},{2,18},{4,20},{6,22},{8,24},{10,26},{12,28},{14,30},{16,0},... | collective-permute-start | bytes 1179656 | tf_op jit(solution)/shard_map/ppermute | solution.py:12
  212.6 7.0 %collective-permute-start.8 = (bf16[6,256,128]{2,0,1:T(8,128)(2,1)S(1)}, bf16[6,256,128]{2,0,1:T(8,128)(2,1)S(1)}, u32[]{:S(2)}, u32[]{:S(2)}) collective-permute-start(bf16[6,256,128]{2,0,1:T(8,128)(2,1)S(1)} %copy.89), channel_id=1, source_target_pairs={{0,2},{2,4},{4,6},{6,8},{8,10},{10,12},{12,14},{14,16},{16,18},{18... | collective-permute-start | bytes 1179656 | tf_op jit(solution)/shard_map/ppermute | solution.py:12
  223.4 27.5 %collective-permute-done.13 = bf16[6,256,128]{2,0,1:T(8,128)(2,1)S(1)} collective-permute-done((bf16[6,256,128]{2,0,1:T(8,128)(2,1)}, bf16[6,256,128]{2,0,1:T(8,128)(2,1)S(1)}, u32[]{:S(2)}, u32[]{:S(2)}) %collective-permute-start.13) | collective-permute-done | bytes 393248 | tf_op jit(solution)/shard_map/ppermute | solution.py:12
  253.0 39.1 %concatenate.3 = bf16[48,256,128]{2,0,1:T(8,128)(2,1)S(1)} concatenate(bf16[6,256,128]{2,0,1:T(8,128)(2,1)} %copy-done.5, bf16[6,256,128]{2,0,1:T(8,128)(2,1)} %collective-permute-done.9, bf16[6,256,128]{2,0,1:T(8,128)(2,1)} %collective-permute-done.10, bf16[6,256,128]{2,0,1:T(8,128)(2,1)} %collective-permute-done.11, bf16[6,256,128]{2,0,1:T(8,128)(2,1)} %collective-permute-done.12, ...), dimensions={0} | concatenate | bytes 6291456 | tf_op jit(solution)/shard_map/concatenate | solution.py:87
  293.6 2.3 convolution_bitcast_fusion
  295.9 145.4 %all-reduce.4.cloned.1.call-done = f32[128,128]{0,1:T(8,128)} async-done(((f32[128,128]{0,1:T(8,128)}), f32[128,128]{0,1:T(8,128)}) %all-reduce.4.cloned.1.call-update) | async-done | bytes 65552 | tf_op jit(solution)/shard_map/psum | solution.py:103
  443.1 11.7 %cholesky.16 = f32[128,128]{1,0:T(8,128)S(1)} custom-call(f32[128,128]{1,0:T(8,128)S(1)} %fusion.17), custom_call_target="Cholesky" | custom-call | tf_op jit(solution)/shard_map/jit(cholesky)/cholesky | solution.py:105
  456.1 9.8 %custom-call.6 = f32[1,128,128]{1,2,0:T(8,128)S(1)} custom-call(f32[1,128,128]{2,1,0:T(8,128)S(1)} %fusion.14), custom_call_target="InvertDiagBlocksLowerTriangular" | custom-call | tf_op jit(solution)/shard_map/triangular_solve | solution.py:107
  466.0 2.0 fusion.15
  (83 shorter events, 22.1 us)
Async XLA Ops:
  6.5 67.0 %all-gather.2.cloned.1.call-start = ((), (), s32[]{:S(2)}) async-start(), calls=%async_computation | async-start | bytes 2228224 | tf_op jit(solution)/shard_map/all_gather | solution.py:48
  8.2 284.4 %all-reduce.6.cloned.1.call-start = ((), (), s32[]{:S(2)}) async-start(), calls=%async_computation.2 | async-start | bytes 1048576
  93.4 0.8 copy-start
  101.3 91.5 %collective-permute-start.10 = (bf16[6,256,128]{2,0,1:T(8,128)(2,1)S(1)}, bf16[6,256,128]{2,0,1:T(8,128)(2,1)}, u32[]{:S(2)}, u32[]{:S(2)}) collective-permute-start(bf16[6,256,128]{2,0,1:T(8,128)(2,1)S(1)} %copy.91), channel_id=1, source_target_pairs={{0,6},{2,8},{4,10},{6,12},{8,14},{10,16},{12,18},{14,20},{16,22},{... | collective-permute-start | bytes 1179656 | tf_op jit(solution)/shard_map/ppermute | solution.py:12
  128.8 91.8 %copy-start.1 = (f32[2,512,128]{2,1,0:T(8,128)S(1)}, f32[2,512,128]{2,1,0:T(8,128)}, u32[]{:S(2)}) copy-start(f32[2,512,128]{2,1,0:T(8,128)} %copy-done) | copy-start | bytes 1572868
  129.1 83.5 %collective-permute-start.11 = (bf16[6,256,128]{2,0,1:T(8,128)(2,1)S(1)}, bf16[6,256,128]{2,0,1:T(8,128)(2,1)}, u32[]{:S(2)}, u32[]{:S(2)}) collective-permute-start(bf16[6,256,128]{2,0,1:T(8,128)(2,1)S(1)} %copy.92), channel_id=1, source_target_pairs={{0,8},{2,10},{4,12},{6,14},{8,16},{10,18},{12,20},{14,22},{16,24},... | collective-permute-start | bytes 1179656 | tf_op jit(solution)/shard_map/ppermute | solution.py:12
  129.5 92.6 %copy-start.6 = (u32[32]{0:T(128)S(1)}, u32[32]{0:T(128)}, u32[]{:S(2)}) copy-start(u32[32]{0:T(128)} %constant.131) | copy-start | bytes 388
  129.5 90.0 %collective-permute-start.12 = (bf16[6,256,128]{2,0,1:T(8,128)(2,1)S(1)}, bf16[6,256,128]{2,0,1:T(8,128)(2,1)}, u32[]{:S(2)}, u32[]{:S(2)}) collective-permute-start(bf16[6,256,128]{2,0,1:T(8,128)(2,1)S(1)} %copy.93), channel_id=1, source_target_pairs={{0,10},{2,12},{4,14},{6,16},{8,18},{10,20},{12,22},{14,24},{16,26}... | collective-permute-start | bytes 1179656 | tf_op jit(solution)/shard_map/ppermute | solution.py:12
  129.7 26.2 %collective-permute-start.2 = (s32[6]{0:T(128)S(1)}, s32[6]{0:T(128)S(1)}, u32[]{:S(2)}, u32[]{:S(2)}) collective-permute-start(s32[6]{0:T(128)S(1)} %get-tuple-element.103), channel_id=1, source_target_pairs={{0,6},{2,8},{4,10},{6,12},{8,14},{10,16},{12,18},{14,20},{16,22},{... | collective-permute-start | bytes 80 | tf_op jit(solution)/shard_map/ppermute | solution.py:12
  132.8 27.6 %collective-permute-start.3 = (s32[6]{0:T(128)S(1)}, s32[6]{0:T(128)S(1)}, u32[]{:S(2)}, u32[]{:S(2)}) collective-permute-start(s32[6]{0:T(128)S(1)} %get-tuple-element.102), channel_id=1, source_target_pairs={{0,8},{2,10},{4,12},{6,14},{8,16},{10,18},{12,20},{14,22},{16,24},... | collective-permute-start | bytes 80 | tf_op jit(solution)/shard_map/ppermute | solution.py:12
  155.9 13.0 %collective-permute-start.4 = (s32[6]{0:T(128)S(1)}, s32[6]{0:T(128)S(1)}, u32[]{:S(2)}, u32[]{:S(2)}) collective-permute-start(s32[6]{0:T(128)S(1)} %get-tuple-element.101), channel_id=1, source_target_pairs={{0,10},{2,12},{4,14},{6,16},{8,18},{10,20},{12,22},{14,24},{16,26}... | collective-permute-start | bytes 80 | tf_op jit(solution)/shard_map/ppermute | solution.py:12
  160.4 20.1 %collective-permute-start.5 = (s32[6]{0:T(128)S(1)}, s32[6]{0:T(128)S(1)}, u32[]{:S(2)}, u32[]{:S(2)}) collective-permute-start(s32[6]{0:T(128)S(1)} %get-tuple-element.100), channel_id=1, source_target_pairs={{0,12},{2,14},{4,16},{6,18},{8,20},{10,22},{12,24},{14,26},{16,28}... | collective-permute-start | bytes 80 | tf_op jit(solution)/shard_map/ppermute | solution.py:12
  168.9 14.2 %collective-permute-start.6 = (s32[6]{0:T(128)S(1)}, s32[6]{0:T(128)S(1)}, u32[]{:S(2)}, u32[]{:S(2)}) collective-permute-start(s32[6]{0:T(128)S(1)} %get-tuple-element.99), channel_id=1, source_target_pairs={{0,14},{2,16},{4,18},{6,20},{8,22},{10,24},{12,26},{14,28},{16,30}... | collective-permute-start | bytes 80 | tf_op jit(solution)/shard_map/ppermute | solution.py:12
  180.5 5.7 %collective-permute-start.7 = (s32[6]{0:T(128)S(1)}, s32[6]{0:T(128)S(1)}, u32[]{:S(2)}, u32[]{:S(2)}) collective-permute-start(s32[6]{0:T(128)S(1)} %get-tuple-element.98), channel_id=1, source_target_pairs={{0,16},{2,18},{4,20},{6,22},{8,24},{10,26},{12,28},{14,30},{16,0},... | collective-permute-start | bytes 80 | tf_op jit(solution)/shard_map/ppermute | solution.py:12
  183.2 7.2 %collective-permute-start = (s32[6]{0:T(128)S(1)}, s32[6]{0:T(128)S(1)}, u32[]{:S(2)}, u32[]{:S(2)}) collective-permute-start(s32[6]{0:T(128)S(1)} %get-tuple-element.105), channel_id=1, source_target_pairs={{0,2},{2,4},{4,6},{6,8},{8,10},{10,12},{12,14},{14,16},{16,18},{18... | collective-permute-start | bytes 80 | tf_op jit(solution)/shard_map/ppermute | solution.py:12
  186.2 6.4 %collective-permute-start.1 = (s32[6]{0:T(128)S(1)}, s32[6]{0:T(128)S(1)}, u32[]{:S(2)}, u32[]{:S(2)}) collective-permute-start(s32[6]{0:T(128)S(1)} %get-tuple-element.104), channel_id=1, source_target_pairs={{0,4},{2,6},{4,8},{6,10},{8,12},{10,14},{12,16},{14,18},{16,20},{1... | collective-permute-start | bytes 80 | tf_op jit(solution)/shard_map/ppermute | solution.py:12
  190.4 60.5 %collective-permute-start.13 = (bf16[6,256,128]{2,0,1:T(8,128)(2,1)}, bf16[6,256,128]{2,0,1:T(8,128)(2,1)S(1)}, u32[]{:S(2)}, u32[]{:S(2)}) collective-permute-start(bf16[6,256,128]{2,0,1:T(8,128)(2,1)} %copy.94), channel_id=1, source_target_pairs={{0,12},{2,14},{4,16},{6,18},{8,20},{10,22},{12,24},{14,26},{16,28}... | collective-permute-start | bytes 1179656 | tf_op jit(solution)/shard_map/ppermute | solution.py:12
  192.6 58.4 %collective-permute-start.14 = (bf16[6,256,128]{2,0,1:T(8,128)(2,1)}, bf16[6,256,128]{2,0,1:T(8,128)(2,1)S(1)}, u32[]{:S(2)}, u32[]{:S(2)}) collective-permute-start(bf16[6,256,128]{2,0,1:T(8,128)(2,1)} %copy.95), channel_id=1, source_target_pairs={{0,14},{2,16},{4,18},{6,20},{8,22},{10,24},{12,26},{14,28},{16,30}... | collective-permute-start | bytes 1179656 | tf_op jit(solution)/shard_map/ppermute | solution.py:12
  192.8 58.2 %collective-permute-start.15 = (bf16[6,256,128]{2,0,1:T(8,128)(2,1)}, bf16[6,256,128]{2,0,1:T(8,128)(2,1)S(1)}, u32[]{:S(2)}, u32[]{:S(2)}) collective-permute-start(bf16[6,256,128]{2,0,1:T(8,128)(2,1)} %copy.96), channel_id=1, source_target_pairs={{0,16},{2,18},{4,20},{6,22},{8,24},{10,26},{12,28},{14,30},{16,0},... | collective-permute-start | bytes 1179656 | tf_op jit(solution)/shard_map/ppermute | solution.py:12
  212.6 38.4 %collective-permute-start.8 = (bf16[6,256,128]{2,0,1:T(8,128)(2,1)S(1)}, bf16[6,256,128]{2,0,1:T(8,128)(2,1)S(1)}, u32[]{:S(2)}, u32[]{:S(2)}) collective-permute-start(bf16[6,256,128]{2,0,1:T(8,128)(2,1)S(1)} %copy.89), channel_id=1, source_target_pairs={{0,2},{2,4},{4,6},{6,8},{8,10},{10,12},{12,14},{14,16},{16,18},{18... | collective-permute-start | bytes 1179656 | tf_op jit(solution)/shard_map/ppermute | solution.py:12
  219.6 33.4 %collective-permute-start.9 = (bf16[6,256,128]{2,0,1:T(8,128)(2,1)S(1)}, bf16[6,256,128]{2,0,1:T(8,128)(2,1)}, u32[]{:S(2)}, u32[]{:S(2)}) collective-permute-start(bf16[6,256,128]{2,0,1:T(8,128)(2,1)S(1)} %copy.90), channel_id=1, source_target_pairs={{0,4},{2,6},{4,8},{6,10},{8,12},{10,14},{12,16},{14,18},{16,20},{1... | collective-permute-start | bytes 1179656 | tf_op jit(solution)/shard_map/ppermute | solution.py:12
  221.8 219.5 %all-reduce.4.cloned.1.call-start = ((), (), s32[]{:S(2)}) async-start(), calls=%async_computation.1 | async-start | bytes 131072 | tf_op jit(solution)/shard_map/psum | solution.py:103
  251.0 0.8 copy-start.2
  251.0 1.0 copy-start.3
  251.0 1.2 copy-start.4
  252.2 0.8 copy-start.5
Sparse Core Ops, SparseCore 0:
  10.1 63.3 all-gather.1
  222.0 20.0 all-reduce.5
  296.0 145.2 all-reduce.3
where the time goes:
time: 480 us; the launch traced here: 475 us
  waiting for transfers between devices  255 us (53%)
  starting transfers between devices  89.3 us (19%)
  local copies, waits for them, and re-layouts  68.2 us (14%)
  other arithmetic  28.4 us (6%)
  matrix products  16.5 us (3%)
  between operations  14.6 us (3%)
    psum x1, waiting for transfers between devices, shards(): gram_matrix = lax.psum(gram_local, ('img', 'rep'))  145 us
    ppermute x16, starting transfers between devices, passed_along(): return lax.ppermute(value, axis, pairs)  89.1 us
    all_gather x1, waiting for transfers between devices, shards(): every_panel = lax.all_gather(rounded, 'img', axis=0, tiled=True)  56.2 us
    ppermute x16, waiting for transfers between devices, passed_along(): return lax.ppermute(value, axis, pairs)  53.3 us
    concatenate x1, local copies, waits for them, and re-layouts, shards(): jnp.concatenate([passed_along(outgoing[step], 'img', step + 1) for step i...  39.1 us
    another operation x3, other arithmetic, shards(): factor = jnp.linalg.cholesky(gram_matrix)  12.4 us
    another operation x2, other arithmetic, shards(): lax.linalg.triangular_solve(factor, stacked, left_side=False, lower=True,...  10.5 us
  transfers between devices with their start and end apart: 19, of which 7 were waited for; matrix products, arithmetic and copies ran while one was open for 11% of the time, Pallas kernels for 0%

commit v1 on v0

v1 whole, which is shorter than its diff:
```python
import functools

import jax
import jax.numpy as jnp
from jax import lax
from jax.experimental import pallas as pl
from jax.experimental.pallas import tpu as pltpu
from jax.sharding import PartitionSpec as P

BAND = 8
GROUP = BAND // 2
SMEM = pl.BlockSpec(memory_space=pltpu.SMEM)
VMEM = pl.BlockSpec(memory_space=pltpu.VMEM)


def passed_along(value, axis, steps):
    count = lax.axis_size(axis)
    pairs = [(source, (source + steps) % count) for source in range(count)]
    return lax.ppermute(value, axis, pairs)


def exchanged(value, axis, bits):
    count = lax.axis_size(axis)
    return lax.ppermute(value, axis, [(source, source ^ bits) for source in range(count)])


def entry(second, own_index, devices, img_dev):
    owner = lax.div(second, img_dev)
    image = second - owner * img_dev
    member = lax.rem(owner, GROUP)
    own_member = lax.rem(own_index, GROUP)
    groups = devices // GROUP
    hop = lax.rem(lax.div(owner, GROUP) - lax.div(own_index, GROUP) + groups, groups)
    turn = hop - jnp.where(member <= own_member, 1, 0)
    return ((member ^ own_member) * 2 + turn) * img_dev + image


def reverse_kernel(per, devices, place, count, pairs, near, far, blocks, *rest):
    outs, (turned, total) = rest[:GROUP], rest[GROUP:]
    own_index, core = place[0], place[1]
    img_dev, half = near.shape[0], near.shape[1]
    units = 2 * img_dev
    near_rows = pl.ds(pl.multiple_of(core * half, half), half)
    far_rows = pl.ds(pl.multiple_of((1 - core) * half, half), half)
    for image in range(img_dev):
        turned[0, image] = near[image].T
        turned[1, image] = far[image].T
    total[...] = jnp.zeros_like(total)

    @pl.loop(0, (count[0] + per - 1) // per)
    def _(step):
        for part in range(per):
            slot = step * per + part
            place_in = entry(pairs[slot, 1], own_index, devices, img_dev)
            place_in = jnp.where(slot < count[0], place_in, GROUP * units)
            first = pairs[slot, 0] - own_index * img_dev
            product = jnp.dot(
                turned[0, first], blocks[slot, near_rows], preferred_element_type=jnp.float32
            )
            product += jnp.dot(
                turned[1, first], blocks[slot, far_rows], preferred_element_type=jnp.float32
            )
            total[place_in] += product.astype(jnp.bfloat16).astype(jnp.float32)

    for member in range(GROUP):
        for unit in range(units):
            outs[member][unit] = total[member * units + unit].astype(jnp.bfloat16).T


def forward_kernel(per, devices, place, count, pairs, panels, *rest):
    tables, blocks, own, send, table, total = rest[:GROUP], *rest[GROUP:]
    own_index, core = place[0], place[1]
    img_dev, half = panels.shape[0], panels.shape[1]
    units = 2 * img_dev
    for member in range(GROUP):
        table[pl.ds(member * units, units)] = tables[member][...]
    total[...] = jnp.zeros_like(total)

    @pl.loop(0, (count[0] + per - 1) // per)
    def _(step):
        for part in range(per):
            slot = step * per + part
            place_in = entry(pairs[slot, 1], own_index, devices, img_dev)
            place_in = jnp.clip(place_in, 0, GROUP * units - 1)
            first = pairs[slot, 0] - own_index * img_dev
            first = jnp.where(slot < count[0], first, img_dev)
            total[first] += jnp.dot(
                blocks[slot], table[place_in], preferred_element_type=jnp.float32
            )

    for image in range(img_dev):
        near_rows = pl.ds(pl.multiple_of(core * half, half), half)
        far_rows = pl.ds(pl.multiple_of((1 - core) * half, half), half)
        own[image] = panels[image] + total[image, near_rows]
        send[image] = total[image, far_rows]


def shards(panels, blocks, pairs, counts):
    devices = lax.axis_size("img")
    own_index = lax.axis_index("img")
    core = lax.axis_index("rep")
    member = own_index % GROUP
    img_dev, half, univ = panels.shape
    slots, keypts, cols = blocks.shape
    units = 2 * img_dev
    per = next(width for width in (8, 6, 4, 3, 2, 1) if slots % width == 0)
    place = jnp.stack([own_index, core]).astype(jnp.int32)
    limit = pltpu.CompilerParams(vmem_limit_bytes=40 << 20)
    work = pl.CostEstimate(
        flops=2 * slots * keypts * cols * univ,
        bytes_accessed=slots * keypts * cols * 2,
        transcendentals=0,
    )

    near = panels.astype(jnp.bfloat16)
    far = exchanged(near, "rep", 1)
    ahead = [near, passed_along(near, "img", -GROUP), passed_along(near, "img", -2 * GROUP)]

    returns = pl.pallas_call(
        functools.partial(reverse_kernel, per, devices),
        in_specs=[SMEM] * 3 + [VMEM] * 3,
        out_specs=[VMEM] * GROUP,
        out_shape=[jax.ShapeDtypeStruct((units, cols, univ), jnp.bfloat16)] * GROUP,
        scratch_shapes=[
            pltpu.VMEM((2, img_dev, univ, half), jnp.bfloat16),
            pltpu.VMEM((GROUP * units + 1, univ, cols), jnp.float32),
        ],
        compiler_params=limit,
        cost_estimate=work,
        name="reverse",
    )(place, counts, pairs, near, far, blocks)

    tables = [jnp.concatenate(ahead[1:])]
    for bits in range(1, GROUP):
        later = member > (member ^ bits)
        sent = jnp.where(later, jnp.concatenate(ahead[:2]), jnp.concatenate(ahead[1:]))
        tables.append(exchanged(sent, "img", bits))

    arrived = [returns[0]] + [exchanged(returns[bits], "img", bits) for bits in range(1, GROUP)]
    sums = [jnp.zeros((img_dev, cols, univ), jnp.float32) for _ in range(3)]
    for bits in range(GROUP):
        first_unit = arrived[bits][:img_dev].astype(jnp.float32)
        second_unit = arrived[bits][img_dev:].astype(jnp.float32)
        earlier = (member ^ bits) < member
        sums[0] += jnp.where(earlier, first_unit, 0)
        sums[1] += jnp.where(earlier, second_unit, first_unit)
        sums[2] += jnp.where(earlier, 0, second_unit)
    back = [
        passed_along(sums[hop].astype(jnp.bfloat16), "img", hop * GROUP) for hop in (1, 2)
    ]

    own, send = pl.pallas_call(
        functools.partial(forward_kernel, per, devices),
        in_specs=[SMEM] * 3 + [VMEM] * (GROUP + 2),
        out_specs=[VMEM] * 2,
        out_shape=[jax.ShapeDtypeStruct((img_dev, half, univ), jnp.float32)] * 2,
        scratch_shapes=[
            pltpu.VMEM((GROUP * units, cols, univ), jnp.bfloat16),
            pltpu.VMEM((img_dev + 1, keypts, univ), jnp.float32),
        ],
        compiler_params=limit,
        cost_estimate=work,
        name="forward",
    )(place, counts, pairs, panels, *tables, blocks)
    other_half = exchanged(send, "rep", 1)

    field = own + other_half + sums[0] + back[0].astype(jnp.float32) + back[1].astype(jnp.float32)
    gram = jnp.einsum(
        "ikn,ikm->nm",
        field,
        field,
        precision=lax.Precision.HIGHEST,
        preferred_element_type=jnp.float32,
    )
    gram = gram + exchanged(gram, "rep", 1)
    bits = 1
    while bits < devices:
        gram = gram + exchanged(gram, "img", bits)
        bits *= 2
    gram = gram / (devices * img_dev * keypts)
    factor = jnp.linalg.cholesky(gram)
    stacked = field.reshape(img_dev * half, univ)
    basis = lax.linalg.triangular_solve(
        factor, stacked, left_side=False, lower=True, transpose_a=True
    )
    return basis.reshape(img_dev, half, univ)


def solution(mesh):
    in_specs = (P("img", "rep", None), P("img", None, "rep"), P("img", None), P("img"))
    out_specs = P("img", "rep", None)
    return jax.shard_map(shards, mesh=mesh, in_specs=in_specs, out_specs=out_specs, check_vma=False)
```

time: 480 us -> 100 us (0.21); the launches traced: 475 us -> 101 us
  waiting for transfers between devices: 255 us -> 36 us
  starting transfers between devices: 89.3 us -> 18 us
  local copies, waits for them, and re-layouts: 68.2 us -> 10 us
  matrix products: 16.5 us -> 1.66 us
  between operations: 14.6 us -> 0.81 us
  Pallas kernels: 0 us -> 8.99 us
    psum x1 -> x0, waiting for transfers between devices: 145 us -> none  [shards(): gram_matrix = lax.psum(gram_local, ('img', 'rep'))]
    ppermute x16 -> x4, starting transfers between devices: 89.1 us -> 9.75 us  [passed_along(): return lax.ppermute(value, axis, pairs)]
    all_gather x1 -> x0, waiting for transfers between devices: 56.2 us -> none  [shards(): every_panel = lax.all_gather(rounded, 'img', axis=0, tiled=True)]
    concatenate x1, local copies, waits for them, and re-layouts: 39.1 us -> 0.02 us  [shards(): tables = [jnp.concatenate(ahead[1:])]]
    ppermute x16 -> x4, waiting for transfers between devices: 53.3 us -> 16.1 us  [passed_along(): return lax.ppermute(value, axis, pairs)]
    ppermute x0 -> x13, waiting for transfers between devices: none -> 19.8 us  [exchanged(): lax.ppermute(value, axis, [(source, source ^ bits) for source in range(co...]
    dot_general x5 -> x0, matrix products: 12.2 us -> none  [the longest x2 6.94 us: one_group(): jnp.einsum('skh,skn->shn', block_rows, near_rows, preferred_element_type=...]
    gather x2 -> x0, local copies, waits for them, and re-layouts: 9.17 us -> none  [the longest x1 4.82 us: shards(): first_panels = own_full[first_local]]
  transfers between devices with their start and end apart: 19 -> 17, of which waited for: 7 -> 10; matrix products, arithmetic and copies ran while one was open for 11% -> 2% of each run, Pallas kernels for 0% -> 9%
where the time goes in v1:
time: 100 us; the launch traced here: 101 us
  waiting for transfers between devices  36 us (36%)
  other arithmetic  25.2 us (25%)
  starting transfers between devices  18 us (18%)
  local copies, waits for them, and re-layouts  10 us (10%)
  Pallas kernels  8.99 us (9%)
  matrix products  1.66 us (2%)
    ppermute x13, waiting for transfers between devices, exchanged(): lax.ppermute(value, axis, [(source, source ^ bits) for source in range(co...  19.8 us
    ppermute x4, waiting for transfers between devices, passed_along(): return lax.ppermute(value, axis, pairs)  16.1 us
    another operation x3, other arithmetic, shards(): factor = jnp.linalg.cholesky(gram)  12.4 us
    another operation x2, other arithmetic, shards(): lax.linalg.triangular_solve(factor, stacked, left_side=False, lower=True,...  10.5 us
    unnamed x8, local copies, waits for them, and re-layouts  9.93 us
    ppermute x4, starting transfers between devices, passed_along(): return lax.ppermute(value, axis, pairs)  9.75 us
    ppermute x13, starting transfers between devices, exchanged(): lax.ppermute(value, axis, [(source, source ^ bits) for source in range(co...  8.23 us
    pallas_call x1, Pallas kernels, shards(): pl.pallas_call(functools.partial(forward_kernel, per, devices), in_specs=...  5.05 us
  transfers between devices with their start and end apart: 17, of which 10 were waited for; matrix products, arithmetic and copies ran while one was open for 2% of the time, Pallas kernels for 9%

profile of v1, /device:TPU:0, one launch (start us, length us, event | category | flops | bytes accessed | tf_op | source)
XLA Modules:
  0.0 100.6 jit_solution(9578609037573988444)
XLA Ops:
  0.0 1.0 %convert_element_type.49.near = bf16[2,256,128]{2,1,0:T(8,128)(2,1)S(1)} convert(f32[2,256,128]{2,1,0:T(8,128)} %panels.1) | non-fusion elementwise | flops 65536 | bytes 393216 | tf_op jit(solution)/shard_map/convert_element_type | solution.py:115
  1.0 5.1 %collective-permute-start = (bf16[2,256,128]{2,1,0:T(8,128)(2,1)S(1)}, bf16[2,256,128]{2,1,0:T(8,128)(2,1)S(1)}, u32[]{:S(2)}, u32[]{:S(2)}) collective-permute-start(bf16[2,256,128]{2,1,0:T(8,128)(2,1)S(1)} %convert_element_type.49.near), channel_id=1, source_target_pairs={{0,24},{2,26},{4,28},{6,30},{8,0},{10,2},{12,4},{14,6},{16,8},{18,... | collective-permute-start | bytes 393224 | tf_op jit(solution)/shard_map/ppermute | solution.py:19
  6.8 0.8 copy.5.pairs
  7.6 2.5 %collective-permute-done = bf16[2,256,128]{2,1,0:T(8,128)(2,1)S(1)} collective-permute-done((bf16[2,256,128]{2,1,0:T(8,128)(2,1)S(1)}, bf16[2,256,128]{2,1,0:T(8,128)(2,1)S(1)}, u32[]{:S(2)}, u32[]{:S(2)}) %collective-permute-start) | collective-permute-done | bytes 131104 | tf_op jit(solution)/shard_map/ppermute | solution.py:19
  10.1 4.5 %collective-permute-done.1 = bf16[2,256,128]{2,1,0:T(8,128)(2,1)S(1)} collective-permute-done((bf16[2,256,128]{2,1,0:T(8,128)(2,1)S(1)}, bf16[2,256,128]{2,1,0:T(8,128)(2,1)S(1)}, u32[]{:S(2)}, u32[]{:S(2)}) %collective-permute-start.1) | collective-permute-done | bytes 131104 | tf_op jit(solution)/shard_map/ppermute | solution.py:19
  14.6 0.9 broadcast_select_fusion
  15.4 2.4 %collective-permute-start.4 = (bf16[4,256,128]{2,1,0:T(8,128)(2,1)S(1)}, bf16[4,256,128]{2,1,0:T(8,128)(2,1)S(1)}, u32[]{:S(2)}, u32[]{:S(2)}) collective-permute-start(bf16[4,256,128]{2,1,0:T(8,128)(2,1)S(1)} %get-tuple-element.19), channel_id=1, source_target_pairs={{0,6},{2,4},{4,2},{6,0},{8,14},{10,12},{12,10},{14,8},{16,22},{18,... | collective-permute-start | bytes 786440 | tf_op jit(solution)/shard_map/ppermute | solution.py:24
  17.9 0.5 collective-permute-start.3
  18.5 0.5 collective-permute-start.2
  19.0 4.6 %copy-done = bf16[48,512,256]{2,1,0:T(8,128)(2,1)S(1)} copy-done((bf16[48,512,256]{2,1,0:T(8,128)(2,1)S(1)}, bf16[48,512,256]{2,1,0:T(8,128)(2,1)}, u32[]{:S(2)}) %copy-start) | copy-done | bytes 12582936
  23.6 3.9 %reverse.1 = (bf16[4,256,128]{2,1,0:T(8,128)(2,1)S(1)}, bf16[4,256,128]{2,1,0:T(8,128)(2,1)S(1)}, bf16[4,256,128]{2,1,0:T(8,128)(2,1)S(1)}, bf16[4,256,128]{2,1,0:T(8,128)(2,1)S(1)}) custom-call(s32[2]{0:T(128)S(1)} %pad_add_fusion.place, s32[1]{0:T(128)S(6)} %copy.19.count, s32[48,2]{1,0:T(8,128)S(1)} %copy.5.pairs, ...), custom_call_target="tpu_custom_call" | custom-call | flops 1610612736 | bytes 12582912 | tf_op jit(solution)/shard_map/reverse/pallas_call | solution.py:119
  27.5 2.1 %collective-permute-start.7 = (bf16[4,256,128]{2,1,0:T(8,128)(2,1)S(1)}, bf16[4,256,128]{2,1,0:T(8,128)(2,1)S(1)}, u32[]{:S(2)}, u32[]{:S(2)}) collective-permute-start(bf16[4,256,128]{2,1,0:T(8,128)(2,1)S(1)} %get-tuple-element.13), channel_id=1, source_target_pairs={{0,2},{2,0},{4,6},{6,4},{8,10},{10,8},{12,14},{14,12},{16,18},{18,... | collective-permute-start | bytes 786440 | tf_op jit(solution)/shard_map/ppermute | solution.py:24
  29.6 1.0 %collective-permute-start.8 = (bf16[4,256,128]{2,1,0:T(8,128)(2,1)S(1)}, bf16[4,256,128]{2,1,0:T(8,128)(2,1)S(1)}, u32[]{:S(2)}, u32[]{:S(2)}) collective-permute-start(bf16[4,256,128]{2,1,0:T(8,128)(2,1)S(1)} %get-tuple-element.14), channel_id=1, source_target_pairs={{0,4},{2,6},{4,0},{6,2},{8,12},{10,14},{12,8},{14,10},{16,20},{18,... | collective-permute-start | bytes 786440 | tf_op jit(solution)/shard_map/ppermute | solution.py:24
  30.6 0.5 collective-permute-start.9
  31.1 4.6 %copy-done.1 = bf16[48,512,256]{2,1,0:T(8,128)(2,1)S(1)} copy-done((bf16[48,512,256]{2,1,0:T(8,128)(2,1)S(1)}, bf16[48,512,256]{2,1,0:T(8,128)(2,1)}, u32[]{:S(2)}) %copy-start.1) | copy-done | bytes 12582936
  35.7 5.0 %forward.1 = (f32[2,256,128]{2,1,0:T(8,128)S(1)}, f32[2,256,128]{2,1,0:T(8,128)S(1)}) custom-call(s32[2]{0:T(128)S(1)} %pad_add_fusion.place, s32[1]{0:T(128)S(6)} %copy.19.count, s32[48,2]{1,0:T(8,128)S(1)} %copy.5.pairs, f32[2,256,128]{2,1,0:T(8,128)S(1)} %copy-done.2, bf16[4,256,128]{2,1,0:T(8,128)(2,1)S(1)} %constant_dynamic-update-slice_fusion.rest_0_, ...), custom_call_target="tpu_custom_call" | custom-call | flops 1610612736 | bytes 12582912 | tf_op jit(solution)/shard_map/forward/pallas_call | solution.py:152
  40.8 0.8 collective-permute-done.8
  42.0 4.5 %collective-permute-start.11 = (bf16[2,256,128]{2,1,0:T(8,128)(2,1)S(1)}, bf16[2,256,128]{2,1,0:T(8,128)(2,1)S(1)}, u32[]{:S(2)}, u32[]{:S(2)}) collective-permute-start(bf16[2,256,128]{2,1,0:T(8,128)(2,1)S(1)} %get-tuple-element.18), channel_id=1, source_target_pairs={{0,16},{2,18},{4,20},{6,22},{8,24},{10,26},{12,28},{14,30},{16,0},... | collective-permute-start | bytes 393224 | tf_op jit(solution)/shard_map/ppermute | solution.py:19
  46.5 3.9 %collective-permute-done.10 = bf16[2,256,128]{2,1,0:T(8,128)(2,1)S(1)} collective-permute-done((bf16[2,256,128]{2,1,0:T(8,128)(2,1)S(1)}, bf16[2,256,128]{2,1,0:T(8,128)(2,1)S(1)}, u32[]{:S(2)}, u32[]{:S(2)}) %collective-permute-start.10) | collective-permute-done | bytes 131104 | tf_op jit(solution)/shard_map/ppermute | solution.py:19
  50.4 5.3 %collective-permute-done.11 = bf16[2,256,128]{2,1,0:T(8,128)(2,1)S(1)} collective-permute-done((bf16[2,256,128]{2,1,0:T(8,128)(2,1)S(1)}, bf16[2,256,128]{2,1,0:T(8,128)(2,1)S(1)}, u32[]{:S(2)}, u32[]{:S(2)}) %collective-permute-start.11) | collective-permute-done | bytes 131104 | tf_op jit(solution)/shard_map/ppermute | solution.py:19
  55.8 0.6 convolution_bitcast_fusion
  56.5 1.2 %collective-permute-done.12 = f32[128,128]{0,1:T(8,128)S(1)} collective-permute-done((f32[128,128]{0,1:T(8,128)S(1)}, f32[128,128]{0,1:T(8,128)S(1)}, u32[]{:S(2)}, u32[]{:S(2)}) %collective-permute-start.12) | collective-permute-done | bytes 65568 | tf_op jit(solution)/shard_map/ppermute | solution.py:24
  57.7 0.7 collective-permute-start.13
  58.5 3.6 %collective-permute-done.13 = f32[128,128]{0,1:T(8,128)S(1)} collective-permute-done((f32[128,128]{0,1:T(8,128)S(1)}, f32[128,128]{0,1:T(8,128)S(1)}, u32[]{:S(2)}, u32[]{:S(2)}) %collective-permute-start.13) | collective-permute-done | bytes 65568 | tf_op jit(solution)/shard_map/ppermute | solution.py:24
  62.2 4.3 %collective-permute-done.14 = f32[128,128]{0,1:T(8,128)S(1)} collective-permute-done((f32[128,128]{0,1:T(8,128)S(1)}, f32[128,128]{0,1:T(8,128)S(1)}, u32[]{:S(2)}, u32[]{:S(2)}) %collective-permute-start.14) | collective-permute-done | bytes 65568 | tf_op jit(solution)/shard_map/ppermute | solution.py:24
  66.5 4.3 %collective-permute-done.15 = f32[128,128]{0,1:T(8,128)S(1)} collective-permute-done((f32[128,128]{0,1:T(8,128)S(1)}, f32[128,128]{0,1:T(8,128)S(1)}, u32[]{:S(2)}, u32[]{:S(2)}) %collective-permute-start.15) | collective-permute-done | bytes 65568 | tf_op jit(solution)/shard_map/ppermute | solution.py:24
  70.8 5.7 %collective-permute-done.16 = f32[128,128]{0,1:T(8,128)S(1)} collective-permute-done((f32[128,128]{0,1:T(8,128)S(1)}, f32[128,128]{0,1:T(8,128)S(1)}, u32[]{:S(2)}, u32[]{:S(2)}) %collective-permute-start.16) | collective-permute-done | bytes 65568 | tf_op jit(solution)/shard_map/ppermute | solution.py:24
  76.7 11.7 %cholesky.16 = f32[128,128]{1,0:T(8,128)S(1)} custom-call(f32[128,128]{1,0:T(8,128)S(1)} %fusion.16), custom_call_target="Cholesky" | custom-call | tf_op jit(solution)/shard_map/jit(cholesky)/cholesky | solution.py:181
  88.5 0.6 compare_reduce_fusion
  89.1 0.7 fusion.13
  89.8 9.8 %custom-call.6 = f32[1,128,128]{1,2,0:T(8,128)S(1)} custom-call(f32[1,128,128]{2,1,0:T(8,128)S(1)} %fusion.13), custom_call_target="InvertDiagBlocksLowerTriangular" | custom-call | tf_op jit(solution)/shard_map/triangular_solve | solution.py:183
  99.6 1.1 %fusion.14 = f32[2,256,128]{2,1,0:T(8,128)} fusion(f32[2,256,128]{2,1,0:T(8,128)S(1)} %fusion.4, f32[1,128,128]{1,2,0:T(8,128)S(1)} %custom-call.6), kind=kOutput, calls=%fused_computation.29 | convolution fusion | flops 100663296 | bytes 589824 | tf_op jit(solution)/shard_map/triangular_solve | solution.py:183
  (32 shorter events, 1.2 us)
Async XLA Ops:
  0.0 31.1 %copy-start.2 = (f32[2,256,128]{2,1,0:T(8,128)S(1)}, f32[2,256,128]{2,1,0:T(8,128)}, u32[]{:S(2)}) copy-start(f32[2,256,128]{2,1,0:T(8,128)} %panels.1) | copy-start | bytes 786436
  1.0 9.0 %collective-permute-start = (bf16[2,256,128]{2,1,0:T(8,128)(2,1)S(1)}, bf16[2,256,128]{2,1,0:T(8,128)(2,1)S(1)}, u32[]{:S(2)}, u32[]{:S(2)}) collective-permute-start(bf16[2,256,128]{2,1,0:T(8,128)(2,1)S(1)} %convert_element_type.49.near), channel_id=1, source_target_pairs={{0,24},{2,26},{4,28},{6,30},{8,0},{10,2},{12,4},{14,6},{16,8},{18,... | collective-permute-start | bytes 393224 | tf_op jit(solution)/shard_map/ppermute | solution.py:19
  6.1 8.4 %collective-permute-start.1 = (bf16[2,256,128]{2,1,0:T(8,128)(2,1)S(1)}, bf16[2,256,128]{2,1,0:T(8,128)(2,1)S(1)}, u32[]{:S(2)}, u32[]{:S(2)}) collective-permute-start(bf16[2,256,128]{2,1,0:T(8,128)(2,1)S(1)} %convert_element_type.49.near), channel_id=1, source_target_pairs={{0,16},{2,18},{4,20},{6,22},{8,24},{10,26},{12,28},{14,30},{16,0},... | collective-permute-start | bytes 393224 | tf_op jit(solution)/shard_map/ppermute | solution.py:19
  6.2 12.8 %collective-permute-start.6 = (bf16[2,256,128]{2,1,0:T(8,128)(2,1)S(1)}, bf16[2,256,128]{2,1,0:T(8,128)(2,1)S(1)}, u32[]{:S(2)}, u32[]{:S(2)}) collective-permute-start(bf16[2,256,128]{2,1,0:T(8,128)(2,1)S(1)} %convert_element_type.49.near), channel_id=1, source_target_pairs={{0,1},{1,0},{2,3},{3,2},{4,5},{5,4},{6,7},{7,6},{8,9},{9,8},{10,11... | collective-permute-start | bytes 393224 | tf_op jit(solution)/shard_map/ppermute | solution.py:24
  15.4 15.2 %collective-permute-start.4 = (bf16[4,256,128]{2,1,0:T(8,128)(2,1)S(1)}, bf16[4,256,128]{2,1,0:T(8,128)(2,1)S(1)}, u32[]{:S(2)}, u32[]{:S(2)}) collective-permute-start(bf16[4,256,128]{2,1,0:T(8,128)(2,1)S(1)} %get-tuple-element.19), channel_id=1, source_target_pairs={{0,6},{2,4},{4,2},{6,0},{8,14},{10,12},{12,10},{14,8},{16,22},{18,... | collective-permute-start | bytes 786440 | tf_op jit(solution)/shard_map/ppermute | solution.py:24
  17.9 13.2 %collective-permute-start.3 = (bf16[4,256,128]{2,1,0:T(8,128)(2,1)}, bf16[4,256,128]{2,1,0:T(8,128)(2,1)S(1)}, u32[]{:S(2)}, u32[]{:S(2)}) collective-permute-start(bf16[4,256,128]{2,1,0:T(8,128)(2,1)} %get-tuple-element.20), channel_id=1, source_target_pairs={{0,4},{2,6},{4,0},{6,2},{8,12},{10,14},{12,8},{14,10},{16,20},{18,... | collective-permute-start | bytes 786440 | tf_op jit(solution)/shard_map/ppermute | solution.py:24
  18.5 12.7 %collective-permute-start.2 = (bf16[4,256,128]{2,1,0:T(8,128)(2,1)}, bf16[4,256,128]{2,1,0:T(8,128)(2,1)S(1)}, u32[]{:S(2)}, u32[]{:S(2)}) collective-permute-start(bf16[4,256,128]{2,1,0:T(8,128)(2,1)} %get-tuple-element.21), channel_id=1, source_target_pairs={{0,2},{2,0},{4,6},{6,4},{8,10},{10,8},{12,14},{14,12},{16,18},{18,... | collective-permute-start | bytes 786440 | tf_op jit(solution)/shard_map/ppermute | solution.py:24
  19.0 4.6 %copy-start = (bf16[48,512,256]{2,1,0:T(8,128)(2,1)S(1)}, bf16[48,512,256]{2,1,0:T(8,128)(2,1)}, u32[]{:S(2)}) copy-start(bf16[48,512,256]{2,1,0:T(8,128)(2,1)} %blocks.1) | copy-start | bytes 37748740
  27.5 13.3 %collective-permute-start.7 = (bf16[4,256,128]{2,1,0:T(8,128)(2,1)S(1)}, bf16[4,256,128]{2,1,0:T(8,128)(2,1)S(1)}, u32[]{:S(2)}, u32[]{:S(2)}) collective-permute-start(bf16[4,256,128]{2,1,0:T(8,128)(2,1)S(1)} %get-tuple-element.13), channel_id=1, source_target_pairs={{0,2},{2,0},{4,6},{6,4},{8,10},{10,8},{12,14},{14,12},{16,18},{18,... | collective-permute-start | bytes 786440 | tf_op jit(solution)/shard_map/ppermute | solution.py:24
  29.6 12.1 %collective-permute-start.8 = (bf16[4,256,128]{2,1,0:T(8,128)(2,1)S(1)}, bf16[4,256,128]{2,1,0:T(8,128)(2,1)S(1)}, u32[]{:S(2)}, u32[]{:S(2)}) collective-permute-start(bf16[4,256,128]{2,1,0:T(8,128)(2,1)S(1)} %get-tuple-element.14), channel_id=1, source_target_pairs={{0,4},{2,6},{4,0},{6,2},{8,12},{10,14},{12,8},{14,10},{16,20},{18,... | collective-permute-start | bytes 786440 | tf_op jit(solution)/shard_map/ppermute | solution.py:24
  30.6 11.0 %collective-permute-start.9 = (bf16[4,256,128]{2,1,0:T(8,128)(2,1)S(1)}, bf16[4,256,128]{2,1,0:T(8,128)(2,1)S(1)}, u32[]{:S(2)}, u32[]{:S(2)}) collective-permute-start(bf16[4,256,128]{2,1,0:T(8,128)(2,1)S(1)} %get-tuple-element.15), channel_id=1, source_target_pairs={{0,6},{2,4},{4,2},{6,0},{8,14},{10,12},{12,10},{14,8},{16,22},{18,... | collective-permute-start | bytes 786440 | tf_op jit(solution)/shard_map/ppermute | solution.py:24
  31.1 4.6 %copy-start.1 = (bf16[48,512,256]{2,1,0:T(8,128)(2,1)S(1)}, bf16[48,512,256]{2,1,0:T(8,128)(2,1)}, u32[]{:S(2)}) copy-start(bf16[48,512,256]{2,1,0:T(8,128)(2,1)} %blocks.1) | copy-start | bytes 37748740
  40.8 14.9 %collective-permute-start.5 = (f32[2,256,128]{2,1,0:T(8,128)S(1)}, f32[2,256,128]{2,1,0:T(8,128)S(1)}, u32[]{:S(2)}, u32[]{:S(2)}) collective-permute-start(f32[2,256,128]{2,1,0:T(8,128)S(1)} %get-tuple-element.12), channel_id=1, source_target_pairs={{0,1},{1,0},{2,3},{3,2},{4,5},{5,4},{6,7},{7,6},{8,9},{9,8},{10,11... | collective-permute-start | bytes 786440 | tf_op jit(solution)/shard_map/ppermute | solution.py:24
  41.8 8.5 %collective-permute-start.10 = (bf16[2,256,128]{2,1,0:T(8,128)(2,1)S(1)}, bf16[2,256,128]{2,1,0:T(8,128)(2,1)S(1)}, u32[]{:S(2)}, u32[]{:S(2)}) collective-permute-start(bf16[2,256,128]{2,1,0:T(8,128)(2,1)S(1)} %get-tuple-element.17), channel_id=1, source_target_pairs={{0,8},{2,10},{4,12},{6,14},{8,16},{10,18},{12,20},{14,22},{16,24},... | collective-permute-start | bytes 393224 | tf_op jit(solution)/shard_map/ppermute | solution.py:19
  42.0 13.7 %collective-permute-start.11 = (bf16[2,256,128]{2,1,0:T(8,128)(2,1)S(1)}, bf16[2,256,128]{2,1,0:T(8,128)(2,1)S(1)}, u32[]{:S(2)}, u32[]{:S(2)}) collective-permute-start(bf16[2,256,128]{2,1,0:T(8,128)(2,1)S(1)} %get-tuple-element.18), channel_id=1, source_target_pairs={{0,16},{2,18},{4,20},{6,22},{8,24},{10,26},{12,28},{14,30},{16,0},... | collective-permute-start | bytes 393224 | tf_op jit(solution)/shard_map/ppermute | solution.py:19
  56.4 1.3 %collective-permute-start.12 = (f32[128,128]{0,1:T(8,128)S(1)}, f32[128,128]{0,1:T(8,128)S(1)}, u32[]{:S(2)}, u32[]{:S(2)}) collective-permute-start(f32[128,128]{0,1:T(8,128)S(1)} %convolution_bitcast_fusion), channel_id=1, source_target_pairs={{0,1},{1,0},{2,3},{3,2},{4,5},{5,4},{6,7},{7,6},{8,9},{9,8},{10,11... | collective-permute-start | bytes 196616 | tf_op jit(solution)/shard_map/ppermute | solution.py:24
  57.7 4.3 %collective-permute-start.13 = (f32[128,128]{0,1:T(8,128)S(1)}, f32[128,128]{0,1:T(8,128)S(1)}, u32[]{:S(2)}, u32[]{:S(2)}) collective-permute-start(f32[128,128]{0,1:T(8,128)S(1)} %add.80), channel_id=1, source_target_pairs={{0,2},{2,0},{4,6},{6,4},{8,10},{10,8},{12,14},{14,12},{16,18},{18,... | collective-permute-start | bytes 196616 | tf_op jit(solution)/shard_map/ppermute | solution.py:24
  62.1 4.3 %collective-permute-start.14 = (f32[128,128]{0,1:T(8,128)S(1)}, f32[128,128]{0,1:T(8,128)S(1)}, u32[]{:S(2)}, u32[]{:S(2)}) collective-permute-start(f32[128,128]{0,1:T(8,128)S(1)} %add.81), channel_id=1, source_target_pairs={{0,4},{2,6},{4,0},{6,2},{8,12},{10,14},{12,8},{14,10},{16,20},{18,... | collective-permute-start | bytes 196616 | tf_op jit(solution)/shard_map/ppermute | solution.py:24
  66.4 4.3 %collective-permute-start.15 = (f32[128,128]{0,1:T(8,128)S(1)}, f32[128,128]{0,1:T(8,128)S(1)}, u32[]{:S(2)}, u32[]{:S(2)}) collective-permute-start(f32[128,128]{0,1:T(8,128)S(1)} %add.82), channel_id=1, source_target_pairs={{0,8},{2,10},{4,12},{6,14},{8,0},{10,2},{12,4},{14,6},{16,24},{18,... | collective-permute-start | bytes 196616 | tf_op jit(solution)/shard_map/ppermute | solution.py:24
  70.8 5.8 %collective-permute-start.16 = (f32[128,128]{0,1:T(8,128)S(1)}, f32[128,128]{0,1:T(8,128)S(1)}, u32[]{:S(2)}, u32[]{:S(2)}) collective-permute-start(f32[128,128]{0,1:T(8,128)S(1)} %add.83), channel_id=1, source_target_pairs={{0,16},{2,18},{4,20},{6,22},{8,24},{10,26},{12,28},{14,30},{16,0},... | collective-permute-start | bytes 196616 | tf_op jit(solution)/shard_map/ppermute | solution.py:24

commit v2 on v1

v2 whole, which is shorter than its diff:
```python
import functools

import jax
import jax.numpy as jnp
from jax import lax
from jax.experimental import pallas as pl
from jax.experimental.pallas import tpu as pltpu
from jax.sharding import PartitionSpec as P

BAND = 8
GROUP = BAND // 2
ROWS = 8
SMEM = pl.BlockSpec(memory_space=pltpu.SMEM)
VMEM = pl.BlockSpec(memory_space=pltpu.VMEM)
SHORT = pl.CostEstimate(flops=1, bytes_accessed=1, transcendentals=0)
LONG = pl.CostEstimate(flops=10**11, bytes_accessed=10**8, transcendentals=0)
LIMIT = pltpu.CompilerParams(vmem_limit_bytes=53 << 20)


def passed_along(value, axis, steps):
    count = lax.axis_size(axis)
    pairs = [(source, (source + steps) % count) for source in range(count)]
    return lax.ppermute(value, axis, pairs)


def exchanged(value, axis, bits):
    count = lax.axis_size(axis)
    return lax.ppermute(value, axis, [(source, source ^ bits) for source in range(count)])


def entry(second, own_index, devices, img_dev):
    owner = lax.div(second, img_dev)
    member = lax.rem(owner, GROUP)
    own_member = lax.rem(own_index, GROUP)
    groups = devices // GROUP
    hop = lax.rem(lax.div(owner, GROUP) - lax.div(own_index, GROUP) + groups, groups)
    turn = hop - jnp.where(member <= own_member, 1, 0)
    return ((member ^ own_member) * 2 + turn) * img_dev + second - owner * img_dev


def reverse_kernel(per, devices, place, count, pairs, near, far, blocks, *rest):
    outs, (kept, turned, total, landed) = rest[:GROUP], rest[GROUP:]
    core, own_index = place[0], place[1]
    img_dev, half = near.shape[0], near.shape[1]
    units = 2 * img_dev
    steps = blocks.shape[0] // per

    def fetch(step):
        rows = pl.ds(step * per, per)
        return pltpu.make_async_copy(blocks.at[rows], kept.at[rows], landed.at[step])

    for step in range(steps):
        fetch(step).start()
    near_columns = pl.ds(pl.multiple_of(core * half, half), half)
    far_columns = pl.ds(pl.multiple_of((1 - core) * half, half), half)
    for image in range(img_dev):
        turned[image, :, near_columns] = near[image].T
        turned[image, :, far_columns] = far[image].T
    total[...] = jnp.zeros_like(total)

    @pl.loop(0, steps)
    def _(step):
        fetch(step).wait()
        for part in range(per):
            slot = step * per + part
            place_in = entry(pairs[slot, 1], own_index, devices, img_dev)
            place_in = jnp.where(slot < count[0], place_in, GROUP * units)
            first = pairs[slot, 0] - own_index * img_dev
            product = jnp.dot(turned[first], kept[slot], preferred_element_type=jnp.float32)
            total[place_in] += product.astype(jnp.bfloat16).astype(jnp.float32)

    for member in range(GROUP):
        for unit in range(units):
            outs[member][unit] = total[member * units + unit].astype(jnp.bfloat16).T


def forward_kernel(per, devices, place, count, pairs, panels, blocks, *rest):
    tables, (own, send, kept, table, total, landed) = rest[:GROUP], rest[GROUP:]
    core, own_index = place[0], place[1]
    img_dev, half = panels.shape[0], panels.shape[1]
    units = 2 * img_dev
    steps = blocks.shape[0] // per

    def fetch(step):
        rows = pl.ds(step * per, per)
        return pltpu.make_async_copy(blocks.at[rows], kept.at[rows], landed.at[step])

    for step in range(steps):
        fetch(step).start()
    for member in range(GROUP):
        table[pl.ds(member * units, units)] = tables[member][...]
    total[...] = jnp.zeros_like(total)

    @pl.loop(0, steps)
    def _(step):
        fetch(step).wait()
        for part in range(per):
            slot = step * per + part
            place_in = entry(pairs[slot, 1], own_index, devices, img_dev)
            place_in = jnp.clip(place_in, 0, GROUP * units - 1)
            first = pairs[slot, 0] - own_index * img_dev
            first = jnp.where(slot < count[0], first, img_dev)
            total[first] += jnp.dot(
                kept[slot], table[place_in], preferred_element_type=jnp.float32
            )

    near_rows = pl.ds(pl.multiple_of(core * half, half), half)
    far_rows = pl.ds(pl.multiple_of((1 - core) * half, half), half)
    for image in range(img_dev):
        own[image] = panels[image] + total[image, near_rows]
        send[image] = total[image, far_rows]


def gram_kernel(own, other, near_sum, back_one, back_two, field, packed):
    univ = packed.shape[1]
    gram = jnp.zeros((univ, univ), jnp.float32)
    for image in range(field.shape[0]):
        rows = own[image] + other[image] + near_sum[image]
        rows += back_one[image].astype(jnp.float32) + back_two[image].astype(jnp.float32)
        field[image] = rows
        gram += lax.dot_general(
            rows,
            rows,
            (((0,), (0,)), ((), ())),
            precision=lax.Precision.HIGHEST,
            preferred_element_type=jnp.float32,
        )
    side = univ // 2
    row_ids = lax.broadcasted_iota(jnp.int32, (side, side), 0)
    column_ids = lax.broadcasted_iota(jnp.int32, (side, side), 1)
    last = gram[side:, side:]
    mixed = jnp.where(row_ids <= column_ids, gram[:side, :side], last)
    packed[pl.ds(0, side), :] = jnp.concatenate([mixed, gram[:side, side:]], axis=1)
    diagonal = jnp.sum(jnp.where(row_ids == column_ids, last, 0.0), axis=0, keepdims=True)
    diagonal = jnp.concatenate([diagonal, diagonal], axis=1)
    packed[pl.ds(side, ROWS), :] = jnp.broadcast_to(diagonal, (ROWS, univ))


def solve_kernel(scale, terms, *rest):
    packs, (field, basis, inverse) = rest[:terms], rest[terms:]
    univ = inverse.shape[0]
    side = univ // 2
    packed = packs[0][...]
    for pack in packs[1:]:
        packed += pack[...]
    packed *= scale
    row_ids = lax.broadcasted_iota(jnp.int32, (side, side), 0)
    column_ids = lax.broadcasted_iota(jnp.int32, (side, side), 1)
    mixed = packed[:side, :side]
    turned = mixed.T
    head = jnp.where(row_ids <= column_ids, mixed, turned)
    last = jnp.where(row_ids > column_ids, mixed, turned)
    diagonal = jnp.broadcast_to(packed[side : side + 1, :side], (side, side))
    last = jnp.where(row_ids == column_ids, diagonal, last)
    inverse[pl.ds(0, side), :] = jnp.concatenate([head, packed[:side, side:]], axis=1)
    inverse[pl.ds(side, side), :] = jnp.concatenate([last, last], axis=1)

    count = univ // ROWS
    shape = (ROWS, univ)
    row_ids = lax.broadcasted_iota(jnp.int32, shape, 0)
    column_ids = lax.broadcasted_iota(jnp.int32, shape, 1)
    left = [inverse[pl.ds(b * ROWS, ROWS), :] for b in range(count)]
    right = [
        jnp.where(column_ids == row_ids + b * ROWS, 1.0, 0.0).astype(jnp.float32)
        for b in range(count)
    ]

    def spread(value, row):
        return jnp.broadcast_to(value[row : row + 1, :], shape)

    for b in range(count):
        rows, tail = left[b], right[b]
        columns = [
            jnp.broadcast_to(rows[:, b * ROWS + j : b * ROWS + j + 1], shape) for j in range(ROWS)
        ]
        pivots = jnp.ones(shape, jnp.float32)
        for j in range(ROWS):
            pivot = spread(columns[j], j)
            pivots = jnp.where(row_ids == j, pivot, pivots)
            if j < ROWS - 1:
                weight = jnp.where(row_ids > j, columns[j] * (1.0 / pivot), 0.0)
                for k in range(j + 1, ROWS):
                    columns[k] = columns[k] - weight * spread(columns[k], j)
                rows = rows - weight * spread(rows, j)
                tail = tail - weight * spread(tail, j)
        inverse[pl.ds(b * ROWS, ROWS), :] = tail * lax.rsqrt(pivots)
        if b < count - 1:
            turned = (rows * (1.0 / pivots)).T
            for c in range(b + 1, count):
                for j in range(ROWS):
                    weight = jnp.broadcast_to(turned[c * ROWS : (c + 1) * ROWS, j : j + 1], shape)
                    left[c] = left[c] - weight * spread(rows, j)
                    right[c] = right[c] - weight * spread(tail, j)
    for image in range(field.shape[0]):
        basis[image] = lax.dot_general(
            field[image],
            inverse[...],
            (((1,), (1,)), ((), ())),
            precision=lax.Precision.HIGHEST,
            preferred_element_type=jnp.float32,
        )


def shards(panels, blocks, pairs, counts):
    devices = lax.axis_size("img")
    own_index = lax.axis_index("img")
    member = own_index % GROUP
    img_dev, half, univ = panels.shape
    slots, keypts, cols = blocks.shape
    units = 2 * img_dev
    per = next(width for width in (8, 6, 4, 3, 2, 1) if slots % width == 0)
    place = jnp.stack([lax.axis_index("rep"), own_index]).astype(jnp.int32)
    anywhere = pl.BlockSpec(memory_space=pl.ANY)

    near = panels.astype(jnp.bfloat16)
    far = exchanged(near, "rep", 1)
    returns = pl.pallas_call(
        functools.partial(reverse_kernel, per, devices),
        in_specs=[SMEM] * 3 + [VMEM] * 2 + [anywhere],
        out_specs=[VMEM] * GROUP,
        out_shape=[jax.ShapeDtypeStruct((units, cols, univ), jnp.bfloat16)] * GROUP,
        scratch_shapes=[
            pltpu.VMEM(blocks.shape, blocks.dtype),
            pltpu.VMEM((img_dev, univ, keypts), jnp.bfloat16),
            pltpu.VMEM((GROUP * units + 1, univ, cols), jnp.float32),
            pltpu.SemaphoreType.DMA((slots // per,)),
        ],
        compiler_params=LIMIT,
        cost_estimate=SHORT,
        name="reverse",
    )(place, counts, pairs, near, far, blocks)

    arrived = [exchanged(returns[bits], "img", bits) for bits in range(1, GROUP)]
    part = (img_dev, cols, univ)
    sums = [jnp.zeros(part, jnp.float32) for _ in range(3)]
    for bits, value in enumerate([returns[0]] + arrived):
        first_unit = value[:img_dev].astype(jnp.float32)
        second_unit = value[img_dev:].astype(jnp.float32)
        earlier = (member ^ bits) < member
        sums[0] += jnp.where(earlier, first_unit, 0)
        sums[1] += jnp.where(earlier, second_unit, first_unit)
        sums[2] += jnp.where(earlier, 0, second_unit)
    near_sum = sums[0]
    ahead_sums = [value.astype(jnp.bfloat16) for value in sums[1:]]
    back = [
        passed_along(value, "img", hop * GROUP) for hop, value in enumerate(ahead_sums, start=1)
    ]

    near_late = near
    ahead = [
        near,
        passed_along(near_late, "img", -GROUP),
        passed_along(near_late, "img", -2 * GROUP),
    ]
    *ahead, _ = lax.optimization_barrier((*ahead, returns[0]))
    tables = [jnp.concatenate(ahead[1:])]
    for bits in range(1, GROUP):
        later = member > (member ^ bits)
        sent = jnp.where(later, jnp.concatenate(ahead[:2]), jnp.concatenate(ahead[1:]))
        tables.append(exchanged(sent, "img", bits))

    tables, near_sum, back = lax.optimization_barrier((tables, near_sum, back))
    own, send = pl.pallas_call(
        functools.partial(forward_kernel, per, devices),
        in_specs=[SMEM] * 3 + [VMEM] + [anywhere] + [VMEM] * GROUP,
        out_specs=[VMEM] * 2,
        out_shape=[jax.ShapeDtypeStruct((img_dev, half, univ), jnp.float32)] * 2,
        scratch_shapes=[
            pltpu.VMEM(blocks.shape, blocks.dtype),
            pltpu.VMEM((GROUP * units, cols, univ), jnp.bfloat16),
            pltpu.VMEM((img_dev + 1, keypts, univ), jnp.float32),
            pltpu.SemaphoreType.DMA((slots // per,)),
        ],
        compiler_params=LIMIT,
        cost_estimate=SHORT,
        name="forward",
    )(place, counts, pairs, panels, blocks, *tables)
    other_half = exchanged(send, "rep", 1)

    field, packed = pl.pallas_call(
        gram_kernel,
        in_specs=[VMEM] * 5,
        out_specs=[VMEM] * 2,
        out_shape=[
            jax.ShapeDtypeStruct(panels.shape, jnp.float32),
            jax.ShapeDtypeStruct((univ // 2 + ROWS, univ), jnp.float32),
        ],
        name="gram",
    )(own, other_half, near_sum, *back)
    terms = [packed, exchanged(packed, "rep", 1)]
    bits = 1
    while bits < devices:
        packed = sum(terms)
        terms = [packed] + [exchanged(packed, "img", bits * k) for k in range(1, min(4, devices // bits))]
        bits *= 4
    return pl.pallas_call(
        functools.partial(solve_kernel, 1 / (devices * img_dev * keypts), len(terms)),
        in_specs=[VMEM] * (len(terms) + 1),
        out_specs=VMEM,
        out_shape=jax.ShapeDtypeStruct(panels.shape, jnp.float32),
        scratch_shapes=[pltpu.VMEM((univ, univ), jnp.float32)],
        name="solve",
    )(*terms, field)


def solution(mesh):
    in_specs = (P("img", "rep", None), P("img", None, "rep"), P("img", None), P("img"))
    out_specs = P("img", "rep", None)
    return jax.shard_map(shards, mesh=mesh, in_specs=in_specs, out_specs=out_specs, check_vma=False)
```

time: 100 us -> 81.7 us (0.82)
  other arithmetic: 25.2 us -> 2.89 us
  Pallas kernels: 8.99 us -> 24.9 us
  waiting for transfers between devices: 36 us -> 24.5 us
  starting transfers between devices: 18 us -> 25.3 us
  local copies, waits for them, and re-layouts: 10 us -> 2.99 us
  matrix products: 1.66 us -> 0 us
    another operation x6 -> x1, other arithmetic: 22.9 us -> 0.08 us  [shards(): place = jnp.stack([lax.axis_index('rep'), own_index]).astype(jnp.int32)]
    ppermute x4, waiting for transfers between devices: 16.1 us -> 0.65 us  [passed_along(): return lax.ppermute(value, axis, pairs)]
    pallas_call x0 -> x2, Pallas kernels: none -> 10.2 us  [the longest x1 7.86 us: shards(): pl.pallas_call(functools.partial(solve_kernel, 1 / (devices * img_dev * k...]
    ppermute x13 -> x15, starting transfers between devices: 8.23 us -> 17.7 us  [exchanged(): lax.ppermute(value, axis, [(source, source ^ bits) for source in range(co...]
    unnamed x8 -> x28, local copies, waits for them, and re-layouts: 9.93 us -> 2.92 us
    ppermute x13 -> x15, waiting for transfers between devices: 19.8 us -> 23.9 us  [exchanged(): lax.ppermute(value, axis, [(source, source ^ bits) for source in range(co...]
    pallas_call x1, Pallas kernels: 3.94 us -> 7.16 us  [shards(): pl.pallas_call(functools.partial(reverse_kernel, per, devices), in_specs=...]
    pallas_call x1, Pallas kernels: 5.05 us -> 7.49 us  [shards(): pl.pallas_call(functools.partial(forward_kernel, per, devices), in_specs=...]
  transfers between devices with their start and end apart: 17 -> 19, of which waited for: 10 -> 11; matrix products, arithmetic and copies ran while one was open for 2% -> 2% of each run, Pallas kernels for 9% -> 9%
where the time goes in v2:
time: 81.7 us; the launch traced here: 81.4 us
  starting transfers between devices  25.3 us (31%)
  Pallas kernels  24.9 us (30%)
  waiting for transfers between devices  24.5 us (30%)
  local copies, waits for them, and re-layouts  2.99 us (4%)
  other arithmetic  2.89 us (4%)
    ppermute x15, waiting for transfers between devices, exchanged(): lax.ppermute(value, axis, [(source, source ^ bits) for source in range(co...  23.9 us
    ppermute x15, starting transfers between devices, exchanged(): lax.ppermute(value, axis, [(source, source ^ bits) for source in range(co...  17.7 us
    pallas_call x1, Pallas kernels, shards(): pl.pallas_call(functools.partial(solve_kernel, 1 / (devices * img_dev * k...  7.86 us
    ppermute x4, starting transfers between devices, passed_along(): return lax.ppermute(value, axis, pairs)  7.63 us
    pallas_call x1, Pallas kernels, shards(): pl.pallas_call(functools.partial(forward_kernel, per, devices), in_specs=...  7.49 us
    pallas_call x1, Pallas kernels, shards(): pl.pallas_call(functools.partial(reverse_kernel, per, devices), in_specs=...  7.16 us
    unnamed x28, local copies, waits for them, and re-layouts  2.92 us
    pallas_call x1, Pallas kernels, shards(): pl.pallas_call(gram_kernel, in_specs=[VMEM] * 5, out_specs=[VMEM] * 2, ou...  2.38 us
  transfers between devices with their start and end apart: 19, of which 11 were waited for; matrix products, arithmetic and copies ran while one was open for 2% of the time, Pallas kernels for 9%

profile of v2, /device:TPU:0, one launch (start us, length us, event | category | flops | bytes accessed | tf_op | source)
XLA Modules:
  0.0 81.4 jit_solution(17610028594156713973)
XLA Ops:
  0.0 1.0 %convert_element_type.43.near = bf16[2,256,128]{2,1,0:T(8,128)(2,1)S(1)} convert(f32[2,256,128]{2,1,0:T(8,128)} %panels.1) | non-fusion elementwise | flops 65536 | bytes 393216 | tf_op jit(solution)/shard_map/convert_element_type | solution.py:215
  1.6 4.7 %collective-permute-start = (bf16[2,256,128]{2,1,0:T(8,128)(2,1)S(1)}, bf16[2,256,128]{2,1,0:T(8,128)(2,1)S(1)}, u32[]{:S(2)}, u32[]{:S(2)}) collective-permute-start(bf16[2,256,128]{2,1,0:T(8,128)(2,1)S(1)} %convert_element_type.43.near), channel_id=1, source_target_pairs={{0,24},{2,26},{4,28},{6,30},{8,0},{10,2},{12,4},{14,6},{16,8},{18,... | collective-permute-start | bytes 393224 | tf_op jit(solution)/shard_map/ppermute | solution.py:23
  6.2 0.8 copy.6.pairs
  7.7 7.2 %reverse.1 = (bf16[4,256,128]{2,1,0:T(8,128)(2,1)S(1)}, bf16[4,256,128]{2,1,0:T(8,128)(2,1)S(1)}, bf16[4,256,128]{2,1,0:T(8,128)(2,1)}, bf16[4,256,128]{2,1,0:T(8,128)(2,1)}) custom-call(s32[2]{0:T(128)S(1)} %pad_add_fusion.place, s32[1]{0:T(128)S(6)} %copy.9.count, s32[48,2]{1,0:T(8,128)S(1)} %copy.6.pairs, ...), custom_call_target="tpu_custom_call" | custom-call | flops 1 | bytes 1 | tf_op jit(solution)/shard_map/reverse/pallas_call | solution.py:217
  14.9 1.6 %collective-permute-start.6 = (bf16[4,256,128]{2,1,0:T(8,128)(2,1)S(1)}, bf16[4,256,128]{2,1,0:T(8,128)(2,1)S(1)}, u32[]{:S(2)}, u32[]{:S(2)}) collective-permute-start(bf16[4,256,128]{2,1,0:T(8,128)(2,1)S(1)} %get-tuple-element.27), channel_id=1, source_target_pairs={{0,2},{2,0},{4,6},{6,4},{8,10},{10,8},{12,14},{14,12},{16,18},{18,... | collective-permute-start | bytes 786440 | tf_op jit(solution)/shard_map/ppermute | solution.py:28
  16.5 1.5 %collective-permute-start.7 = (bf16[4,256,128]{2,1,0:T(8,128)(2,1)}, bf16[4,256,128]{2,1,0:T(8,128)(2,1)S(1)}, u32[]{:S(2)}, u32[]{:S(2)}) collective-permute-start(bf16[4,256,128]{2,1,0:T(8,128)(2,1)} %get-tuple-element.28), channel_id=1, source_target_pairs={{0,4},{2,6},{4,0},{6,2},{8,12},{10,14},{12,8},{14,10},{16,20},{18,... | collective-permute-start | bytes 786440 | tf_op jit(solution)/shard_map/ppermute | solution.py:28
  18.6 1.6 %collective-permute-start.3 = (bf16[4,256,128]{2,1,0:T(8,128)(2,1)S(1)}, bf16[4,256,128]{2,1,0:T(8,128)(2,1)S(1)}, u32[]{:S(2)}, u32[]{:S(2)}) collective-permute-start(bf16[4,256,128]{2,1,0:T(8,128)(2,1)S(1)} %get-tuple-element.46), channel_id=1, source_target_pairs={{0,2},{2,0},{4,6},{6,4},{8,10},{10,8},{12,14},{14,12},{16,18},{18,... | collective-permute-start | bytes 786440 | tf_op jit(solution)/shard_map/ppermute | solution.py:28
  20.2 1.5 %collective-permute-start.4 = (bf16[4,256,128]{2,1,0:T(8,128)(2,1)S(1)}, bf16[4,256,128]{2,1,0:T(8,128)(2,1)S(1)}, u32[]{:S(2)}, u32[]{:S(2)}) collective-permute-start(bf16[4,256,128]{2,1,0:T(8,128)(2,1)S(1)} %get-tuple-element.45), channel_id=1, source_target_pairs={{0,4},{2,6},{4,0},{6,2},{8,12},{10,14},{12,8},{14,10},{16,20},{18,... | collective-permute-start | bytes 786440 | tf_op jit(solution)/shard_map/ppermute | solution.py:28
  21.7 2.4 %collective-permute-done.6 = bf16[4,256,128]{2,1,0:T(8,128)(2,1)S(1)} collective-permute-done((bf16[4,256,128]{2,1,0:T(8,128)(2,1)S(1)}, bf16[4,256,128]{2,1,0:T(8,128)(2,1)S(1)}, u32[]{:S(2)}, u32[]{:S(2)}) %collective-permute-start.6) | collective-permute-done | bytes 262176 | tf_op jit(solution)/shard_map/ppermute | solution.py:28
  24.1 2.4 %collective-permute-start.5 = (bf16[4,256,128]{2,1,0:T(8,128)(2,1)S(1)}, bf16[4,256,128]{2,1,0:T(8,128)(2,1)S(1)}, u32[]{:S(2)}, u32[]{:S(2)}) collective-permute-start(bf16[4,256,128]{2,1,0:T(8,128)(2,1)S(1)} %get-tuple-element.44), channel_id=1, source_target_pairs={{0,6},{2,4},{4,2},{6,0},{8,14},{10,12},{12,10},{14,8},{16,22},{18,... | collective-permute-start | bytes 786440 | tf_op jit(solution)/shard_map/ppermute | solution.py:28
  26.6 4.9 %collective-permute-done.7 = bf16[4,256,128]{2,1,0:T(8,128)(2,1)S(1)} collective-permute-done((bf16[4,256,128]{2,1,0:T(8,128)(2,1)}, bf16[4,256,128]{2,1,0:T(8,128)(2,1)S(1)}, u32[]{:S(2)}, u32[]{:S(2)}) %collective-permute-start.7) | collective-permute-done | bytes 262176 | tf_op jit(solution)/shard_map/ppermute | solution.py:28
  31.5 0.9 %fusion.9 = (bf16[2,256,128]{2,1,0:T(8,128)(2,1)S(1)}, bf16[2,256,128]{2,1,0:T(8,128)(2,1)S(1)}, f32[2,256,128]{2,1,0:T(8,128)}) fusion(bf16[4,256,128]{2,1,0:T(8,128)(2,1)S(1)} %get-tuple-element.23, pred[]{:T(512)S(6)} %lt.18, pred[]{:T(512)S(6)} %lt.17, pred[]{:T(512)S(6)} %lt.16, bf16[4,256,128]{2,1,0:T(8,128)(2,1)S(1)} %collective-permute-done.8, ...), kind=kLoop, calls=%fused_computation.18 | loop fusion | flops 1769472 | bytes 1572867 | tf_op jit(solution)/shard_map/convert_element_type | solution.py:244
  32.4 3.0 %collective-permute-start.10 = (bf16[2,256,128]{2,1,0:T(8,128)(2,1)S(1)}, bf16[2,256,128]{2,1,0:T(8,128)(2,1)S(1)}, u32[]{:S(2)}, u32[]{:S(2)}) collective-permute-start(bf16[2,256,128]{2,1,0:T(8,128)(2,1)S(1)} %get-tuple-element.41), channel_id=1, source_target_pairs={{0,16},{2,18},{4,20},{6,22},{8,24},{10,26},{12,28},{14,30},{16,0},... | collective-permute-start | bytes 393224 | tf_op jit(solution)/shard_map/ppermute | solution.py:23
  35.4 6.2 %collective-permute-done.4.rest_2_ = bf16[4,256,128]{2,1,0:T(8,128)(2,1)S(1)} collective-permute-done((bf16[4,256,128]{2,1,0:T(8,128)(2,1)S(1)}, bf16[4,256,128]{2,1,0:T(8,128)(2,1)S(1)}, u32[]{:S(2)}, u32[]{:S(2)}) %collective-permute-start.4) | collective-permute-done | bytes 262176 | tf_op jit(solution)/shard_map/ppermute | solution.py:28
  42.4 7.5 %forward.1 = (f32[2,256,128]{2,1,0:T(8,128)S(1)}, f32[2,256,128]{2,1,0:T(8,128)S(1)}) custom-call(s32[2]{0:T(128)S(1)} %pad_add_fusion.place, s32[1]{0:T(128)S(6)} %copy.9.count, s32[48,2]{1,0:T(8,128)S(1)} %copy.6.pairs, f32[2,256,128]{2,1,0:T(8,128)S(1)} %copy-done, bf16[48,512,256]{2,1,0:T(8,128)(2,1)} %blocks.3, bf16[4,256,128]{2,1,0:T(8,128)(2,1)} %copy-done.2, ...), custom_call_target="tpu_custom_call" | custom-call | flops 1 | bytes 1 | tf_op jit(solution)/shard_map/forward/pallas_call | solution.py:263
  49.9 0.7 copy-done.1
  50.6 1.5 %collective-permute-done.11.other = f32[2,256,128]{2,1,0:T(8,128)S(1)} collective-permute-done((f32[2,256,128]{2,1,0:T(8,128)S(1)}, f32[2,256,128]{2,1,0:T(8,128)S(1)}, u32[]{:S(2)}, u32[]{:S(2)}) %collective-permute-start.11) | collective-permute-done | bytes 262176 | tf_op jit(solution)/shard_map/ppermute | solution.py:28
  52.2 0.7 copy-done.6
  52.9 2.4 %gram.1 = (f32[2,256,128]{2,1,0:T(8,128)}, f32[72,128]{1,0:T(8,128)}) custom-call(f32[2,256,128]{2,1,0:T(8,128)} %copy-done.1, f32[2,256,128]{2,1,0:T(8,128)} %copy-done.6, f32[2,256,128]{2,1,0:T(8,128)} %get-tuple-element.36.near_sum, bf16[2,256,128]{2,1,0:T(8,128)(2,1)} %copy-done.9, bf16[2,256,128]{2,1,0:T(8,128)(2,1)} %copy-done.8), custom_call_target="tpu_custom_call" | custom-call | tf_op jit(solution)/shard_map/gram/pallas_call | solution.py:280
  55.4 1.3 %collective-permute-done.12 = f32[72,128]{1,0:T(8,128)S(1)} collective-permute-done((f32[72,128]{1,0:T(8,128)}, f32[72,128]{1,0:T(8,128)S(1)}, u32[]{:S(2)}, u32[]{:S(2)}) %collective-permute-start.12) | collective-permute-done | bytes 36896 | tf_op jit(solution)/shard_map/ppermute | solution.py:28
  56.7 0.8 add.50
  57.4 1.2 %collective-permute-start.13 = (f32[72,128]{1,0:T(8,128)S(1)}, f32[72,128]{1,0:T(8,128)S(1)}, u32[]{:S(2)}, u32[]{:S(2)}) collective-permute-start(f32[72,128]{1,0:T(8,128)S(1)} %add.50), channel_id=1, source_target_pairs={{0,2},{2,0},{4,6},{6,4},{8,10},{10,8},{12,14},{14,12},{16,18},{18,... | collective-permute-start | bytes 110600 | tf_op jit(solution)/shard_map/ppermute | solution.py:28
  58.6 0.9 %collective-permute-start.14 = (f32[72,128]{1,0:T(8,128)S(1)}, f32[72,128]{1,0:T(8,128)S(1)}, u32[]{:S(2)}, u32[]{:S(2)}) collective-permute-start(f32[72,128]{1,0:T(8,128)S(1)} %add.50), channel_id=1, source_target_pairs={{0,4},{2,6},{4,0},{6,2},{8,12},{10,14},{12,8},{14,10},{16,20},{18,... | collective-permute-start | bytes 110600 | tf_op jit(solution)/shard_map/ppermute | solution.py:28
  59.5 1.4 %collective-permute-start.15 = (f32[72,128]{1,0:T(8,128)S(1)}, f32[72,128]{1,0:T(8,128)S(1)}, u32[]{:S(2)}, u32[]{:S(2)}) collective-permute-start(f32[72,128]{1,0:T(8,128)S(1)} %add.50), channel_id=1, source_target_pairs={{0,6},{2,4},{4,2},{6,0},{8,14},{10,12},{12,10},{14,8},{16,22},{18,... | collective-permute-start | bytes 110600 | tf_op jit(solution)/shard_map/ppermute | solution.py:28
  61.4 1.2 %collective-permute-done.14 = f32[72,128]{1,0:T(8,128)S(1)} collective-permute-done((f32[72,128]{1,0:T(8,128)S(1)}, f32[72,128]{1,0:T(8,128)S(1)}, u32[]{:S(2)}, u32[]{:S(2)}) %collective-permute-start.14) | collective-permute-done | bytes 36896 | tf_op jit(solution)/shard_map/ppermute | solution.py:28
  62.6 1.8 %collective-permute-done.15 = f32[72,128]{1,0:T(8,128)S(1)} collective-permute-done((f32[72,128]{1,0:T(8,128)S(1)}, f32[72,128]{1,0:T(8,128)S(1)}, u32[]{:S(2)}, u32[]{:S(2)}) %collective-permute-start.15) | collective-permute-done | bytes 36896 | tf_op jit(solution)/shard_map/ppermute | solution.py:28
  64.4 0.8 collective-permute-start.16
  65.2 2.0 %collective-permute-start.17 = (f32[72,128]{1,0:T(8,128)S(1)}, f32[72,128]{1,0:T(8,128)S(1)}, u32[]{:S(2)}, u32[]{:S(2)}) collective-permute-start(f32[72,128]{1,0:T(8,128)S(1)} %add_add_fusion.rest_0_), channel_id=1, source_target_pairs={{0,16},{2,18},{4,20},{6,22},{8,24},{10,26},{12,28},{14,30},{16,0},... | collective-permute-start | bytes 110600 | tf_op jit(solution)/shard_map/ppermute | solution.py:28
  67.2 1.7 %collective-permute-start.18 = (f32[72,128]{1,0:T(8,128)S(1)}, f32[72,128]{1,0:T(8,128)S(1)}, u32[]{:S(2)}, u32[]{:S(2)}) collective-permute-start(f32[72,128]{1,0:T(8,128)S(1)} %add_add_fusion.rest_0_), channel_id=1, source_target_pairs={{0,24},{2,26},{4,28},{6,30},{8,16},{10,18},{12,20},{14,22},{16,8},... | collective-permute-start | bytes 110600 | tf_op jit(solution)/shard_map/ppermute | solution.py:28
  68.8 1.6 %collective-permute-done.17.rest_2_ = f32[72,128]{1,0:T(8,128)S(1)} collective-permute-done((f32[72,128]{1,0:T(8,128)S(1)}, f32[72,128]{1,0:T(8,128)S(1)}, u32[]{:S(2)}, u32[]{:S(2)}) %collective-permute-start.17) | collective-permute-done | bytes 36896 | tf_op jit(solution)/shard_map/ppermute | solution.py:28
  70.4 2.5 %collective-permute-done.18.rest_3_ = f32[72,128]{1,0:T(8,128)S(1)} collective-permute-done((f32[72,128]{1,0:T(8,128)S(1)}, f32[72,128]{1,0:T(8,128)S(1)}, u32[]{:S(2)}, u32[]{:S(2)}) %collective-permute-start.18) | collective-permute-done | bytes 36896 | tf_op jit(solution)/shard_map/ppermute | solution.py:28
  73.5 7.9 %solve.1 = f32[2,256,128]{2,1,0:T(8,128)} custom-call(f32[72,128]{1,0:T(8,128)} %copy-done.7, f32[72,128]{1,0:T(8,128)} %copy-done.10, f32[72,128]{1,0:T(8,128)} %copy-done.11, f32[72,128]{1,0:T(8,128)} %copy-done.12, f32[2,256,128]{2,1,0:T(8,128)} %get-tuple-element.40.rest_4_), custom_call_target="tpu_custom_call" | custom-call | tf_op jit(solution)/shard_map/solve/pallas_call | solution.py:296
  (46 shorter events, 3.3 us)
Async XLA Ops:
  0.0 42.4 %copy-start = (f32[2,256,128]{2,1,0:T(8,128)S(1)}, f32[2,256,128]{2,1,0:T(8,128)}, u32[]{:S(2)}) copy-start(f32[2,256,128]{2,1,0:T(8,128)} %panels.1) | copy-start | bytes 786436
  1.0 6.7 %collective-permute-start.2 = (bf16[2,256,128]{2,1,0:T(8,128)(2,1)S(1)}, bf16[2,256,128]{2,1,0:T(8,128)(2,1)S(1)}, u32[]{:S(2)}, u32[]{:S(2)}) collective-permute-start(bf16[2,256,128]{2,1,0:T(8,128)(2,1)S(1)} %convert_element_type.43.near), channel_id=1, source_target_pairs={{0,1},{1,0},{2,3},{3,2},{4,5},{5,4},{6,7},{7,6},{8,9},{9,8},{10,11... | collective-permute-start | bytes 393224 | tf_op jit(solution)/shard_map/ppermute | solution.py:28
  1.6 16.9 %collective-permute-start = (bf16[2,256,128]{2,1,0:T(8,128)(2,1)S(1)}, bf16[2,256,128]{2,1,0:T(8,128)(2,1)S(1)}, u32[]{:S(2)}, u32[]{:S(2)}) collective-permute-start(bf16[2,256,128]{2,1,0:T(8,128)(2,1)S(1)} %convert_element_type.43.near), channel_id=1, source_target_pairs={{0,24},{2,26},{4,28},{6,30},{8,0},{10,2},{12,4},{14,6},{16,8},{18,... | collective-permute-start | bytes 393224 | tf_op jit(solution)/shard_map/ppermute | solution.py:23
  6.2 12.2 %collective-permute-start.1 = (bf16[2,256,128]{2,1,0:T(8,128)(2,1)S(1)}, bf16[2,256,128]{2,1,0:T(8,128)(2,1)S(1)}, u32[]{:S(2)}, u32[]{:S(2)}) collective-permute-start(bf16[2,256,128]{2,1,0:T(8,128)(2,1)S(1)} %convert_element_type.43.near), channel_id=1, source_target_pairs={{0,16},{2,18},{4,20},{6,22},{8,24},{10,26},{12,28},{14,30},{16,0},... | collective-permute-start | bytes 393224 | tf_op jit(solution)/shard_map/ppermute | solution.py:23
  14.9 9.2 %collective-permute-start.6 = (bf16[4,256,128]{2,1,0:T(8,128)(2,1)S(1)}, bf16[4,256,128]{2,1,0:T(8,128)(2,1)S(1)}, u32[]{:S(2)}, u32[]{:S(2)}) collective-permute-start(bf16[4,256,128]{2,1,0:T(8,128)(2,1)S(1)} %get-tuple-element.27), channel_id=1, source_target_pairs={{0,2},{2,0},{4,6},{6,4},{8,10},{10,8},{12,14},{14,12},{16,18},{18,... | collective-permute-start | bytes 786440 | tf_op jit(solution)/shard_map/ppermute | solution.py:28
  16.5 15.0 %collective-permute-start.7 = (bf16[4,256,128]{2,1,0:T(8,128)(2,1)}, bf16[4,256,128]{2,1,0:T(8,128)(2,1)S(1)}, u32[]{:S(2)}, u32[]{:S(2)}) collective-permute-start(bf16[4,256,128]{2,1,0:T(8,128)(2,1)} %get-tuple-element.28), channel_id=1, source_target_pairs={{0,4},{2,6},{4,0},{6,2},{8,12},{10,14},{12,8},{14,10},{16,20},{18,... | collective-permute-start | bytes 786440 | tf_op jit(solution)/shard_map/ppermute | solution.py:28
  18.0 13.5 %collective-permute-start.8 = (bf16[4,256,128]{2,1,0:T(8,128)(2,1)}, bf16[4,256,128]{2,1,0:T(8,128)(2,1)S(1)}, u32[]{:S(2)}, u32[]{:S(2)}) collective-permute-start(bf16[4,256,128]{2,1,0:T(8,128)(2,1)} %get-tuple-element.29), channel_id=1, source_target_pairs={{0,6},{2,4},{4,2},{6,0},{8,14},{10,12},{12,10},{14,8},{16,22},{18,... | collective-permute-start | bytes 786440 | tf_op jit(solution)/shard_map/ppermute | solution.py:28
  18.6 23.7 %copy-start.2 = (bf16[4,256,128]{2,1,0:T(8,128)(2,1)}, bf16[4,256,128]{2,1,0:T(8,128)(2,1)S(1)}, u32[]{:S(2)}) copy-start(bf16[4,256,128]{2,1,0:T(8,128)(2,1)S(1)} %constant_dynamic-update-slice_fusion.rest_0_) | copy-start | bytes 786436
  18.6 16.8 %collective-permute-start.3 = (bf16[4,256,128]{2,1,0:T(8,128)(2,1)S(1)}, bf16[4,256,128]{2,1,0:T(8,128)(2,1)S(1)}, u32[]{:S(2)}, u32[]{:S(2)}) collective-permute-start(bf16[4,256,128]{2,1,0:T(8,128)(2,1)S(1)} %get-tuple-element.46), channel_id=1, source_target_pairs={{0,2},{2,0},{4,6},{6,4},{8,10},{10,8},{12,14},{14,12},{16,18},{18,... | collective-permute-start | bytes 786440 | tf_op jit(solution)/shard_map/ppermute | solution.py:28
  20.2 21.4 %collective-permute-start.4 = (bf16[4,256,128]{2,1,0:T(8,128)(2,1)S(1)}, bf16[4,256,128]{2,1,0:T(8,128)(2,1)S(1)}, u32[]{:S(2)}, u32[]{:S(2)}) collective-permute-start(bf16[4,256,128]{2,1,0:T(8,128)(2,1)S(1)} %get-tuple-element.45), channel_id=1, source_target_pairs={{0,4},{2,6},{4,0},{6,2},{8,12},{10,14},{12,8},{14,10},{16,20},{18,... | collective-permute-start | bytes 786440 | tf_op jit(solution)/shard_map/ppermute | solution.py:28
  24.1 17.5 %collective-permute-start.5 = (bf16[4,256,128]{2,1,0:T(8,128)(2,1)S(1)}, bf16[4,256,128]{2,1,0:T(8,128)(2,1)S(1)}, u32[]{:S(2)}, u32[]{:S(2)}) collective-permute-start(bf16[4,256,128]{2,1,0:T(8,128)(2,1)S(1)} %get-tuple-element.44), channel_id=1, source_target_pairs={{0,6},{2,4},{4,2},{6,0},{8,14},{10,12},{12,10},{14,8},{16,22},{18,... | collective-permute-start | bytes 786440 | tf_op jit(solution)/shard_map/ppermute | solution.py:28
  32.4 9.9 %collective-permute-start.10 = (bf16[2,256,128]{2,1,0:T(8,128)(2,1)S(1)}, bf16[2,256,128]{2,1,0:T(8,128)(2,1)S(1)}, u32[]{:S(2)}, u32[]{:S(2)}) collective-permute-start(bf16[2,256,128]{2,1,0:T(8,128)(2,1)S(1)} %get-tuple-element.41), channel_id=1, source_target_pairs={{0,16},{2,18},{4,20},{6,22},{8,24},{10,26},{12,28},{14,30},{16,0},... | collective-permute-start | bytes 393224 | tf_op jit(solution)/shard_map/ppermute | solution.py:23
  35.4 6.9 %collective-permute-start.9 = (bf16[2,256,128]{2,1,0:T(8,128)(2,1)S(1)}, bf16[2,256,128]{2,1,0:T(8,128)(2,1)S(1)}, u32[]{:S(2)}, u32[]{:S(2)}) collective-permute-start(bf16[2,256,128]{2,1,0:T(8,128)(2,1)S(1)} %get-tuple-element.42), channel_id=1, source_target_pairs={{0,8},{2,10},{4,12},{6,14},{8,16},{10,18},{12,20},{14,22},{16,24},... | collective-permute-start | bytes 393224 | tf_op jit(solution)/shard_map/ppermute | solution.py:23
  35.4 6.9 %copy-start.3 = (bf16[4,256,128]{2,1,0:T(8,128)(2,1)}, bf16[4,256,128]{2,1,0:T(8,128)(2,1)S(1)}, u32[]{:S(2)}) copy-start(bf16[4,256,128]{2,1,0:T(8,128)(2,1)S(1)} %collective-permute-done.3.rest_1_) | copy-start | bytes 786436
  41.6 0.7 copy-start.4
  41.6 0.8 copy-start.5
  42.3 9.9 %copy-start.8 = (bf16[2,256,128]{2,1,0:T(8,128)(2,1)}, bf16[2,256,128]{2,1,0:T(8,128)(2,1)S(1)}, u32[]{:S(2)}) copy-start(bf16[2,256,128]{2,1,0:T(8,128)(2,1)S(1)} %collective-permute-done.10.back_two) | copy-start | bytes 393220
  42.3 9.9 %copy-start.9 = (bf16[2,256,128]{2,1,0:T(8,128)(2,1)}, bf16[2,256,128]{2,1,0:T(8,128)(2,1)S(1)}, u32[]{:S(2)}) copy-start(bf16[2,256,128]{2,1,0:T(8,128)(2,1)S(1)} %collective-permute-done.9.back_one) | copy-start | bytes 393220
  49.9 0.7 copy-start.1
  50.6 1.5 %collective-permute-start.11 = (f32[2,256,128]{2,1,0:T(8,128)S(1)}, f32[2,256,128]{2,1,0:T(8,128)S(1)}, u32[]{:S(2)}, u32[]{:S(2)}) collective-permute-start(f32[2,256,128]{2,1,0:T(8,128)S(1)} %get-tuple-element.35), channel_id=1, source_target_pairs={{0,1},{1,0},{2,3},{3,2},{4,5},{5,4},{6,7},{7,6},{8,9},{9,8},{10,11... | collective-permute-start | bytes 786440 | tf_op jit(solution)/shard_map/ppermute | solution.py:28
  52.2 0.7 copy-start.6
  55.2 1.4 %collective-permute-start.12 = (f32[72,128]{1,0:T(8,128)}, f32[72,128]{1,0:T(8,128)S(1)}, u32[]{:S(2)}, u32[]{:S(2)}) collective-permute-start(f32[72,128]{1,0:T(8,128)} %get-tuple-element.39), channel_id=1, source_target_pairs={{0,1},{1,0},{2,3},{3,2},{4,5},{5,4},{6,7},{7,6},{8,9},{9,8},{10,11... | collective-permute-start | bytes 110600 | tf_op jit(solution)/shard_map/ppermute | solution.py:28
  57.4 4.0 %collective-permute-start.13 = (f32[72,128]{1,0:T(8,128)S(1)}, f32[72,128]{1,0:T(8,128)S(1)}, u32[]{:S(2)}, u32[]{:S(2)}) collective-permute-start(f32[72,128]{1,0:T(8,128)S(1)} %add.50), channel_id=1, source_target_pairs={{0,2},{2,0},{4,6},{6,4},{8,10},{10,8},{12,14},{14,12},{16,18},{18,... | collective-permute-start | bytes 110600 | tf_op jit(solution)/shard_map/ppermute | solution.py:28
  58.6 4.0 %collective-permute-start.14 = (f32[72,128]{1,0:T(8,128)S(1)}, f32[72,128]{1,0:T(8,128)S(1)}, u32[]{:S(2)}, u32[]{:S(2)}) collective-permute-start(f32[72,128]{1,0:T(8,128)S(1)} %add.50), channel_id=1, source_target_pairs={{0,4},{2,6},{4,0},{6,2},{8,12},{10,14},{12,8},{14,10},{16,20},{18,... | collective-permute-start | bytes 110600 | tf_op jit(solution)/shard_map/ppermute | solution.py:28
  59.5 4.9 %collective-permute-start.15 = (f32[72,128]{1,0:T(8,128)S(1)}, f32[72,128]{1,0:T(8,128)S(1)}, u32[]{:S(2)}, u32[]{:S(2)}) collective-permute-start(f32[72,128]{1,0:T(8,128)S(1)} %add.50), channel_id=1, source_target_pairs={{0,6},{2,4},{4,2},{6,0},{8,14},{10,12},{12,10},{14,8},{16,22},{18,... | collective-permute-start | bytes 110600 | tf_op jit(solution)/shard_map/ppermute | solution.py:28
  64.4 8.6 %copy-start.7 = (f32[72,128]{1,0:T(8,128)}, f32[72,128]{1,0:T(8,128)S(1)}, u32[]{:S(2)}) copy-start(f32[72,128]{1,0:T(8,128)S(1)} %add_add_fusion.rest_0_) | copy-start | bytes 110596
  64.4 4.5 %collective-permute-start.16 = (f32[72,128]{1,0:T(8,128)S(1)}, f32[72,128]{1,0:T(8,128)S(1)}, u32[]{:S(2)}, u32[]{:S(2)}) collective-permute-start(f32[72,128]{1,0:T(8,128)S(1)} %add_add_fusion.rest_0_), channel_id=1, source_target_pairs={{0,8},{2,10},{4,12},{6,14},{8,0},{10,2},{12,4},{14,6},{16,24},{18,... | collective-permute-start | bytes 110600 | tf_op jit(solution)/shard_map/ppermute | solution.py:28
  65.2 5.3 %collective-permute-start.17 = (f32[72,128]{1,0:T(8,128)S(1)}, f32[72,128]{1,0:T(8,128)S(1)}, u32[]{:S(2)}, u32[]{:S(2)}) collective-permute-start(f32[72,128]{1,0:T(8,128)S(1)} %add_add_fusion.rest_0_), channel_id=1, source_target_pairs={{0,16},{2,18},{4,20},{6,22},{8,24},{10,26},{12,28},{14,30},{16,0},... | collective-permute-start | bytes 110600 | tf_op jit(solution)/shard_map/ppermute | solution.py:28
  67.2 5.8 %collective-permute-start.18 = (f32[72,128]{1,0:T(8,128)S(1)}, f32[72,128]{1,0:T(8,128)S(1)}, u32[]{:S(2)}, u32[]{:S(2)}) collective-permute-start(f32[72,128]{1,0:T(8,128)S(1)} %add_add_fusion.rest_0_), channel_id=1, source_target_pairs={{0,24},{2,26},{4,28},{6,30},{8,16},{10,18},{12,20},{14,22},{16,8},... | collective-permute-start | bytes 110600 | tf_op jit(solution)/shard_map/ppermute | solution.py:28
  68.8 4.1 %copy-start.10 = (f32[72,128]{1,0:T(8,128)}, f32[72,128]{1,0:T(8,128)S(1)}, u32[]{:S(2)}) copy-start(f32[72,128]{1,0:T(8,128)S(1)} %collective-permute-done.16.rest_1_) | copy-start | bytes 110596
  70.4 2.5 %copy-start.11 = (f32[72,128]{1,0:T(8,128)}, f32[72,128]{1,0:T(8,128)S(1)}, u32[]{:S(2)}) copy-start(f32[72,128]{1,0:T(8,128)S(1)} %collective-permute-done.17.rest_2_) | copy-start | bytes 110596
  72.9 0.6 copy-start.12

commit v3 on v2

--- a/solution.py
+++ b/solution.py
@@ -9,12 +9,14 @@
 
 BAND = 8
 GROUP = BAND // 2
-ROWS = 8
+WAIT = 6
+ROWS = 16
 SMEM = pl.BlockSpec(memory_space=pltpu.SMEM)
 VMEM = pl.BlockSpec(memory_space=pltpu.VMEM)
 SHORT = pl.CostEstimate(flops=1, bytes_accessed=1, transcendentals=0)
 LONG = pl.CostEstimate(flops=10**11, bytes_accessed=10**8, transcendentals=0)
-LIMIT = pltpu.CompilerParams(vmem_limit_bytes=53 << 20)
+SMALL = pltpu.CompilerParams(vmem_limit_bytes=8 << 20)
+LIMIT = pltpu.CompilerParams(vmem_limit_bytes=50 << 20)
 
 
 def passed_along(value, axis, steps):
@@ -38,19 +40,42 @@
     return ((member ^ own_member) * 2 + turn) * img_dev + second - owner * img_dev
 
 
-def reverse_kernel(per, devices, place, count, pairs, near, far, blocks, *rest):
-    outs, (kept, turned, total, landed) = rest[:GROUP], rest[GROUP:]
-    core, own_index = place[0], place[1]
+def start_kernel(panels, pairs, counts, near, numbers):
+    near[...] = panels[...].astype(jnp.bfloat16)
+    row = (1, pairs.shape[1])
+    numbers[...] = jnp.zeros_like(numbers)
+    numbers[pl.ds(0, 2), :] = pairs[...]
+    numbers[pl.ds(2, 1), :] = jnp.broadcast_to(counts[...], row)
+    numbers[pl.ds(3, 1), :] = jnp.full(row, lax.axis_index("rep"), jnp.int32)
+    numbers[pl.ds(4, 1), :] = jnp.full(row, lax.axis_index("img"), jnp.int32)
+
+
+def reverse_kernel(per, devices, numbers, near, far, blocks, *rest):
+    outs, order, rest = rest[:GROUP], rest[GROUP : GROUP + 3], rest[GROUP + 3 :]
+    kept, turned, total, landed, held, listed, filled = rest
+    members, units_of, firsts = order
+    bucket = members.shape[0] // GROUP
+    slots = blocks.shape[0]
     img_dev, half = near.shape[0], near.shape[1]
     units = 2 * img_dev
-    steps = blocks.shape[0] // per
+    steps = slots // per
 
     def fetch(step):
         rows = pl.ds(step * per, per)
         return pltpu.make_async_copy(blocks.at[rows], kept.at[rows], landed.at[step])
 
+    lists = pltpu.make_async_copy(numbers, held, listed)
+    lists.start()
     for step in range(steps):
         fetch(step).start()
+    for member in range(GROUP):
+        filled[member] = 0
+        for rank in range(bucket):
+            members[member * bucket + rank] = 0
+            units_of[member * bucket + rank] = 0
+            firsts[member * bucket + rank] = img_dev
+    lists.wait()
+    count, core, own_index = held[2, 0], held[3, 0], held[4, 0]
     near_columns = pl.ds(pl.multiple_of(core * half, half), half)
     far_columns = pl.ds(pl.multiple_of((1 - core) * half, half), half)
     for image in range(img_dev):
@@ -63,9 +88,16 @@
         fetch(step).wait()
         for part in range(per):
             slot = step * per + part
-            place_in = entry(pairs[slot, 1], own_index, devices, img_dev)
-            place_in = jnp.where(slot < count[0], place_in, GROUP * units)
-            first = pairs[slot, 0] - own_index * img_dev
+            alive = slot < count
+            place_in = entry(held[1, slot], own_index, devices, img_dev)
+            first = held[0, slot] - own_index * img_dev
+            apart = lax.div(place_in, units)
+            rank = filled[apart]
+            filled[apart] = rank + jnp.where(alive, 1, 0)
+            members[apart * bucket + rank] = slot
+            units_of[apart * bucket + rank] = place_in - apart * units
+            firsts[apart * bucket + rank] = jnp.where(alive, first, img_dev)
+            place_in = jnp.where(alive, place_in, GROUP * units)
             product = jnp.dot(turned[first], kept[slot], preferred_element_type=jnp.float32)
             total[place_in] += product.astype(jnp.bfloat16).astype(jnp.float32)
 
@@ -74,57 +106,65 @@
             outs[member][unit] = total[member * units + unit].astype(jnp.bfloat16).T
 
 
-def forward_kernel(per, devices, place, count, pairs, panels, blocks, *rest):
-    tables, (own, send, kept, table, total, landed) = rest[:GROUP], rest[GROUP:]
-    core, own_index = place[0], place[1]
+def forward_slots(picked, members, units, firsts, blocks, tables, kept, total, landed):
+    bucket = members.shape[0] // GROUP
+    listed = [member * bucket + rank for member in picked for rank in range(bucket)]
+
+    def fetch(at):
+        return pltpu.make_async_copy(blocks.at[members[listed[at]]], kept.at[at], landed.at[at])
+
+    for at in range(len(listed)):
+        fetch(at).start()
+    for at, target in enumerate(listed):
+        if at % WAIT == 0:
+            for more in range(at, min(at + WAIT, len(listed))):
+                fetch(more).wait()
+        table = tables[at // bucket]
+        total[firsts[target]] += jnp.dot(
+            kept[at], table[units[target]], preferred_element_type=jnp.float32
+        )
+
+
+def forward_first_kernel(picked, members, units, firsts, blocks, *rest):
+    tables, (sums, kept, total, landed) = rest[: len(picked)], rest[len(picked) :]
+    total[...] = jnp.zeros_like(total)
+    forward_slots(picked, members, units, firsts, blocks, tables, kept, total, landed)
+    for image in range(sums.shape[0]):
+        sums[image] = total[image]
+
+
+def forward_last_kernel(picked, place, members, units, firsts, blocks, panels, before, *rest):
+    tables, (own, send, kept, total, landed) = rest[: len(picked)], rest[len(picked) :]
+    core = place[0]
     img_dev, half = panels.shape[0], panels.shape[1]
-    units = 2 * img_dev
-    steps = blocks.shape[0] // per
-
-    def fetch(step):
-        rows = pl.ds(step * per, per)
-        return pltpu.make_async_copy(blocks.at[rows], kept.at[rows], landed.at[step])
-
-    for step in range(steps):
-        fetch(step).start()
-    for member in range(GROUP):
-        table[pl.ds(member * units, units)] = tables[member][...]
     total[...] = jnp.zeros_like(total)
-
-    @pl.loop(0, steps)
-    def _(step):
-        fetch(step).wait()
-        for part in range(per):
-            slot = step * per + part
-            place_in = entry(pairs[slot, 1], own_index, devices, img_dev)
-            place_in = jnp.clip(place_in, 0, GROUP * units - 1)
-            first = pairs[slot, 0] - own_index * img_dev
-            first = jnp.where(slot < count[0], first, img_dev)
-            total[first] += jnp.dot(
-                kept[slot], table[place_in], preferred_element_type=jnp.float32
-            )
-
+    forward_slots(picked, members, units, firsts, blocks, tables, kept, total, landed)
     near_rows = pl.ds(pl.multiple_of(core * half, half), half)
     far_rows = pl.ds(pl.multiple_of((1 - core) * half, half), half)
     for image in range(img_dev):
-        own[image] = panels[image] + total[image, near_rows]
-        send[image] = total[image, far_rows]
+        own[image] = panels[image] + before[image, near_rows] + total[image, near_rows]
+        send[image] = before[image, far_rows] + total[image, far_rows]
+
+
+def split(value):
+    high = value.astype(jnp.bfloat16)
+    return high, (value - high.astype(jnp.float32)).astype(jnp.bfloat16)
 
 
 def gram_kernel(own, other, near_sum, back_one, back_two, field, packed):
     univ = packed.shape[1]
-    gram = jnp.zeros((univ, univ), jnp.float32)
+    gram = jnp.zeros((univ, 2 * univ), jnp.float32)
     for image in range(field.shape[0]):
         rows = own[image] + other[image] + near_sum[image]
         rows += back_one[image].astype(jnp.float32) + back_two[image].astype(jnp.float32)
         field[image] = rows
+        high, low = split(rows)
+        both = jnp.concatenate([high, low], axis=1)
         gram += lax.dot_general(
-            rows,
-            rows,
-            (((0,), (0,)), ((), ())),
-            precision=lax.Precision.HIGHEST,
-            preferred_element_type=jnp.float32,
+            high, both, (((0,), (0,)), ((), ())), preferred_element_type=jnp.float32
         )
+    crossed = gram[:, univ:]
+    gram = gram[:, :univ] + crossed + crossed.T
     side = univ // 2
     row_ids = lax.broadcasted_iota(jnp.int32, (side, side), 0)
     column_ids = lax.broadcasted_iota(jnp.int32, (side, side), 1)
@@ -133,7 +173,7 @@
     packed[pl.ds(0, side), :] = jnp.concatenate([mixed, gram[:side, side:]], axis=1)
     diagonal = jnp.sum(jnp.where(row_ids == column_ids, last, 0.0), axis=0, keepdims=True)
     diagonal = jnp.concatenate([diagonal, diagonal], axis=1)
-    packed[pl.ds(side, ROWS), :] = jnp.broadcast_to(diagonal, (ROWS, univ))
+    packed[pl.ds(side, 8), :] = jnp.broadcast_to(diagonal, (8, univ))
 
 
 def solve_kernel(scale, terms, *rest):
@@ -191,13 +231,14 @@
                     weight = jnp.broadcast_to(turned[c * ROWS : (c + 1) * ROWS, j : j + 1], shape)
                     left[c] = left[c] - weight * spread(rows, j)
                     right[c] = right[c] - weight * spread(tail, j)
+    inverse_high, inverse_low = split(inverse[...].T)
+    wide = jnp.concatenate([inverse_high, inverse_low], axis=1)
     for image in range(field.shape[0]):
-        basis[image] = lax.dot_general(
-            field[image],
-            inverse[...],
-            (((1,), (1,)), ((), ())),
-            precision=lax.Precision.HIGHEST,
-            preferred_element_type=jnp.float32,
+        high, low = split(field[image])
+        products = jnp.dot(high, wide, preferred_element_type=jnp.float32)
+        products = products[:, :univ] + products[:, univ:]
+        basis[image] = products + jnp.dot(
+            low, inverse_high, preferred_element_type=jnp.float32
         )
 
 
@@ -212,23 +253,38 @@
     place = jnp.stack([lax.axis_index("rep"), own_index]).astype(jnp.int32)
     anywhere = pl.BlockSpec(memory_space=pl.ANY)
 
-    near = panels.astype(jnp.bfloat16)
+    near, numbers = pl.pallas_call(
+        start_kernel,
+        in_specs=[VMEM] * 3,
+        out_specs=[VMEM] * 2,
+        out_shape=[
+            jax.ShapeDtypeStruct(panels.shape, jnp.bfloat16),
+            jax.ShapeDtypeStruct((8, slots), jnp.int32),
+        ],
+        compiler_params=SMALL,
+        name="start",
+    )(panels, pairs.T, counts.reshape(1, 1))
     far = exchanged(near, "rep", 1)
-    returns = pl.pallas_call(
+    bucket = 2 * (slots // BAND)
+    *returns, members, units_of, firsts = pl.pallas_call(
         functools.partial(reverse_kernel, per, devices),
-        in_specs=[SMEM] * 3 + [VMEM] * 2 + [anywhere],
-        out_specs=[VMEM] * GROUP,
-        out_shape=[jax.ShapeDtypeStruct((units, cols, univ), jnp.bfloat16)] * GROUP,
+        in_specs=[anywhere] + [VMEM] * 2 + [anywhere],
+        out_specs=[VMEM] * GROUP + [SMEM] * 3,
+        out_shape=[jax.ShapeDtypeStruct((units, cols, univ), jnp.bfloat16)] * GROUP
+        + [jax.ShapeDtypeStruct((GROUP * bucket,), jnp.int32)] * 3,
         scratch_shapes=[
             pltpu.VMEM(blocks.shape, blocks.dtype),
             pltpu.VMEM((img_dev, univ, keypts), jnp.bfloat16),
             pltpu.VMEM((GROUP * units + 1, univ, cols), jnp.float32),
             pltpu.SemaphoreType.DMA((slots // per,)),
+            pltpu.SMEM(numbers.shape, numbers.dtype),
+            pltpu.SemaphoreType.DMA(()),
+            pltpu.SMEM((GROUP,), jnp.int32),
         ],
         compiler_params=LIMIT,
         cost_estimate=SHORT,
         name="reverse",
-    )(place, counts, pairs, near, far, blocks)
+    )(numbers, near, far, blocks)
 
     arrived = [exchanged(returns[bits], "img", bits) for bits in range(1, GROUP)]
     part = (img_dev, cols, univ)
@@ -259,22 +315,37 @@
         sent = jnp.where(later, jnp.concatenate(ahead[:2]), jnp.concatenate(ahead[1:]))
         tables.append(exchanged(sent, "img", bits))
 
-    tables, near_sum, back = lax.optimization_barrier((tables, near_sum, back))
+    def forward_scratch(picked):
+        return [
+            pltpu.VMEM((len(picked) * bucket, keypts, cols), jnp.bfloat16),
+            pltpu.VMEM((img_dev + 1, keypts, univ), jnp.float32),
+            pltpu.SemaphoreType.DMA((len(picked) * bucket,)),
+        ]
+
+    early, late = tuple(range(GROUP // 2)), tuple(range(GROUP // 2, GROUP))
+    members, units_of, firsts, _ = lax.optimization_barrier((members, units_of, firsts, near_sum))
+    before = pl.pallas_call(
+        functools.partial(forward_first_kernel, early),
+        in_specs=[SMEM] * 3 + [anywhere] + [VMEM] * len(early),
+        out_specs=VMEM,
+        out_shape=jax.ShapeDtypeStruct((img_dev, keypts, univ), jnp.float32),
+        scratch_shapes=forward_scratch(early),
+        compiler_params=LIMIT,
+        cost_estimate=SHORT,
+        name="forward_first",
+    )(members, units_of, firsts, blocks, *[tables[index] for index in early])
+    last_tables = [tables[index] for index in late]
+    last_tables, near_sum, back = lax.optimization_barrier((last_tables, near_sum, back))
     own, send = pl.pallas_call(
-        functools.partial(forward_kernel, per, devices),
-        in_specs=[SMEM] * 3 + [VMEM] + [anywhere] + [VMEM] * GROUP,
+        functools.partial(forward_last_kernel, late),
+        in_specs=[SMEM] * 4 + [anywhere] + [VMEM] * (2 + len(late)),
         out_specs=[VMEM] * 2,
         out_shape=[jax.ShapeDtypeStruct((img_dev, half, univ), jnp.float32)] * 2,
-        scratch_shapes=[
-            pltpu.VMEM(blocks.shape, blocks.dtype),
-            pltpu.VMEM((GROUP * units, cols, univ), jnp.bfloat16),
-            pltpu.VMEM((img_dev + 1, keypts, univ), jnp.float32),
-            pltpu.SemaphoreType.DMA((slots // per,)),
-        ],
+        scratch_shapes=forward_scratch(late),
         compiler_params=LIMIT,
         cost_estimate=SHORT,
-        name="forward",
-    )(place, counts, pairs, panels, blocks, *tables)
+        name="forward_last",
+    )(place, members, units_of, firsts, blocks, panels, before, *last_tables)
     other_half = exchanged(send, "rep", 1)
 
     field, packed = pl.pallas_call(
@@ -283,8 +354,9 @@
         out_specs=[VMEM] * 2,
         out_shape=[
             jax.ShapeDtypeStruct(panels.shape, jnp.float32),
-            jax.ShapeDtypeStruct((univ // 2 + ROWS, univ), jnp.float32),
+            jax.ShapeDtypeStruct((univ // 2 + 8, univ), jnp.float32),
         ],
+        compiler_params=SMALL,
         name="gram",
     )(own, other_half, near_sum, *back)
     terms = [packed, exchanged(packed, "rep", 1)]
@@ -299,6 +371,7 @@
         out_specs=VMEM,
         out_shape=jax.ShapeDtypeStruct(panels.shape, jnp.float32),
         scratch_shapes=[pltpu.VMEM((univ, univ), jnp.float32)],
+        compiler_params=SMALL,
         name="solve",
     )(*terms, field)
 

time: 81.7 us -> 71.3 us (0.87)
  waiting for transfers between devices: 24.5 us -> 20.3 us
  Pallas kernels: 24.9 us -> 21.3 us
  other arithmetic: 2.89 us -> 0.39 us
  local copies, waits for them, and re-layouts: 2.99 us -> 1.7 us
    ppermute x15, waiting for transfers between devices: 23.9 us -> 18.9 us  [exchanged(): lax.ppermute(value, axis, [(source, source ^ bits) for source in range(co...]
    pallas_call x1, Pallas kernels: 7.86 us -> 5.35 us  [shards(): pl.pallas_call(functools.partial(solve_kernel, 1 / (devices * img_dev * k...]
    pallas_call x1 -> x3, Pallas kernels: 7.49 us -> 9.43 us  [the longest x1 4.7 us: shards(): pl.pallas_call(functools.partial(forward_last_kernel, late), in_specs=[SM...]
    pallas_call x1, Pallas kernels: 2.38 us -> 0.47 us  [shards(): pl.pallas_call(gram_kernel, in_specs=[VMEM] * 5, out_specs=[VMEM] * 2, ou...]
    unnamed x28 -> x7, local copies, waits for them, and re-layouts: 2.92 us -> 1.64 us
    pallas_call x1, Pallas kernels: 7.16 us -> 6.07 us  [shards(): pl.pallas_call(functools.partial(reverse_kernel, per, devices), in_specs=...]
    convert_element_type x1 -> x0, other arithmetic: 1.04 us -> none  [shards(): near = panels.astype(jnp.bfloat16)]
  transfers between devices with their start and end apart: 19 -> 19, of which waited for: 11 -> 13; matrix products, arithmetic and copies ran while one was open for 2% -> 1% of each run, Pallas kernels for 9% -> 15%
where the time goes in v3:
time: 71.3 us; the launch traced here: 70.6 us
  starting transfers between devices  26.1 us (37%)
  Pallas kernels  21.3 us (30%)
  waiting for transfers between devices  20.3 us (28%)
  local copies, waits for them, and re-layouts  1.7 us (2%)
  between operations  0.76 us (1%)
    ppermute x15, waiting for transfers between devices, exchanged(): lax.ppermute(value, axis, [(source, source ^ bits) for source in range(co...  18.9 us
    ppermute x15, starting transfers between devices, exchanged(): lax.ppermute(value, axis, [(source, source ^ bits) for source in range(co...  18.3 us
    ppermute x4, starting transfers between devices, passed_along(): return lax.ppermute(value, axis, pairs)  7.75 us
    pallas_call x1, Pallas kernels, shards(): pl.pallas_call(functools.partial(reverse_kernel, per, devices), in_specs=...  6.07 us
    pallas_call x1, Pallas kernels, shards(): pl.pallas_call(functools.partial(solve_kernel, 1 / (devices * img_dev * k...  5.35 us
    pallas_call x1, Pallas kernels, shards(): pl.pallas_call(functools.partial(forward_last_kernel, late), in_specs=[SM...  4.7 us
    pallas_call x1, Pallas kernels, shards(): pl.pallas_call(functools.partial(forward_first_kernel, early), in_specs=[...  4.66 us
    unnamed x7, local copies, waits for them, and re-layouts  1.64 us
  transfers between devices with their start and end apart: 19, of which 13 were waited for; matrix products, arithmetic and copies ran while one was open for 1% of the time, Pallas kernels for 15%

profile of v3, /device:TPU:0, one launch (start us, length us, event | category | flops | bytes accessed | tf_op | source)
XLA Modules:
  0.0 70.6 jit_solution(1973743933827526458)
XLA Ops:
  0.7 0.9 %copy-done = f32[2,256,128]{2,1,0:T(8,128)S(1)} copy-done((f32[2,256,128]{2,1,0:T(8,128)S(1)}, f32[2,256,128]{2,1,0:T(8,128)}, u32[]{:S(2)}) %copy-start) | copy-done | bytes 262168
  1.6 0.7 copy-done.2
  2.8 4.7 %collective-permute-start.4 = (bf16[2,256,128]{2,1,0:T(8,128)(2,1)S(1)}, bf16[2,256,128]{2,1,0:T(8,128)(2,1)S(1)}, u32[]{:S(2)}, u32[]{:S(2)}) collective-permute-start(bf16[2,256,128]{2,1,0:T(8,128)(2,1)S(1)} %get-tuple-element.43.near), channel_id=1, source_target_pairs={{0,24},{2,26},{4,28},{6,30},{8,0},{10,2},{12,4},{14,6},{16,8},{18,... | collective-permute-start | bytes 393224 | tf_op jit(solution)/shard_map/ppermute | solution.py:25
  7.5 6.1 %reverse.1 = (bf16[4,256,128]{2,1,0:T(8,128)(2,1)S(1)}, bf16[4,256,128]{2,1,0:T(8,128)(2,1)S(1)}, bf16[4,256,128]{2,1,0:T(8,128)(2,1)S(1)}, bf16[4,256,128]{2,1,...) custom-call(s32[8,48]{1,0:T(8,128)S(1)} %get-tuple-element.29.numbers, ...), custom_call_target="tpu_custom_call" | custom-call | flops 1 | bytes 1 | tf_op jit(solution)/shard_map/reverse/pallas_call | solution.py:269
  13.6 2.5 %collective-permute-start.3 = (bf16[4,256,128]{2,1,0:T(8,128)(2,1)S(1)}, bf16[4,256,128]{2,1,0:T(8,128)(2,1)S(1)}, u32[]{:S(2)}, u32[]{:S(2)}) collective-permute-start(bf16[4,256,128]{2,1,0:T(8,128)(2,1)S(1)} %get-tuple-element.36), channel_id=1, source_target_pairs={{0,6},{2,4},{4,2},{6,0},{8,14},{10,12},{12,10},{14,8},{16,22},{18,... | collective-permute-start | bytes 786440 | tf_op jit(solution)/shard_map/ppermute | solution.py:30
  16.1 0.5 collective-permute-start.2
  16.6 0.5 collective-permute-start.1
  17.3 1.6 %collective-permute-start.6 = (bf16[4,256,128]{2,1,0:T(8,128)(2,1)S(1)}, bf16[4,256,128]{2,1,0:T(8,128)(2,1)S(1)}, u32[]{:S(2)}, u32[]{:S(2)}) collective-permute-start(bf16[4,256,128]{2,1,0:T(8,128)(2,1)S(1)} %get-tuple-element.58), channel_id=1, source_target_pairs={{0,2},{2,0},{4,6},{6,4},{8,10},{10,8},{12,14},{14,12},{16,18},{18,... | collective-permute-start | bytes 786440 | tf_op jit(solution)/shard_map/ppermute | solution.py:30
  18.9 1.5 %collective-permute-start.7 = (bf16[4,256,128]{2,1,0:T(8,128)(2,1)S(1)}, bf16[4,256,128]{2,1,0:T(8,128)(2,1)S(1)}, u32[]{:S(2)}, u32[]{:S(2)}) collective-permute-start(bf16[4,256,128]{2,1,0:T(8,128)(2,1)S(1)} %get-tuple-element.57), channel_id=1, source_target_pairs={{0,4},{2,6},{4,0},{6,2},{8,12},{10,14},{12,8},{14,10},{16,20},{18,... | collective-permute-start | bytes 786440 | tf_op jit(solution)/shard_map/ppermute | solution.py:30
  20.4 3.4 %collective-permute-done.3 = bf16[4,256,128]{2,1,0:T(8,128)(2,1)S(1)} collective-permute-done((bf16[4,256,128]{2,1,0:T(8,128)(2,1)S(1)}, bf16[4,256,128]{2,1,0:T(8,128)(2,1)S(1)}, u32[]{:S(2)}, u32[]{:S(2)}) %collective-permute-start.3) | collective-permute-done | bytes 262176 | tf_op jit(solution)/shard_map/ppermute | solution.py:30
  23.7 2.4 %collective-permute-start.8 = (bf16[4,256,128]{2,1,0:T(8,128)(2,1)S(1)}, bf16[4,256,128]{2,1,0:T(8,128)(2,1)S(1)}, u32[]{:S(2)}, u32[]{:S(2)}) collective-permute-start(bf16[4,256,128]{2,1,0:T(8,128)(2,1)S(1)} %get-tuple-element.56), channel_id=1, source_target_pairs={{0,6},{2,4},{4,2},{6,0},{8,14},{10,12},{12,10},{14,8},{16,22},{18,... | collective-permute-start | bytes 786440 | tf_op jit(solution)/shard_map/ppermute | solution.py:30
  26.2 2.4 %collective-permute-done.2 = bf16[4,256,128]{2,1,0:T(8,128)(2,1)S(1)} collective-permute-done((bf16[4,256,128]{2,1,0:T(8,128)(2,1)S(1)}, bf16[4,256,128]{2,1,0:T(8,128)(2,1)S(1)}, u32[]{:S(2)}, u32[]{:S(2)}) %collective-permute-start.2) | collective-permute-done | bytes 262176 | tf_op jit(solution)/shard_map/ppermute | solution.py:30
  28.6 0.8 %collective-permute-done.1 = bf16[4,256,128]{2,1,0:T(8,128)(2,1)S(1)} collective-permute-done((bf16[4,256,128]{2,1,0:T(8,128)(2,1)S(1)}, bf16[4,256,128]{2,1,0:T(8,128)(2,1)S(1)}, u32[]{:S(2)}, u32[]{:S(2)}) %collective-permute-start.1) | collective-permute-done | bytes 262176 | tf_op jit(solution)/shard_map/ppermute | solution.py:30
  29.7 1.1 %collective-permute-start.9 = (bf16[2,256,128]{2,1,0:T(8,128)(2,1)S(1)}, bf16[2,256,128]{2,1,0:T(8,128)(2,1)S(1)}, u32[]{:S(2)}, u32[]{:S(2)}) collective-permute-start(bf16[2,256,128]{2,1,0:T(8,128)(2,1)S(1)} %get-tuple-element.54), channel_id=1, source_target_pairs={{0,8},{2,10},{4,12},{6,14},{8,16},{10,18},{12,20},{14,22},{16,24},... | collective-permute-start | bytes 393224 | tf_op jit(solution)/shard_map/ppermute | solution.py:25
  30.8 2.0 %collective-permute-start.10 = (bf16[2,256,128]{2,1,0:T(8,128)(2,1)S(1)}, bf16[2,256,128]{2,1,0:T(8,128)(2,1)S(1)}, u32[]{:S(2)}, u32[]{:S(2)}) collective-permute-start(bf16[2,256,128]{2,1,0:T(8,128)(2,1)S(1)} %get-tuple-element.53), channel_id=1, source_target_pairs={{0,16},{2,18},{4,20},{6,22},{8,24},{10,26},{12,28},{14,30},{16,0},... | collective-permute-start | bytes 393224 | tf_op jit(solution)/shard_map/ppermute | solution.py:25
  32.8 2.2 %collective-permute-done.6.rest_1_ = bf16[4,256,128]{2,1,0:T(8,128)(2,1)S(1)} collective-permute-done((bf16[4,256,128]{2,1,0:T(8,128)(2,1)S(1)}, bf16[4,256,128]{2,1,0:T(8,128)(2,1)S(1)}, u32[]{:S(2)}, u32[]{:S(2)}) %collective-permute-start.6) | collective-permute-done | bytes 262176 | tf_op jit(solution)/shard_map/ppermute | solution.py:30
  35.0 4.7 %forward_first.1.before = f32[2,512,128]{2,1,0:T(8,128)S(1)} custom-call(s32[48]{0:T(128)S(1)} %get-tuple-element.37.members, s32[48]{0:T(128)S(1)} %get-tuple-element.38.units, s32[48]{0:T(128)S(1)} %get-tuple-element.39.firsts, bf16[48,512,256]{2,1,0:T(8,128)(2,1)} %blocks.5, bf16[4,256,128]{2,1,0:T(8,128)(2,1)S(1)} %constant_dynamic-update-slice_fusion.rest_0_, ...), custom_call_target="tpu_custom_call" | custom-call | flops 1 | bytes 1 | tf_op jit(solution)/shard_map/forward_first/pallas_call | solution.py:327
  39.8 1.4 %collective-permute-done.10.back_two = bf16[2,256,128]{2,1,0:T(8,128)(2,1)S(1)} collective-permute-done((bf16[2,256,128]{2,1,0:T(8,128)(2,1)S(1)}, bf16[2,256,128]{2,1,0:T(8,128)(2,1)S(1)}, u32[]{:S(2)}, u32[]{:S(2)}) %collective-permute-start.10) | collective-permute-done | bytes 131104 | tf_op jit(solution)/shard_map/ppermute | solution.py:25
  41.2 4.7 %forward_last.1 = (f32[2,256,128]{2,1,0:T(8,128)S(1)}, f32[2,256,128]{2,1,0:T(8,128)S(1)}) custom-call(s32[2]{0:T(128)S(1)} %pad_add_fusion.place, s32[48]{0:T(128)S(1)} %get-tuple-element.37.members, s32[48]{0:T(128)S(1)} %get-tuple-element.38.units, s32[48]{0:T(128)S(1)} %get-tuple-element.39.firsts, bf16[48,512,256]{2,1,0:T(8,128)(2,1)} %blocks.5, ...), custom_call_target="tpu_custom_call" | custom-call | flops 1 | bytes 1 | tf_op jit(solution)/shard_map/forward_last/pallas_call | solution.py:339
  46.0 1.5 %collective-permute-done.11.other = f32[2,256,128]{2,1,0:T(8,128)S(1)} collective-permute-done((f32[2,256,128]{2,1,0:T(8,128)S(1)}, f32[2,256,128]{2,1,0:T(8,128)S(1)}, u32[]{:S(2)}, u32[]{:S(2)}) %collective-permute-start.11) | collective-permute-done | bytes 262176 | tf_op jit(solution)/shard_map/ppermute | solution.py:30
  47.5 0.5 gram.1
  48.1 1.1 %collective-permute-done.12 = f32[72,128]{1,0:T(8,128)S(1)} collective-permute-done((f32[72,128]{1,0:T(8,128)S(1)}, f32[72,128]{1,0:T(8,128)S(1)}, u32[]{:S(2)}, u32[]{:S(2)}) %collective-permute-start.12) | collective-permute-done | bytes 36896 | tf_op jit(solution)/shard_map/ppermute | solution.py:30
  49.2 2.1 %collective-permute-start.15 = (f32[72,128]{1,0:T(8,128)S(1)}, f32[72,128]{1,0:T(8,128)S(1)}, u32[]{:S(2)}, u32[]{:S(2)}) collective-permute-start(f32[72,128]{1,0:T(8,128)S(1)} %add.50), channel_id=1, source_target_pairs={{0,6},{2,4},{4,2},{6,0},{8,14},{10,12},{12,10},{14,8},{16,22},{18,... | collective-permute-start | bytes 110600 | tf_op jit(solution)/shard_map/ppermute | solution.py:30
  51.3 2.0 %collective-permute-start.14 = (f32[72,128]{1,0:T(8,128)S(1)}, f32[72,128]{1,0:T(8,128)S(1)}, u32[]{:S(2)}, u32[]{:S(2)}) collective-permute-start(f32[72,128]{1,0:T(8,128)S(1)} %add.50), channel_id=1, source_target_pairs={{0,4},{2,6},{4,0},{6,2},{8,12},{10,14},{12,8},{14,10},{16,20},{18,... | collective-permute-start | bytes 110600 | tf_op jit(solution)/shard_map/ppermute | solution.py:30
  53.4 0.7 %collective-permute-done.15 = f32[72,128]{1,0:T(8,128)S(1)} collective-permute-done((f32[72,128]{1,0:T(8,128)S(1)}, f32[72,128]{1,0:T(8,128)S(1)}, u32[]{:S(2)}, u32[]{:S(2)}) %collective-permute-start.15) | collective-permute-done | bytes 36896 | tf_op jit(solution)/shard_map/ppermute | solution.py:30
  54.1 1.2 %collective-permute-done.14 = f32[72,128]{1,0:T(8,128)S(1)} collective-permute-done((f32[72,128]{1,0:T(8,128)S(1)}, f32[72,128]{1,0:T(8,128)S(1)}, u32[]{:S(2)}, u32[]{:S(2)}) %collective-permute-start.14) | collective-permute-done | bytes 36896 | tf_op jit(solution)/shard_map/ppermute | solution.py:30
  55.3 2.0 %collective-permute-done.13 = f32[72,128]{1,0:T(8,128)S(1)} collective-permute-done((f32[72,128]{1,0:T(8,128)S(1)}, f32[72,128]{1,0:T(8,128)S(1)}, u32[]{:S(2)}, u32[]{:S(2)}) %collective-permute-start.13) | collective-permute-done | bytes 36896 | tf_op jit(solution)/shard_map/ppermute | solution.py:30
  57.4 2.1 %collective-permute-start.17 = (f32[72,128]{1,0:T(8,128)S(1)}, f32[72,128]{1,0:T(8,128)S(1)}, u32[]{:S(2)}, u32[]{:S(2)}) collective-permute-start(f32[72,128]{1,0:T(8,128)S(1)} %add_add_fusion.rest_0_), channel_id=1, source_target_pairs={{0,16},{2,18},{4,20},{6,22},{8,24},{10,26},{12,28},{14,30},{16,0},... | collective-permute-start | bytes 110600 | tf_op jit(solution)/shard_map/ppermute | solution.py:30
  59.5 2.3 %collective-permute-start.18 = (f32[72,128]{1,0:T(8,128)S(1)}, f32[72,128]{1,0:T(8,128)S(1)}, u32[]{:S(2)}, u32[]{:S(2)}) collective-permute-start(f32[72,128]{1,0:T(8,128)S(1)} %add_add_fusion.rest_0_), channel_id=1, source_target_pairs={{0,24},{2,26},{4,28},{6,30},{8,16},{10,18},{12,20},{14,22},{16,8},... | collective-permute-start | bytes 110600 | tf_op jit(solution)/shard_map/ppermute | solution.py:30
  61.8 0.9 %collective-permute-done.17.rest_2_ = f32[72,128]{1,0:T(8,128)S(1)} collective-permute-done((f32[72,128]{1,0:T(8,128)S(1)}, f32[72,128]{1,0:T(8,128)S(1)}, u32[]{:S(2)}, u32[]{:S(2)}) %collective-permute-start.17) | collective-permute-done | bytes 36896 | tf_op jit(solution)/shard_map/ppermute | solution.py:30
  62.7 2.6 %collective-permute-done.18.rest_3_ = f32[72,128]{1,0:T(8,128)S(1)} collective-permute-done((f32[72,128]{1,0:T(8,128)S(1)}, f32[72,128]{1,0:T(8,128)S(1)}, u32[]{:S(2)}, u32[]{:S(2)}) %collective-permute-start.18) | collective-permute-done | bytes 36896 | tf_op jit(solution)/shard_map/ppermute | solution.py:30
  65.3 5.3 %solve.1 = f32[2,256,128]{2,1,0:T(8,128)} custom-call(f32[72,128]{1,0:T(8,128)S(1)} %add_add_fusion.rest_0_, f32[72,128]{1,0:T(8,128)S(1)} %collective-permute-done.16.rest_1_, f32[72,128]{1,0:T(8,128)S(1)} %collective-permute-done.17.rest_2_, f32[72,128]{1,0:T(8,128)S(1)} %collective-permute-done.18.rest_3_, f32[2,256,128]{2,1,0:T(8,128)S(1)} %get-tuple-element.52.rest_4_), custom_call_target="tpu_custom_call" | custom-call | tf_op jit(solution)/shard_map/solve/pallas_call | solution.py:368
  (26 shorter events, 1.4 us)
Async XLA Ops:
  0.7 1.0 %copy-start = (f32[2,256,128]{2,1,0:T(8,128)S(1)}, f32[2,256,128]{2,1,0:T(8,128)}, u32[]{:S(2)}) copy-start(f32[2,256,128]{2,1,0:T(8,128)} %panels.3) | copy-start | bytes 786436
  1.6 0.7 copy-start.2
  2.4 5.1 %collective-permute-start = (bf16[2,256,128]{2,1,0:T(8,128)(2,1)S(1)}, bf16[2,256,128]{2,1,0:T(8,128)(2,1)S(1)}, u32[]{:S(2)}, u32[]{:S(2)}) collective-permute-start(bf16[2,256,128]{2,1,0:T(8,128)(2,1)S(1)} %get-tuple-element.43.near), channel_id=1, source_target_pairs={{0,1},{1,0},{2,3},{3,2},{4,5},{5,4},{6,7},{7,6},{8,9},{9,8},{10,11... | collective-permute-start | bytes 393224 | tf_op jit(solution)/shard_map/ppermute | solution.py:30
  2.8 14.3 %collective-permute-start.4 = (bf16[2,256,128]{2,1,0:T(8,128)(2,1)S(1)}, bf16[2,256,128]{2,1,0:T(8,128)(2,1)S(1)}, u32[]{:S(2)}, u32[]{:S(2)}) collective-permute-start(bf16[2,256,128]{2,1,0:T(8,128)(2,1)S(1)} %get-tuple-element.43.near), channel_id=1, source_target_pairs={{0,24},{2,26},{4,28},{6,30},{8,0},{10,2},{12,4},{14,6},{16,8},{18,... | collective-permute-start | bytes 393224 | tf_op jit(solution)/shard_map/ppermute | solution.py:25
  7.5 9.7 %collective-permute-start.5 = (bf16[2,256,128]{2,1,0:T(8,128)(2,1)S(1)}, bf16[2,256,128]{2,1,0:T(8,128)(2,1)S(1)}, u32[]{:S(2)}, u32[]{:S(2)}) collective-permute-start(bf16[2,256,128]{2,1,0:T(8,128)(2,1)S(1)} %get-tuple-element.43.near), channel_id=1, source_target_pairs={{0,16},{2,18},{4,20},{6,22},{8,24},{10,26},{12,28},{14,30},{16,0},... | collective-permute-start | bytes 393224 | tf_op jit(solution)/shard_map/ppermute | solution.py:25
  7.5 33.7 %copy-start.1 = (f32[2,256,128]{2,1,0:T(8,128)S(1)}, f32[2,256,128]{2,1,0:T(8,128)}, u32[]{:S(2)}) copy-start(f32[2,256,128]{2,1,0:T(8,128)} %panels.3) | copy-start | bytes 786436
  13.6 10.2 %collective-permute-start.3 = (bf16[4,256,128]{2,1,0:T(8,128)(2,1)S(1)}, bf16[4,256,128]{2,1,0:T(8,128)(2,1)S(1)}, u32[]{:S(2)}, u32[]{:S(2)}) collective-permute-start(bf16[4,256,128]{2,1,0:T(8,128)(2,1)S(1)} %get-tuple-element.36), channel_id=1, source_target_pairs={{0,6},{2,4},{4,2},{6,0},{8,14},{10,12},{12,10},{14,8},{16,22},{18,... | collective-permute-start | bytes 786440 | tf_op jit(solution)/shard_map/ppermute | solution.py:30
  16.1 12.5 %collective-permute-start.2 = (bf16[4,256,128]{2,1,0:T(8,128)(2,1)S(1)}, bf16[4,256,128]{2,1,0:T(8,128)(2,1)S(1)}, u32[]{:S(2)}, u32[]{:S(2)}) collective-permute-start(bf16[4,256,128]{2,1,0:T(8,128)(2,1)S(1)} %get-tuple-element.35), channel_id=1, source_target_pairs={{0,4},{2,6},{4,0},{6,2},{8,12},{10,14},{12,8},{14,10},{16,20},{18,... | collective-permute-start | bytes 786440 | tf_op jit(solution)/shard_map/ppermute | solution.py:30
  16.6 12.8 %collective-permute-start.1 = (bf16[4,256,128]{2,1,0:T(8,128)(2,1)S(1)}, bf16[4,256,128]{2,1,0:T(8,128)(2,1)S(1)}, u32[]{:S(2)}, u32[]{:S(2)}) collective-permute-start(bf16[4,256,128]{2,1,0:T(8,128)(2,1)S(1)} %get-tuple-element.34), channel_id=1, source_target_pairs={{0,2},{2,0},{4,6},{6,4},{8,10},{10,8},{12,14},{14,12},{16,18},{18,... | collective-permute-start | bytes 786440 | tf_op jit(solution)/shard_map/ppermute | solution.py:30
  17.3 17.7 %collective-permute-start.6 = (bf16[4,256,128]{2,1,0:T(8,128)(2,1)S(1)}, bf16[4,256,128]{2,1,0:T(8,128)(2,1)S(1)}, u32[]{:S(2)}, u32[]{:S(2)}) collective-permute-start(bf16[4,256,128]{2,1,0:T(8,128)(2,1)S(1)} %get-tuple-element.58), channel_id=1, source_target_pairs={{0,2},{2,0},{4,6},{6,4},{8,10},{10,8},{12,14},{14,12},{16,18},{18,... | collective-permute-start | bytes 786440 | tf_op jit(solution)/shard_map/ppermute | solution.py:30
  18.9 20.8 %collective-permute-start.7 = (bf16[4,256,128]{2,1,0:T(8,128)(2,1)S(1)}, bf16[4,256,128]{2,1,0:T(8,128)(2,1)S(1)}, u32[]{:S(2)}, u32[]{:S(2)}) collective-permute-start(bf16[4,256,128]{2,1,0:T(8,128)(2,1)S(1)} %get-tuple-element.57), channel_id=1, source_target_pairs={{0,4},{2,6},{4,0},{6,2},{8,12},{10,14},{12,8},{14,10},{16,20},{18,... | collective-permute-start | bytes 786440 | tf_op jit(solution)/shard_map/ppermute | solution.py:30
  23.7 16.1 %collective-permute-start.8 = (bf16[4,256,128]{2,1,0:T(8,128)(2,1)S(1)}, bf16[4,256,128]{2,1,0:T(8,128)(2,1)S(1)}, u32[]{:S(2)}, u32[]{:S(2)}) collective-permute-start(bf16[4,256,128]{2,1,0:T(8,128)(2,1)S(1)} %get-tuple-element.56), channel_id=1, source_target_pairs={{0,6},{2,4},{4,2},{6,0},{8,14},{10,12},{12,10},{14,8},{16,22},{18,... | collective-permute-start | bytes 786440 | tf_op jit(solution)/shard_map/ppermute | solution.py:30
  29.7 10.2 %collective-permute-start.9 = (bf16[2,256,128]{2,1,0:T(8,128)(2,1)S(1)}, bf16[2,256,128]{2,1,0:T(8,128)(2,1)S(1)}, u32[]{:S(2)}, u32[]{:S(2)}) collective-permute-start(bf16[2,256,128]{2,1,0:T(8,128)(2,1)S(1)} %get-tuple-element.54), channel_id=1, source_target_pairs={{0,8},{2,10},{4,12},{6,14},{8,16},{10,18},{12,20},{14,22},{16,24},... | collective-permute-start | bytes 393224 | tf_op jit(solution)/shard_map/ppermute | solution.py:25
  30.8 10.5 %collective-permute-start.10 = (bf16[2,256,128]{2,1,0:T(8,128)(2,1)S(1)}, bf16[2,256,128]{2,1,0:T(8,128)(2,1)S(1)}, u32[]{:S(2)}, u32[]{:S(2)}) collective-permute-start(bf16[2,256,128]{2,1,0:T(8,128)(2,1)S(1)} %get-tuple-element.53), channel_id=1, source_target_pairs={{0,16},{2,18},{4,20},{6,22},{8,24},{10,26},{12,28},{14,30},{16,0},... | collective-permute-start | bytes 393224 | tf_op jit(solution)/shard_map/ppermute | solution.py:25
  45.9 1.6 %collective-permute-start.11 = (f32[2,256,128]{2,1,0:T(8,128)S(1)}, f32[2,256,128]{2,1,0:T(8,128)S(1)}, u32[]{:S(2)}, u32[]{:S(2)}) collective-permute-start(f32[2,256,128]{2,1,0:T(8,128)S(1)} %get-tuple-element.47), channel_id=1, source_target_pairs={{0,1},{1,0},{2,3},{3,2},{4,5},{5,4},{6,7},{7,6},{8,9},{9,8},{10,11... | collective-permute-start | bytes 786440 | tf_op jit(solution)/shard_map/ppermute | solution.py:30
  48.0 1.2 %collective-permute-start.12 = (f32[72,128]{1,0:T(8,128)S(1)}, f32[72,128]{1,0:T(8,128)S(1)}, u32[]{:S(2)}, u32[]{:S(2)}) collective-permute-start(f32[72,128]{1,0:T(8,128)S(1)} %get-tuple-element.51), channel_id=1, source_target_pairs={{0,1},{1,0},{2,3},{3,2},{4,5},{5,4},{6,7},{7,6},{8,9},{9,8},{10,11... | collective-permute-start | bytes 110600 | tf_op jit(solution)/shard_map/ppermute | solution.py:30
  49.2 4.9 %collective-permute-start.15 = (f32[72,128]{1,0:T(8,128)S(1)}, f32[72,128]{1,0:T(8,128)S(1)}, u32[]{:S(2)}, u32[]{:S(2)}) collective-permute-start(f32[72,128]{1,0:T(8,128)S(1)} %add.50), channel_id=1, source_target_pairs={{0,6},{2,4},{4,2},{6,0},{8,14},{10,12},{12,10},{14,8},{16,22},{18,... | collective-permute-start | bytes 110600 | tf_op jit(solution)/shard_map/ppermute | solution.py:30
  51.3 4.0 %collective-permute-start.14 = (f32[72,128]{1,0:T(8,128)S(1)}, f32[72,128]{1,0:T(8,128)S(1)}, u32[]{:S(2)}, u32[]{:S(2)}) collective-permute-start(f32[72,128]{1,0:T(8,128)S(1)} %add.50), channel_id=1, source_target_pairs={{0,4},{2,6},{4,0},{6,2},{8,12},{10,14},{12,8},{14,10},{16,20},{18,... | collective-permute-start | bytes 110600 | tf_op jit(solution)/shard_map/ppermute | solution.py:30
  53.4 4.0 %collective-permute-start.13 = (f32[72,128]{1,0:T(8,128)S(1)}, f32[72,128]{1,0:T(8,128)S(1)}, u32[]{:S(2)}, u32[]{:S(2)}) collective-permute-start(f32[72,128]{1,0:T(8,128)S(1)} %add.50), channel_id=1, source_target_pairs={{0,2},{2,0},{4,6},{6,4},{8,10},{10,8},{12,14},{14,12},{16,18},{18,... | collective-permute-start | bytes 110600 | tf_op jit(solution)/shard_map/ppermute | solution.py:30
  57.3 4.5 %collective-permute-start.16 = (f32[72,128]{1,0:T(8,128)S(1)}, f32[72,128]{1,0:T(8,128)S(1)}, u32[]{:S(2)}, u32[]{:S(2)}) collective-permute-start(f32[72,128]{1,0:T(8,128)S(1)} %add_add_fusion.rest_0_), channel_id=1, source_target_pairs={{0,8},{2,10},{4,12},{6,14},{8,0},{10,2},{12,4},{14,6},{16,24},{18,... | collective-permute-start | bytes 110600 | tf_op jit(solution)/shard_map/ppermute | solution.py:30
  57.4 5.3 %collective-permute-start.17 = (f32[72,128]{1,0:T(8,128)S(1)}, f32[72,128]{1,0:T(8,128)S(1)}, u32[]{:S(2)}, u32[]{:S(2)}) collective-permute-start(f32[72,128]{1,0:T(8,128)S(1)} %add_add_fusion.rest_0_), channel_id=1, source_target_pairs={{0,16},{2,18},{4,20},{6,22},{8,24},{10,26},{12,28},{14,30},{16,0},... | collective-permute-start | bytes 110600 | tf_op jit(solution)/shard_map/ppermute | solution.py:30
  59.5 5.8 %collective-permute-start.18 = (f32[72,128]{1,0:T(8,128)S(1)}, f32[72,128]{1,0:T(8,128)S(1)}, u32[]{:S(2)}, u32[]{:S(2)}) collective-permute-start(f32[72,128]{1,0:T(8,128)S(1)} %add_add_fusion.rest_0_), channel_id=1, source_target_pairs={{0,24},{2,26},{4,28},{6,30},{8,16},{10,18},{12,20},{14,22},{16,8},... | collective-permute-start | bytes 110600 | tf_op jit(solution)/shard_map/ppermute | solution.py:30

commit v4 on v3

--- a/solution.py
+++ b/solution.py
@@ -115,6 +115,7 @@
 
     for at in range(len(listed)):
         fetch(at).start()
+    total[...] = jnp.zeros_like(total)
     for at, target in enumerate(listed):
         if at % WAIT == 0:
             for more in range(at, min(at + WAIT, len(listed))):
@@ -127,17 +128,22 @@
 
 def forward_first_kernel(picked, members, units, firsts, blocks, *rest):
     tables, (sums, kept, total, landed) = rest[: len(picked)], rest[len(picked) :]
-    total[...] = jnp.zeros_like(total)
     forward_slots(picked, members, units, firsts, blocks, tables, kept, total, landed)
     for image in range(sums.shape[0]):
         sums[image] = total[image]
+
+
+def forward_next_kernel(picked, members, units, firsts, blocks, before, *rest):
+    tables, (sums, kept, total, landed) = rest[: len(picked)], rest[len(picked) :]
+    forward_slots(picked, members, units, firsts, blocks, tables, kept, total, landed)
+    for image in range(sums.shape[0]):
+        sums[image] = before[image] + total[image]
 
 
 def forward_last_kernel(picked, place, members, units, firsts, blocks, panels, before, *rest):
     tables, (own, send, kept, total, landed) = rest[: len(picked)], rest[len(picked) :]
     core = place[0]
     img_dev, half = panels.shape[0], panels.shape[1]
-    total[...] = jnp.zeros_like(total)
     forward_slots(picked, members, units, firsts, blocks, tables, kept, total, landed)
     near_rows = pl.ds(pl.multiple_of(core * half, half), half)
     far_rows = pl.ds(pl.multiple_of((1 - core) * half, half), half)
@@ -310,11 +316,6 @@
     ]
     *ahead, _ = lax.optimization_barrier((*ahead, returns[0]))
     tables = [jnp.concatenate(ahead[1:])]
-    for bits in range(1, GROUP):
-        later = member > (member ^ bits)
-        sent = jnp.where(later, jnp.concatenate(ahead[:2]), jnp.concatenate(ahead[1:]))
-        tables.append(exchanged(sent, "img", bits))
-
     def forward_scratch(picked):
         return [
             pltpu.VMEM((len(picked) * bucket, keypts, cols), jnp.bfloat16),
@@ -322,18 +323,34 @@
             pltpu.SemaphoreType.DMA((len(picked) * bucket,)),
         ]
 
-    early, late = tuple(range(GROUP // 2)), tuple(range(GROUP // 2, GROUP))
-    members, units_of, firsts, _ = lax.optimization_barrier((members, units_of, firsts, near_sum))
     before = pl.pallas_call(
-        functools.partial(forward_first_kernel, early),
-        in_specs=[SMEM] * 3 + [anywhere] + [VMEM] * len(early),
+        functools.partial(forward_first_kernel, (0,)),
+        in_specs=[SMEM] * 3 + [anywhere, VMEM],
         out_specs=VMEM,
         out_shape=jax.ShapeDtypeStruct((img_dev, keypts, univ), jnp.float32),
-        scratch_shapes=forward_scratch(early),
+        scratch_shapes=forward_scratch((0,)),
         compiler_params=LIMIT,
         cost_estimate=SHORT,
         name="forward_first",
-    )(members, units_of, firsts, blocks, *[tables[index] for index in early])
+    )(members, units_of, firsts, blocks, tables[0])
+    for bits in range(1, GROUP):
+        later = member > (member ^ bits)
+        if bits == GROUP - 1:
+            *ahead, before, arrived[1] = lax.optimization_barrier((*ahead, before, arrived[1]))
+        sent = jnp.where(later, jnp.concatenate(ahead[:2]), jnp.concatenate(ahead[1:]))
+        tables.append(exchanged(sent, "img", bits))
+
+    middle, late = tuple(range(1, GROUP - 1)), (GROUP - 1,)
+    before = pl.pallas_call(
+        functools.partial(forward_next_kernel, middle),
+        in_specs=[SMEM] * 3 + [anywhere] + [VMEM] * (1 + len(middle)),
+        out_specs=VMEM,
+        out_shape=jax.ShapeDtypeStruct((img_dev, keypts, univ), jnp.float32),
+        scratch_shapes=forward_scratch(middle),
+        compiler_params=LIMIT,
+        cost_estimate=SHORT,
+        name="forward_next",
+    )(members, units_of, firsts, blocks, before, *[tables[index] for index in middle])
     last_tables = [tables[index] for index in late]
     last_tables, near_sum, back = lax.optimization_barrier((last_tables, near_sum, back))
     own, send = pl.pallas_call(

time: 71.3 us -> 68.7 us (0.964)
  waiting for transfers between devices: 20.3 us -> 15.9 us
  Pallas kernels: 21.3 us -> 24.3 us
    pallas_call x1 -> x2, Pallas kernels: 4.66 us -> 8.91 us  [the longest x1 5.4 us: shards(): pl.pallas_call(functools.partial(forward_next_kernel, middle), in_specs=[...]
    ppermute x15, waiting for transfers between devices: 18.9 us -> 15.9 us  [exchanged(): lax.ppermute(value, axis, [(source, source ^ bits) for source in range(co...]
    ppermute x4, waiting for transfers between devices: 1.4 us -> 0.01 us  [passed_along(): return lax.ppermute(value, axis, pairs)]
    pallas_call x1, Pallas kernels: 4.7 us -> 3.43 us  [shards(): pl.pallas_call(functools.partial(forward_last_kernel, late), in_specs=[SM...]
  transfers between devices with their start and end apart: 19 -> 19, of which waited for: 13 -> 9; matrix products, arithmetic and copies ran while one was open for 1% -> 1% of each run, Pallas kernels for 15% -> 22%
where the time goes in v4:
time: 68.7 us; the launch traced here: 68.6 us
  starting transfers between devices  25.5 us (37%)
  Pallas kernels  24.3 us (35%)
  waiting for transfers between devices  15.9 us (23%)
  local copies, waits for them, and re-layouts  1.7 us (2%)
  between operations  0.8 us (1%)
    ppermute x15, starting transfers between devices, exchanged(): lax.ppermute(value, axis, [(source, source ^ bits) for source in range(co...  17.8 us
    ppermute x15, waiting for transfers between devices, exchanged(): lax.ppermute(value, axis, [(source, source ^ bits) for source in range(co...  15.9 us
    ppermute x4, starting transfers between devices, passed_along(): return lax.ppermute(value, axis, pairs)  7.69 us
    pallas_call x1, Pallas kernels, shards(): pl.pallas_call(functools.partial(reverse_kernel, per, devices), in_specs=...  6.04 us
    pallas_call x1, Pallas kernels, shards(): pl.pallas_call(functools.partial(forward_next_kernel, middle), in_specs=[...  5.4 us
    pallas_call x1, Pallas kernels, shards(): pl.pallas_call(functools.partial(solve_kernel, 1 / (devices * img_dev * k...  5.35 us
    pallas_call x1, Pallas kernels, shards(): pl.pallas_call(functools.partial(forward_first_kernel, (0,)), in_specs=[S...  3.51 us
    pallas_call x1, Pallas kernels, shards(): pl.pallas_call(functools.partial(forward_last_kernel, late), in_specs=[SM...  3.43 us
  transfers between devices with their start and end apart: 19, of which 9 were waited for; matrix products, arithmetic and copies ran while one was open for 1% of the time, Pallas kernels for 22%

profile of v4, /device:TPU:0, one launch (start us, length us, event | category | flops | bytes accessed | tf_op | source)
XLA Modules:
  0.0 68.6 jit_solution(8356749829365510190)
XLA Ops:
  0.7 0.9 %copy-done = f32[2,256,128]{2,1,0:T(8,128)S(1)} copy-done((f32[2,256,128]{2,1,0:T(8,128)S(1)}, f32[2,256,128]{2,1,0:T(8,128)}, u32[]{:S(2)}) %copy-start) | copy-done | bytes 262168
  1.6 0.7 copy-done.2
  2.4 0.5 collective-permute-start
  2.8 4.7 %collective-permute-start.1 = (bf16[2,256,128]{2,1,0:T(8,128)(2,1)S(1)}, bf16[2,256,128]{2,1,0:T(8,128)(2,1)S(1)}, u32[]{:S(2)}, u32[]{:S(2)}) collective-permute-start(bf16[2,256,128]{2,1,0:T(8,128)(2,1)S(1)} %get-tuple-element.40.near), channel_id=1, source_target_pairs={{0,24},{2,26},{4,28},{6,30},{8,0},{10,2},{12,4},{14,6},{16,8},{18,... | collective-permute-start | bytes 393224 | tf_op jit(solution)/shard_map/ppermute | solution.py:25
  7.5 6.0 %reverse.1 = (bf16[4,256,128]{2,1,0:T(8,128)(2,1)S(1)}, bf16[4,256,128]{2,1,0:T(8,128)(2,1)S(1)}, bf16[4,256,128]{2,1,0:T(8,128)(2,1)S(1)}, bf16[4,256,128]{2,1,...) custom-call(s32[8,48]{1,0:T(8,128)S(1)} %get-tuple-element.29.numbers, ...), custom_call_target="tpu_custom_call" | custom-call | flops 1 | bytes 1 | tf_op jit(solution)/shard_map/reverse/pallas_call | solution.py:275
  13.5 1.6 %collective-permute-start.3 = (bf16[4,256,128]{2,1,0:T(8,128)(2,1)S(1)}, bf16[4,256,128]{2,1,0:T(8,128)(2,1)S(1)}, u32[]{:S(2)}, u32[]{:S(2)}) collective-permute-start(bf16[4,256,128]{2,1,0:T(8,128)(2,1)S(1)} %get-tuple-element.38), channel_id=1, source_target_pairs={{0,4},{2,6},{4,0},{6,2},{8,12},{10,14},{12,8},{14,10},{16,20},{18,... | collective-permute-start | bytes 786440 | tf_op jit(solution)/shard_map/ppermute | solution.py:30
  15.1 1.5 %collective-permute-start.7 = (bf16[4,256,128]{2,1,0:T(8,128)(2,1)S(1)}, bf16[4,256,128]{2,1,0:T(8,128)(2,1)S(1)}, u32[]{:S(2)}, u32[]{:S(2)}) collective-permute-start(bf16[4,256,128]{2,1,0:T(8,128)(2,1)S(1)} %get-tuple-element.43), channel_id=1, source_target_pairs={{0,2},{2,0},{4,6},{6,4},{8,10},{10,8},{12,14},{14,12},{16,18},{18,... | collective-permute-start | bytes 786440 | tf_op jit(solution)/shard_map/ppermute | solution.py:30
  16.6 0.5 collective-permute-start.8
  17.3 1.6 %collective-permute-start.4 = (bf16[4,256,128]{2,1,0:T(8,128)(2,1)S(1)}, bf16[4,256,128]{2,1,0:T(8,128)(2,1)S(1)}, u32[]{:S(2)}, u32[]{:S(2)}) collective-permute-start(bf16[4,256,128]{2,1,0:T(8,128)(2,1)S(1)} %get-tuple-element.57), channel_id=1, source_target_pairs={{0,2},{2,0},{4,6},{6,4},{8,10},{10,8},{12,14},{14,12},{16,18},{18,... | collective-permute-start | bytes 786440 | tf_op jit(solution)/shard_map/ppermute | solution.py:30
  18.8 1.5 %collective-permute-start.5 = (bf16[4,256,128]{2,1,0:T(8,128)(2,1)S(1)}, bf16[4,256,128]{2,1,0:T(8,128)(2,1)S(1)}, u32[]{:S(2)}, u32[]{:S(2)}) collective-permute-start(bf16[4,256,128]{2,1,0:T(8,128)(2,1)S(1)} %get-tuple-element.56), channel_id=1, source_target_pairs={{0,4},{2,6},{4,0},{6,2},{8,12},{10,14},{12,8},{14,10},{16,20},{18,... | collective-permute-start | bytes 786440 | tf_op jit(solution)/shard_map/ppermute | solution.py:30
  20.3 3.5 %forward_first.1.before = f32[2,512,128]{2,1,0:T(8,128)S(1)} custom-call(s32[48]{0:T(128)S(1)} %get-tuple-element.31.members, s32[48]{0:T(128)S(1)} %get-tuple-element.32.units, s32[48]{0:T(128)S(1)} %get-tuple-element.33.firsts, bf16[48,512,256]{2,1,0:T(8,128)(2,1)} %blocks.7, bf16[4,256,128]{2,1,0:T(8,128)(2,1)S(1)} %constant_dynamic-update-slice_fusion.rest_0_), custom_call_target="tpu_custom_call" | custom-call | flops 1 | bytes 1 | tf_op jit(solution)/shard_map/forward_first/pallas_call | solution.py:326
  23.9 2.1 %collective-permute-start.6 = (bf16[4,256,128]{2,1,0:T(8,128)(2,1)S(1)}, bf16[4,256,128]{2,1,0:T(8,128)(2,1)S(1)}, u32[]{:S(2)}, u32[]{:S(2)}) collective-permute-start(bf16[4,256,128]{2,1,0:T(8,128)(2,1)S(1)} %maximum_select_fusion), channel_id=1, source_target_pairs={{0,6},{2,4},{4,2},{6,0},{8,14},{10,12},{12,10},{14,8},{16,22},{18,... | collective-permute-start | bytes 786440 | tf_op jit(solution)/shard_map/ppermute | solution.py:30
  26.0 3.9 %collective-permute-done.8 = bf16[4,256,128]{2,1,0:T(8,128)(2,1)S(1)} collective-permute-done((bf16[4,256,128]{2,1,0:T(8,128)(2,1)S(1)}, bf16[4,256,128]{2,1,0:T(8,128)(2,1)S(1)}, u32[]{:S(2)}, u32[]{:S(2)}) %collective-permute-start.8) | collective-permute-done | bytes 262176 | tf_op jit(solution)/shard_map/ppermute | solution.py:30
  29.9 0.2 fusion.9
  30.2 3.0 %collective-permute-start.10 = (bf16[2,256,128]{2,1,0:T(8,128)(2,1)S(1)}, bf16[2,256,128]{2,1,0:T(8,128)(2,1)S(1)}, u32[]{:S(2)}, u32[]{:S(2)}) collective-permute-start(bf16[2,256,128]{2,1,0:T(8,128)(2,1)S(1)} %get-tuple-element.53), channel_id=1, source_target_pairs={{0,16},{2,18},{4,20},{6,22},{8,24},{10,26},{12,28},{14,30},{16,0},... | collective-permute-start | bytes 393224 | tf_op jit(solution)/shard_map/ppermute | solution.py:25
  33.3 2.3 %collective-permute-done.4.rest_0_ = bf16[4,256,128]{2,1,0:T(8,128)(2,1)S(1)} collective-permute-done((bf16[4,256,128]{2,1,0:T(8,128)(2,1)S(1)}, bf16[4,256,128]{2,1,0:T(8,128)(2,1)S(1)}, u32[]{:S(2)}, u32[]{:S(2)}) %collective-permute-start.4) | collective-permute-done | bytes 262176 | tf_op jit(solution)/shard_map/ppermute | solution.py:30
  35.6 5.4 %forward_next.1.before = f32[2,512,128]{2,1,0:T(8,128)S(1)} custom-call(s32[48]{0:T(128)S(1)} %get-tuple-element.31.members, s32[48]{0:T(128)S(1)} %get-tuple-element.32.units, s32[48]{0:T(128)S(1)} %get-tuple-element.33.firsts, bf16[48,512,256]{2,1,0:T(8,128)(2,1)} %blocks.7, f32[2,512,128]{2,1,0:T(8,128)S(1)} %forward_first.1.before, ...), custom_call_target="tpu_custom_call" | custom-call | flops 1 | bytes 1 | tf_op jit(solution)/shard_map/forward_next/pallas_call | solution.py:344
  41.0 3.4 %forward_last.1 = (f32[2,256,128]{2,1,0:T(8,128)S(1)}, f32[2,256,128]{2,1,0:T(8,128)S(1)}) custom-call(s32[2]{0:T(128)S(1)} %pad_add_fusion.place, s32[48]{0:T(128)S(1)} %get-tuple-element.31.members, s32[48]{0:T(128)S(1)} %get-tuple-element.32.units, s32[48]{0:T(128)S(1)} %get-tuple-element.33.firsts, bf16[48,512,256]{2,1,0:T(8,128)(2,1)} %blocks.7, ...), custom_call_target="tpu_custom_call" | custom-call | flops 1 | bytes 1 | tf_op jit(solution)/shard_map/forward_last/pallas_call | solution.py:356
  44.6 1.5 %collective-permute-done.11.other = f32[2,256,128]{2,1,0:T(8,128)S(1)} collective-permute-done((f32[2,256,128]{2,1,0:T(8,128)S(1)}, f32[2,256,128]{2,1,0:T(8,128)S(1)}, u32[]{:S(2)}, u32[]{:S(2)}) %collective-permute-start.11) | collective-permute-done | bytes 262176 | tf_op jit(solution)/shard_map/ppermute | solution.py:30
  46.1 0.5 gram.1
  46.7 1.1 %collective-permute-done.12 = f32[72,128]{1,0:T(8,128)S(1)} collective-permute-done((f32[72,128]{1,0:T(8,128)S(1)}, f32[72,128]{1,0:T(8,128)S(1)}, u32[]{:S(2)}, u32[]{:S(2)}) %collective-permute-start.12) | collective-permute-done | bytes 36896 | tf_op jit(solution)/shard_map/ppermute | solution.py:30
  47.8 2.4 %collective-permute-start.13 = (f32[72,128]{1,0:T(8,128)S(1)}, f32[72,128]{1,0:T(8,128)S(1)}, u32[]{:S(2)}, u32[]{:S(2)}) collective-permute-start(f32[72,128]{1,0:T(8,128)S(1)} %add.50), channel_id=1, source_target_pairs={{0,2},{2,0},{4,6},{6,4},{8,10},{10,8},{12,14},{14,12},{16,18},{18,... | collective-permute-start | bytes 110600 | tf_op jit(solution)/shard_map/ppermute | solution.py:30
  50.2 1.5 %collective-permute-start.15 = (f32[72,128]{1,0:T(8,128)S(1)}, f32[72,128]{1,0:T(8,128)S(1)}, u32[]{:S(2)}, u32[]{:S(2)}) collective-permute-start(f32[72,128]{1,0:T(8,128)S(1)} %add.50), channel_id=1, source_target_pairs={{0,6},{2,4},{4,2},{6,0},{8,14},{10,12},{12,10},{14,8},{16,22},{18,... | collective-permute-start | bytes 110600 | tf_op jit(solution)/shard_map/ppermute | solution.py:30
  51.7 0.4 collective-permute-done.13
  52.1 2.2 %collective-permute-done.14 = f32[72,128]{1,0:T(8,128)S(1)} collective-permute-done((f32[72,128]{1,0:T(8,128)S(1)}, f32[72,128]{1,0:T(8,128)S(1)}, u32[]{:S(2)}, u32[]{:S(2)}) %collective-permute-start.14) | collective-permute-done | bytes 36896 | tf_op jit(solution)/shard_map/ppermute | solution.py:30
  54.4 0.7 %collective-permute-done.15 = f32[72,128]{1,0:T(8,128)S(1)} collective-permute-done((f32[72,128]{1,0:T(8,128)S(1)}, f32[72,128]{1,0:T(8,128)S(1)}, u32[]{:S(2)}, u32[]{:S(2)}) %collective-permute-start.15) | collective-permute-done | bytes 36896 | tf_op jit(solution)/shard_map/ppermute | solution.py:30
  55.1 0.4 collective-permute-start.16
  55.5 1.9 %collective-permute-start.17 = (f32[72,128]{1,0:T(8,128)S(1)}, f32[72,128]{1,0:T(8,128)S(1)}, u32[]{:S(2)}, u32[]{:S(2)}) collective-permute-start(f32[72,128]{1,0:T(8,128)S(1)} %add_add_fusion.rest_0_), channel_id=1, source_target_pairs={{0,16},{2,18},{4,20},{6,22},{8,24},{10,26},{12,28},{14,30},{16,0},... | collective-permute-start | bytes 110600 | tf_op jit(solution)/shard_map/ppermute | solution.py:30
  57.4 2.1 %collective-permute-start.18 = (f32[72,128]{1,0:T(8,128)S(1)}, f32[72,128]{1,0:T(8,128)S(1)}, u32[]{:S(2)}, u32[]{:S(2)}) collective-permute-start(f32[72,128]{1,0:T(8,128)S(1)} %add_add_fusion.rest_0_), channel_id=1, source_target_pairs={{0,24},{2,26},{4,28},{6,30},{8,16},{10,18},{12,20},{14,22},{16,8},... | collective-permute-start | bytes 110600 | tf_op jit(solution)/shard_map/ppermute | solution.py:30
  59.5 1.2 %collective-permute-done.17.rest_2_ = f32[72,128]{1,0:T(8,128)S(1)} collective-permute-done((f32[72,128]{1,0:T(8,128)S(1)}, f32[72,128]{1,0:T(8,128)S(1)}, u32[]{:S(2)}, u32[]{:S(2)}) %collective-permute-start.17) | collective-permute-done | bytes 36896 | tf_op jit(solution)/shard_map/ppermute | solution.py:30
  60.8 2.4 %collective-permute-done.18.rest_3_ = f32[72,128]{1,0:T(8,128)S(1)} collective-permute-done((f32[72,128]{1,0:T(8,128)S(1)}, f32[72,128]{1,0:T(8,128)S(1)}, u32[]{:S(2)}, u32[]{:S(2)}) %collective-permute-start.18) | collective-permute-done | bytes 36896 | tf_op jit(solution)/shard_map/ppermute | solution.py:30
  63.2 5.3 %solve.1 = f32[2,256,128]{2,1,0:T(8,128)} custom-call(f32[72,128]{1,0:T(8,128)S(1)} %add_add_fusion.rest_0_, f32[72,128]{1,0:T(8,128)S(1)} %collective-permute-done.16.rest_1_, f32[72,128]{1,0:T(8,128)S(1)} %collective-permute-done.17.rest_2_, f32[72,128]{1,0:T(8,128)S(1)} %collective-permute-done.18.rest_3_, f32[2,256,128]{2,1,0:T(8,128)S(1)} %get-tuple-element.52.rest_4_), custom_call_target="tpu_custom_call" | custom-call | tf_op jit(solution)/shard_map/solve/pallas_call | solution.py:385
  (28 shorter events, 0.6 us)
Async XLA Ops:
  0.7 1.0 %copy-start = (f32[2,256,128]{2,1,0:T(8,128)S(1)}, f32[2,256,128]{2,1,0:T(8,128)}, u32[]{:S(2)}) copy-start(f32[2,256,128]{2,1,0:T(8,128)} %panels.3) | copy-start | bytes 786436
  1.6 0.7 copy-start.2
  2.4 5.1 %collective-permute-start = (bf16[2,256,128]{2,1,0:T(8,128)(2,1)S(1)}, bf16[2,256,128]{2,1,0:T(8,128)(2,1)S(1)}, u32[]{:S(2)}, u32[]{:S(2)}) collective-permute-start(bf16[2,256,128]{2,1,0:T(8,128)(2,1)S(1)} %get-tuple-element.40.near), channel_id=1, source_target_pairs={{0,1},{1,0},{2,3},{3,2},{4,5},{5,4},{6,7},{7,6},{8,9},{9,8},{10,11... | collective-permute-start | bytes 393224 | tf_op jit(solution)/shard_map/ppermute | solution.py:30
  2.8 14.3 %collective-permute-start.1 = (bf16[2,256,128]{2,1,0:T(8,128)(2,1)S(1)}, bf16[2,256,128]{2,1,0:T(8,128)(2,1)S(1)}, u32[]{:S(2)}, u32[]{:S(2)}) collective-permute-start(bf16[2,256,128]{2,1,0:T(8,128)(2,1)S(1)} %get-tuple-element.40.near), channel_id=1, source_target_pairs={{0,24},{2,26},{4,28},{6,30},{8,0},{10,2},{12,4},{14,6},{16,8},{18,... | collective-permute-start | bytes 393224 | tf_op jit(solution)/shard_map/ppermute | solution.py:25
  7.5 9.6 %collective-permute-start.2 = (bf16[2,256,128]{2,1,0:T(8,128)(2,1)S(1)}, bf16[2,256,128]{2,1,0:T(8,128)(2,1)S(1)}, u32[]{:S(2)}, u32[]{:S(2)}) collective-permute-start(bf16[2,256,128]{2,1,0:T(8,128)(2,1)S(1)} %get-tuple-element.40.near), channel_id=1, source_target_pairs={{0,16},{2,18},{4,20},{6,22},{8,24},{10,26},{12,28},{14,30},{16,0},... | collective-permute-start | bytes 393224 | tf_op jit(solution)/shard_map/ppermute | solution.py:25
  13.5 10.3 %collective-permute-start.3 = (bf16[4,256,128]{2,1,0:T(8,128)(2,1)S(1)}, bf16[4,256,128]{2,1,0:T(8,128)(2,1)S(1)}, u32[]{:S(2)}, u32[]{:S(2)}) collective-permute-start(bf16[4,256,128]{2,1,0:T(8,128)(2,1)S(1)} %get-tuple-element.38), channel_id=1, source_target_pairs={{0,4},{2,6},{4,0},{6,2},{8,12},{10,14},{12,8},{14,10},{16,20},{18,... | collective-permute-start | bytes 786440 | tf_op jit(solution)/shard_map/ppermute | solution.py:30
  15.1 10.9 %collective-permute-start.7 = (bf16[4,256,128]{2,1,0:T(8,128)(2,1)S(1)}, bf16[4,256,128]{2,1,0:T(8,128)(2,1)S(1)}, u32[]{:S(2)}, u32[]{:S(2)}) collective-permute-start(bf16[4,256,128]{2,1,0:T(8,128)(2,1)S(1)} %get-tuple-element.43), channel_id=1, source_target_pairs={{0,2},{2,0},{4,6},{6,4},{8,10},{10,8},{12,14},{14,12},{16,18},{18,... | collective-permute-start | bytes 786440 | tf_op jit(solution)/shard_map/ppermute | solution.py:30
  16.6 13.3 %collective-permute-start.8 = (bf16[4,256,128]{2,1,0:T(8,128)(2,1)S(1)}, bf16[4,256,128]{2,1,0:T(8,128)(2,1)S(1)}, u32[]{:S(2)}, u32[]{:S(2)}) collective-permute-start(bf16[4,256,128]{2,1,0:T(8,128)(2,1)S(1)} %get-tuple-element.44), channel_id=1, source_target_pairs={{0,6},{2,4},{4,2},{6,0},{8,14},{10,12},{12,10},{14,8},{16,22},{18,... | collective-permute-start | bytes 786440 | tf_op jit(solution)/shard_map/ppermute | solution.py:30
  17.3 18.3 %collective-permute-start.4 = (bf16[4,256,128]{2,1,0:T(8,128)(2,1)S(1)}, bf16[4,256,128]{2,1,0:T(8,128)(2,1)S(1)}, u32[]{:S(2)}, u32[]{:S(2)}) collective-permute-start(bf16[4,256,128]{2,1,0:T(8,128)(2,1)S(1)} %get-tuple-element.57), channel_id=1, source_target_pairs={{0,2},{2,0},{4,6},{6,4},{8,10},{10,8},{12,14},{14,12},{16,18},{18,... | collective-permute-start | bytes 786440 | tf_op jit(solution)/shard_map/ppermute | solution.py:30
  18.8 16.8 %collective-permute-start.5 = (bf16[4,256,128]{2,1,0:T(8,128)(2,1)S(1)}, bf16[4,256,128]{2,1,0:T(8,128)(2,1)S(1)}, u32[]{:S(2)}, u32[]{:S(2)}) collective-permute-start(bf16[4,256,128]{2,1,0:T(8,128)(2,1)S(1)} %get-tuple-element.56), channel_id=1, source_target_pairs={{0,4},{2,6},{4,0},{6,2},{8,12},{10,14},{12,8},{14,10},{16,20},{18,... | collective-permute-start | bytes 786440 | tf_op jit(solution)/shard_map/ppermute | solution.py:30
  20.3 20.7 %copy-start.1 = (f32[2,256,128]{2,1,0:T(8,128)S(1)}, f32[2,256,128]{2,1,0:T(8,128)}, u32[]{:S(2)}) copy-start(f32[2,256,128]{2,1,0:T(8,128)} %panels.3) | copy-start | bytes 786436
  23.9 17.1 %collective-permute-start.6 = (bf16[4,256,128]{2,1,0:T(8,128)(2,1)S(1)}, bf16[4,256,128]{2,1,0:T(8,128)(2,1)S(1)}, u32[]{:S(2)}, u32[]{:S(2)}) collective-permute-start(bf16[4,256,128]{2,1,0:T(8,128)(2,1)S(1)} %maximum_select_fusion), channel_id=1, source_target_pairs={{0,6},{2,4},{4,2},{6,0},{8,14},{10,12},{12,10},{14,8},{16,22},{18,... | collective-permute-start | bytes 786440 | tf_op jit(solution)/shard_map/ppermute | solution.py:30
  30.2 10.9 %collective-permute-start.10 = (bf16[2,256,128]{2,1,0:T(8,128)(2,1)S(1)}, bf16[2,256,128]{2,1,0:T(8,128)(2,1)S(1)}, u32[]{:S(2)}, u32[]{:S(2)}) collective-permute-start(bf16[2,256,128]{2,1,0:T(8,128)(2,1)S(1)} %get-tuple-element.53), channel_id=1, source_target_pairs={{0,16},{2,18},{4,20},{6,22},{8,24},{10,26},{12,28},{14,30},{16,0},... | collective-permute-start | bytes 393224 | tf_op jit(solution)/shard_map/ppermute | solution.py:25
  33.2 7.8 %collective-permute-start.9 = (bf16[2,256,128]{2,1,0:T(8,128)(2,1)S(1)}, bf16[2,256,128]{2,1,0:T(8,128)(2,1)S(1)}, u32[]{:S(2)}, u32[]{:S(2)}) collective-permute-start(bf16[2,256,128]{2,1,0:T(8,128)(2,1)S(1)} %get-tuple-element.54), channel_id=1, source_target_pairs={{0,8},{2,10},{4,12},{6,14},{8,16},{10,18},{12,20},{14,22},{16,24},... | collective-permute-start | bytes 393224 | tf_op jit(solution)/shard_map/ppermute | solution.py:25
  44.5 1.6 %collective-permute-start.11 = (f32[2,256,128]{2,1,0:T(8,128)S(1)}, f32[2,256,128]{2,1,0:T(8,128)S(1)}, u32[]{:S(2)}, u32[]{:S(2)}) collective-permute-start(f32[2,256,128]{2,1,0:T(8,128)S(1)} %get-tuple-element.47), channel_id=1, source_target_pairs={{0,1},{1,0},{2,3},{3,2},{4,5},{5,4},{6,7},{7,6},{8,9},{9,8},{10,11... | collective-permute-start | bytes 786440 | tf_op jit(solution)/shard_map/ppermute | solution.py:30
  46.6 1.2 %collective-permute-start.12 = (f32[72,128]{1,0:T(8,128)S(1)}, f32[72,128]{1,0:T(8,128)S(1)}, u32[]{:S(2)}, u32[]{:S(2)}) collective-permute-start(f32[72,128]{1,0:T(8,128)S(1)} %get-tuple-element.51), channel_id=1, source_target_pairs={{0,1},{1,0},{2,3},{3,2},{4,5},{5,4},{6,7},{7,6},{8,9},{9,8},{10,11... | collective-permute-start | bytes 110600 | tf_op jit(solution)/shard_map/ppermute | solution.py:30
  47.8 4.3 %collective-permute-start.13 = (f32[72,128]{1,0:T(8,128)S(1)}, f32[72,128]{1,0:T(8,128)S(1)}, u32[]{:S(2)}, u32[]{:S(2)}) collective-permute-start(f32[72,128]{1,0:T(8,128)S(1)} %add.50), channel_id=1, source_target_pairs={{0,2},{2,0},{4,6},{6,4},{8,10},{10,8},{12,14},{14,12},{16,18},{18,... | collective-permute-start | bytes 110600 | tf_op jit(solution)/shard_map/ppermute | solution.py:30
  50.2 4.2 %collective-permute-start.14 = (f32[72,128]{1,0:T(8,128)S(1)}, f32[72,128]{1,0:T(8,128)S(1)}, u32[]{:S(2)}, u32[]{:S(2)}) collective-permute-start(f32[72,128]{1,0:T(8,128)S(1)} %add.50), channel_id=1, source_target_pairs={{0,4},{2,6},{4,0},{6,2},{8,12},{10,14},{12,8},{14,10},{16,20},{18,... | collective-permute-start | bytes 110600 | tf_op jit(solution)/shard_map/ppermute | solution.py:30
  50.2 4.9 %collective-permute-start.15 = (f32[72,128]{1,0:T(8,128)S(1)}, f32[72,128]{1,0:T(8,128)S(1)}, u32[]{:S(2)}, u32[]{:S(2)}) collective-permute-start(f32[72,128]{1,0:T(8,128)S(1)} %add.50), channel_id=1, source_target_pairs={{0,6},{2,4},{4,2},{6,0},{8,14},{10,12},{12,10},{14,8},{16,22},{18,... | collective-permute-start | bytes 110600 | tf_op jit(solution)/shard_map/ppermute | solution.py:30
  55.1 4.5 %collective-permute-start.16 = (f32[72,128]{1,0:T(8,128)S(1)}, f32[72,128]{1,0:T(8,128)S(1)}, u32[]{:S(2)}, u32[]{:S(2)}) collective-permute-start(f32[72,128]{1,0:T(8,128)S(1)} %add_add_fusion.rest_0_), channel_id=1, source_target_pairs={{0,8},{2,10},{4,12},{6,14},{8,0},{10,2},{12,4},{14,6},{16,24},{18,... | collective-permute-start | bytes 110600 | tf_op jit(solution)/shard_map/ppermute | solution.py:30
  55.5 5.3 %collective-permute-start.17 = (f32[72,128]{1,0:T(8,128)S(1)}, f32[72,128]{1,0:T(8,128)S(1)}, u32[]{:S(2)}, u32[]{:S(2)}) collective-permute-start(f32[72,128]{1,0:T(8,128)S(1)} %add_add_fusion.rest_0_), channel_id=1, source_target_pairs={{0,16},{2,18},{4,20},{6,22},{8,24},{10,26},{12,28},{14,30},{16,0},... | collective-permute-start | bytes 110600 | tf_op jit(solution)/shard_map/ppermute | solution.py:30
  57.4 5.8 %collective-permute-start.18 = (f32[72,128]{1,0:T(8,128)S(1)}, f32[72,128]{1,0:T(8,128)S(1)}, u32[]{:S(2)}, u32[]{:S(2)}) collective-permute-start(f32[72,128]{1,0:T(8,128)S(1)} %add_add_fusion.rest_0_), channel_id=1, source_target_pairs={{0,24},{2,26},{4,28},{6,30},{8,16},{10,18},{12,20},{14,22},{16,8},... | collective-permute-start | bytes 110600 | tf_op jit(solution)/shard_map/ppermute | solution.py:30

commit v5 on v4

--- a/solution.py
+++ b/solution.py
@@ -94,9 +94,10 @@
             apart = lax.div(place_in, units)
             rank = filled[apart]
             filled[apart] = rank + jnp.where(alive, 1, 0)
-            members[apart * bucket + rank] = slot
-            units_of[apart * bucket + rank] = place_in - apart * units
-            firsts[apart * bucket + rank] = jnp.where(alive, first, img_dev)
+            target = jnp.where(alive, apart * bucket + rank, GROUP * bucket)
+            members[target] = slot
+            units_of[target] = place_in - apart * units
+            firsts[target] = first
             place_in = jnp.where(alive, place_in, GROUP * units)
             product = jnp.dot(turned[first], kept[slot], preferred_element_type=jnp.float32)
             total[place_in] += product.astype(jnp.bfloat16).astype(jnp.float32)
@@ -205,20 +206,19 @@
     shape = (ROWS, univ)
     row_ids = lax.broadcasted_iota(jnp.int32, shape, 0)
     column_ids = lax.broadcasted_iota(jnp.int32, shape, 1)
-    left = [inverse[pl.ds(b * ROWS, ROWS), :] for b in range(count)]
-    right = [
-        jnp.where(column_ids == row_ids + b * ROWS, 1.0, 0.0).astype(jnp.float32)
-        for b in range(count)
-    ]
+    held = [inverse[pl.ds(b * ROWS, ROWS), :] for b in range(count)]
 
     def spread(value, row):
         return jnp.broadcast_to(value[row : row + 1, :], shape)
 
     for b in range(count):
-        rows, tail = left[b], right[b]
+        rows = held[b]
         columns = [
             jnp.broadcast_to(rows[:, b * ROWS + j : b * ROWS + j + 1], shape) for j in range(ROWS)
         ]
+        done = column_ids < (b + 1) * ROWS
+        inside = done & (column_ids >= b * ROWS)
+        rows = jnp.where(inside, jnp.where(column_ids == row_ids + b * ROWS, 1.0, 0.0), rows)
         pivots = jnp.ones(shape, jnp.float32)
         for j in range(ROWS):
             pivot = spread(columns[j], j)
@@ -228,15 +228,15 @@
                 for k in range(j + 1, ROWS):
                     columns[k] = columns[k] - weight * spread(columns[k], j)
                 rows = rows - weight * spread(rows, j)
-                tail = tail - weight * spread(tail, j)
-        inverse[pl.ds(b * ROWS, ROWS), :] = tail * lax.rsqrt(pivots)
+        inverse[pl.ds(b * ROWS, ROWS), :] = jnp.where(done, rows * lax.rsqrt(pivots), 0.0)
         if b < count - 1:
             turned = (rows * (1.0 / pivots)).T
             for c in range(b + 1, count):
+                below = jnp.where(inside, 0.0, held[c])
                 for j in range(ROWS):
                     weight = jnp.broadcast_to(turned[c * ROWS : (c + 1) * ROWS, j : j + 1], shape)
-                    left[c] = left[c] - weight * spread(rows, j)
-                    right[c] = right[c] - weight * spread(tail, j)
+                    below = below - weight * spread(rows, j)
+                held[c] = below
     inverse_high, inverse_low = split(inverse[...].T)
     wide = jnp.concatenate([inverse_high, inverse_low], axis=1)
     for image in range(field.shape[0]):
@@ -277,7 +277,7 @@
         in_specs=[anywhere] + [VMEM] * 2 + [anywhere],
         out_specs=[VMEM] * GROUP + [SMEM] * 3,
         out_shape=[jax.ShapeDtypeStruct((units, cols, univ), jnp.bfloat16)] * GROUP
-        + [jax.ShapeDtypeStruct((GROUP * bucket,), jnp.int32)] * 3,
+        + [jax.ShapeDtypeStruct((GROUP * bucket + 1,), jnp.int32)] * 3,
         scratch_shapes=[
             pltpu.VMEM(blocks.shape, blocks.dtype),
             pltpu.VMEM((img_dev, univ, keypts), jnp.bfloat16),

time: 68.7 us -> 69.4 us (1.010); the launches traced: 68.6 us -> 68.4 us
  transfers between devices with their start and end apart: 19 -> 19, of which waited for: 9 -> 9; matrix products, arithmetic and copies ran while one was open for 1% -> 1% of each run, Pallas kernels for 22% -> 23%
where the time goes in v5:
time: 69.4 us; the launch traced here: 68.4 us
  starting transfers between devices  25.2 us (36%)
  Pallas kernels  24.9 us (36%)
  waiting for transfers between devices  15.4 us (22%)
  local copies, waits for them, and re-layouts  1.7 us (2%)
  between operations  0.8 us (1%)
    ppermute x15, starting transfers between devices, exchanged(): lax.ppermute(value, axis, [(source, source ^ bits) for source in range(co...  17.5 us
    ppermute x15, waiting for transfers between devices, exchanged(): lax.ppermute(value, axis, [(source, source ^ bits) for source in range(co...  15.4 us
    ppermute x4, starting transfers between devices, passed_along(): return lax.ppermute(value, axis, pairs)  7.69 us
    pallas_call x1, Pallas kernels, shards(): pl.pallas_call(functools.partial(reverse_kernel, per, devices), in_specs=...  6.04 us
    pallas_call x1, Pallas kernels, shards(): pl.pallas_call(functools.partial(forward_next_kernel, middle), in_specs=[...  5.78 us
    pallas_call x1, Pallas kernels, shards(): pl.pallas_call(functools.partial(solve_kernel, 1 / (devices * img_dev * k...  5.29 us
    pallas_call x1, Pallas kernels, shards(): pl.pallas_call(functools.partial(forward_last_kernel, late), in_specs=[SM...  3.63 us
    pallas_call x1, Pallas kernels, shards(): pl.pallas_call(functools.partial(forward_first_kernel, (0,)), in_specs=[S...  3.61 us
  transfers between devices with their start and end apart: 19, of which 9 were waited for; matrix products, arithmetic and copies ran while one was open for 1% of the time, Pallas kernels for 23%

profile of v5, /device:TPU:0, one launch (start us, length us, event | category | flops | bytes accessed | tf_op | source)
XLA Modules:
  0.0 68.4 jit_solution(6072450641029317163)
XLA Ops:
  0.7 0.9 %copy-done = f32[2,256,128]{2,1,0:T(8,128)S(1)} copy-done((f32[2,256,128]{2,1,0:T(8,128)S(1)}, f32[2,256,128]{2,1,0:T(8,128)}, u32[]{:S(2)}) %copy-start) | copy-done | bytes 262168
  1.6 0.7 copy-done.2
  2.4 0.5 collective-permute-start
  2.8 4.7 %collective-permute-start.1 = (bf16[2,256,128]{2,1,0:T(8,128)(2,1)S(1)}, bf16[2,256,128]{2,1,0:T(8,128)(2,1)S(1)}, u32[]{:S(2)}, u32[]{:S(2)}) collective-permute-start(bf16[2,256,128]{2,1,0:T(8,128)(2,1)S(1)} %get-tuple-element.40.near), channel_id=1, source_target_pairs={{0,24},{2,26},{4,28},{6,30},{8,0},{10,2},{12,4},{14,6},{16,8},{18,... | collective-permute-start | bytes 393224 | tf_op jit(solution)/shard_map/ppermute | solution.py:25
  7.5 6.0 %reverse.1 = (bf16[4,256,128]{2,1,0:T(8,128)(2,1)S(1)}, bf16[4,256,128]{2,1,0:T(8,128)(2,1)S(1)}, bf16[4,256,128]{2,1,0:T(8,128)(2,1)S(1)}, bf16[4,256,128]{2,1,...) custom-call(s32[8,48]{1,0:T(8,128)S(1)} %get-tuple-element.29.numbers, ...), custom_call_target="tpu_custom_call" | custom-call | flops 1 | bytes 1 | tf_op jit(solution)/shard_map/reverse/pallas_call | solution.py:275
  13.5 1.6 %collective-permute-start.3 = (bf16[4,256,128]{2,1,0:T(8,128)(2,1)S(1)}, bf16[4,256,128]{2,1,0:T(8,128)(2,1)S(1)}, u32[]{:S(2)}, u32[]{:S(2)}) collective-permute-start(bf16[4,256,128]{2,1,0:T(8,128)(2,1)S(1)} %get-tuple-element.38), channel_id=1, source_target_pairs={{0,4},{2,6},{4,0},{6,2},{8,12},{10,14},{12,8},{14,10},{16,20},{18,... | collective-permute-start | bytes 786440 | tf_op jit(solution)/shard_map/ppermute | solution.py:30
  15.1 1.5 %collective-permute-start.7 = (bf16[4,256,128]{2,1,0:T(8,128)(2,1)S(1)}, bf16[4,256,128]{2,1,0:T(8,128)(2,1)S(1)}, u32[]{:S(2)}, u32[]{:S(2)}) collective-permute-start(bf16[4,256,128]{2,1,0:T(8,128)(2,1)S(1)} %get-tuple-element.43), channel_id=1, source_target_pairs={{0,2},{2,0},{4,6},{6,4},{8,10},{10,8},{12,14},{14,12},{16,18},{18,... | collective-permute-start | bytes 786440 | tf_op jit(solution)/shard_map/ppermute | solution.py:30
  16.6 0.5 collective-permute-start.8
  17.3 1.6 %collective-permute-start.4 = (bf16[4,256,128]{2,1,0:T(8,128)(2,1)S(1)}, bf16[4,256,128]{2,1,0:T(8,128)(2,1)S(1)}, u32[]{:S(2)}, u32[]{:S(2)}) collective-permute-start(bf16[4,256,128]{2,1,0:T(8,128)(2,1)S(1)} %get-tuple-element.57), channel_id=1, source_target_pairs={{0,2},{2,0},{4,6},{6,4},{8,10},{10,8},{12,14},{14,12},{16,18},{18,... | collective-permute-start | bytes 786440 | tf_op jit(solution)/shard_map/ppermute | solution.py:30
  18.8 1.5 %collective-permute-start.5 = (bf16[4,256,128]{2,1,0:T(8,128)(2,1)S(1)}, bf16[4,256,128]{2,1,0:T(8,128)(2,1)S(1)}, u32[]{:S(2)}, u32[]{:S(2)}) collective-permute-start(bf16[4,256,128]{2,1,0:T(8,128)(2,1)S(1)} %get-tuple-element.56), channel_id=1, source_target_pairs={{0,4},{2,6},{4,0},{6,2},{8,12},{10,14},{12,8},{14,10},{16,20},{18,... | collective-permute-start | bytes 786440 | tf_op jit(solution)/shard_map/ppermute | solution.py:30
  20.3 3.6 %forward_first.1.before = f32[2,512,128]{2,1,0:T(8,128)S(1)} custom-call(s32[49]{0:T(128)S(1)} %get-tuple-element.31.members, s32[49]{0:T(128)S(1)} %get-tuple-element.32.units, s32[49]{0:T(128)S(1)} %get-tuple-element.33.firsts, bf16[48,512,256]{2,1,0:T(8,128)(2,1)} %blocks.7, bf16[4,256,128]{2,1,0:T(8,128)(2,1)S(1)} %constant_dynamic-update-slice_fusion.rest_0_), custom_call_target="tpu_custom_call" | custom-call | flops 1 | bytes 1 | tf_op jit(solution)/shard_map/forward_first/pallas_call | solution.py:326
  24.0 2.0 %collective-permute-start.6 = (bf16[4,256,128]{2,1,0:T(8,128)(2,1)S(1)}, bf16[4,256,128]{2,1,0:T(8,128)(2,1)S(1)}, u32[]{:S(2)}, u32[]{:S(2)}) collective-permute-start(bf16[4,256,128]{2,1,0:T(8,128)(2,1)S(1)} %maximum_select_fusion), channel_id=1, source_target_pairs={{0,6},{2,4},{4,2},{6,0},{8,14},{10,12},{12,10},{14,8},{16,22},{18,... | collective-permute-start | bytes 786440 | tf_op jit(solution)/shard_map/ppermute | solution.py:30
  26.0 3.9 %collective-permute-done.8 = bf16[4,256,128]{2,1,0:T(8,128)(2,1)S(1)} collective-permute-done((bf16[4,256,128]{2,1,0:T(8,128)(2,1)S(1)}, bf16[4,256,128]{2,1,0:T(8,128)(2,1)S(1)}, u32[]{:S(2)}, u32[]{:S(2)}) %collective-permute-start.8) | collective-permute-done | bytes 262176 | tf_op jit(solution)/shard_map/ppermute | solution.py:30
  29.9 0.2 fusion.9
  30.2 3.0 %collective-permute-start.10 = (bf16[2,256,128]{2,1,0:T(8,128)(2,1)S(1)}, bf16[2,256,128]{2,1,0:T(8,128)(2,1)S(1)}, u32[]{:S(2)}, u32[]{:S(2)}) collective-permute-start(bf16[2,256,128]{2,1,0:T(8,128)(2,1)S(1)} %get-tuple-element.53), channel_id=1, source_target_pairs={{0,16},{2,18},{4,20},{6,22},{8,24},{10,26},{12,28},{14,30},{16,0},... | collective-permute-start | bytes 393224 | tf_op jit(solution)/shard_map/ppermute | solution.py:25
  33.3 2.3 %collective-permute-done.4.rest_0_ = bf16[4,256,128]{2,1,0:T(8,128)(2,1)S(1)} collective-permute-done((bf16[4,256,128]{2,1,0:T(8,128)(2,1)S(1)}, bf16[4,256,128]{2,1,0:T(8,128)(2,1)S(1)}, u32[]{:S(2)}, u32[]{:S(2)}) %collective-permute-start.4) | collective-permute-done | bytes 262176 | tf_op jit(solution)/shard_map/ppermute | solution.py:30
  35.6 5.8 %forward_next.1.before = f32[2,512,128]{2,1,0:T(8,128)S(1)} custom-call(s32[49]{0:T(128)S(1)} %get-tuple-element.31.members, s32[49]{0:T(128)S(1)} %get-tuple-element.32.units, s32[49]{0:T(128)S(1)} %get-tuple-element.33.firsts, bf16[48,512,256]{2,1,0:T(8,128)(2,1)} %blocks.7, f32[2,512,128]{2,1,0:T(8,128)S(1)} %forward_first.1.before, ...), custom_call_target="tpu_custom_call" | custom-call | flops 1 | bytes 1 | tf_op jit(solution)/shard_map/forward_next/pallas_call | solution.py:344
  41.4 3.6 %forward_last.1 = (f32[2,256,128]{2,1,0:T(8,128)S(1)}, f32[2,256,128]{2,1,0:T(8,128)S(1)}) custom-call(s32[2]{0:T(128)S(1)} %pad_add_fusion.place, s32[49]{0:T(128)S(1)} %get-tuple-element.31.members, s32[49]{0:T(128)S(1)} %get-tuple-element.32.units, s32[49]{0:T(128)S(1)} %get-tuple-element.33.firsts, bf16[48,512,256]{2,1,0:T(8,128)(2,1)} %blocks.7, ...), custom_call_target="tpu_custom_call" | custom-call | flops 1 | bytes 1 | tf_op jit(solution)/shard_map/forward_last/pallas_call | solution.py:356
  45.2 1.5 %collective-permute-done.11.other = f32[2,256,128]{2,1,0:T(8,128)S(1)} collective-permute-done((f32[2,256,128]{2,1,0:T(8,128)S(1)}, f32[2,256,128]{2,1,0:T(8,128)S(1)}, u32[]{:S(2)}, u32[]{:S(2)}) %collective-permute-start.11) | collective-permute-done | bytes 262176 | tf_op jit(solution)/shard_map/ppermute | solution.py:30
  46.7 0.5 gram.1
  47.3 1.1 %collective-permute-done.12 = f32[72,128]{1,0:T(8,128)S(1)} collective-permute-done((f32[72,128]{1,0:T(8,128)S(1)}, f32[72,128]{1,0:T(8,128)S(1)}, u32[]{:S(2)}, u32[]{:S(2)}) %collective-permute-start.12) | collective-permute-done | bytes 36896 | tf_op jit(solution)/shard_map/ppermute | solution.py:30
  48.4 2.2 %collective-permute-start.13 = (f32[72,128]{1,0:T(8,128)S(1)}, f32[72,128]{1,0:T(8,128)S(1)}, u32[]{:S(2)}, u32[]{:S(2)}) collective-permute-start(f32[72,128]{1,0:T(8,128)S(1)} %add.50), channel_id=1, source_target_pairs={{0,2},{2,0},{4,6},{6,4},{8,10},{10,8},{12,14},{14,12},{16,18},{18,... | collective-permute-start | bytes 110600 | tf_op jit(solution)/shard_map/ppermute | solution.py:30
  50.6 1.5 %collective-permute-start.15 = (f32[72,128]{1,0:T(8,128)S(1)}, f32[72,128]{1,0:T(8,128)S(1)}, u32[]{:S(2)}, u32[]{:S(2)}) collective-permute-start(f32[72,128]{1,0:T(8,128)S(1)} %add.50), channel_id=1, source_target_pairs={{0,6},{2,4},{4,2},{6,0},{8,14},{10,12},{12,10},{14,8},{16,22},{18,... | collective-permute-start | bytes 110600 | tf_op jit(solution)/shard_map/ppermute | solution.py:30
  52.1 0.4 collective-permute-done.13
  52.5 2.2 %collective-permute-done.14 = f32[72,128]{1,0:T(8,128)S(1)} collective-permute-done((f32[72,128]{1,0:T(8,128)S(1)}, f32[72,128]{1,0:T(8,128)S(1)}, u32[]{:S(2)}, u32[]{:S(2)}) %collective-permute-start.14) | collective-permute-done | bytes 36896 | tf_op jit(solution)/shard_map/ppermute | solution.py:30
  54.8 0.7 %collective-permute-done.15 = f32[72,128]{1,0:T(8,128)S(1)} collective-permute-done((f32[72,128]{1,0:T(8,128)S(1)}, f32[72,128]{1,0:T(8,128)S(1)}, u32[]{:S(2)}, u32[]{:S(2)}) %collective-permute-start.15) | collective-permute-done | bytes 36896 | tf_op jit(solution)/shard_map/ppermute | solution.py:30
  55.5 1.7 %collective-permute-start.16 = (f32[72,128]{1,0:T(8,128)S(1)}, f32[72,128]{1,0:T(8,128)S(1)}, u32[]{:S(2)}, u32[]{:S(2)}) collective-permute-start(f32[72,128]{1,0:T(8,128)S(1)} %add_add_fusion.rest_0_), channel_id=1, source_target_pairs={{0,8},{2,10},{4,12},{6,14},{8,0},{10,2},{12,4},{14,6},{16,24},{18,... | collective-permute-start | bytes 110600 | tf_op jit(solution)/shard_map/ppermute | solution.py:30
  57.1 0.2 collective-permute-start.17
  57.4 2.6 %collective-permute-start.18 = (f32[72,128]{1,0:T(8,128)S(1)}, f32[72,128]{1,0:T(8,128)S(1)}, u32[]{:S(2)}, u32[]{:S(2)}) collective-permute-start(f32[72,128]{1,0:T(8,128)S(1)} %add_add_fusion.rest_0_), channel_id=1, source_target_pairs={{0,24},{2,26},{4,28},{6,30},{8,16},{10,18},{12,20},{14,22},{16,8},... | collective-permute-start | bytes 110600 | tf_op jit(solution)/shard_map/ppermute | solution.py:30
  59.9 2.3 %collective-permute-done.17.rest_2_ = f32[72,128]{1,0:T(8,128)S(1)} collective-permute-done((f32[72,128]{1,0:T(8,128)S(1)}, f32[72,128]{1,0:T(8,128)S(1)}, u32[]{:S(2)}, u32[]{:S(2)}) %collective-permute-start.17) | collective-permute-done | bytes 36896 | tf_op jit(solution)/shard_map/ppermute | solution.py:30
  62.3 0.9 %collective-permute-done.18.rest_3_ = f32[72,128]{1,0:T(8,128)S(1)} collective-permute-done((f32[72,128]{1,0:T(8,128)S(1)}, f32[72,128]{1,0:T(8,128)S(1)}, u32[]{:S(2)}, u32[]{:S(2)}) %collective-permute-start.18) | collective-permute-done | bytes 36896 | tf_op jit(solution)/shard_map/ppermute | solution.py:30
  63.1 5.3 %solve.1 = f32[2,256,128]{2,1,0:T(8,128)} custom-call(f32[72,128]{1,0:T(8,128)S(1)} %add_add_fusion.rest_0_, f32[72,128]{1,0:T(8,128)S(1)} %collective-permute-done.16.rest_1_, f32[72,128]{1,0:T(8,128)S(1)} %collective-permute-done.17.rest_2_, f32[72,128]{1,0:T(8,128)S(1)} %collective-permute-done.18.rest_3_, f32[2,256,128]{2,1,0:T(8,128)S(1)} %get-tuple-element.52.rest_4_), custom_call_target="tpu_custom_call" | custom-call | tf_op jit(solution)/shard_map/solve/pallas_call | solution.py:385
  (28 shorter events, 0.6 us)
Async XLA Ops:
  0.7 1.0 %copy-start = (f32[2,256,128]{2,1,0:T(8,128)S(1)}, f32[2,256,128]{2,1,0:T(8,128)}, u32[]{:S(2)}) copy-start(f32[2,256,128]{2,1,0:T(8,128)} %panels.3) | copy-start | bytes 786436
  1.6 0.7 copy-start.2
  2.4 5.1 %collective-permute-start = (bf16[2,256,128]{2,1,0:T(8,128)(2,1)S(1)}, bf16[2,256,128]{2,1,0:T(8,128)(2,1)S(1)}, u32[]{:S(2)}, u32[]{:S(2)}) collective-permute-start(bf16[2,256,128]{2,1,0:T(8,128)(2,1)S(1)} %get-tuple-element.40.near), channel_id=1, source_target_pairs={{0,1},{1,0},{2,3},{3,2},{4,5},{5,4},{6,7},{7,6},{8,9},{9,8},{10,11... | collective-permute-start | bytes 393224 | tf_op jit(solution)/shard_map/ppermute | solution.py:30
  2.8 14.3 %collective-permute-start.1 = (bf16[2,256,128]{2,1,0:T(8,128)(2,1)S(1)}, bf16[2,256,128]{2,1,0:T(8,128)(2,1)S(1)}, u32[]{:S(2)}, u32[]{:S(2)}) collective-permute-start(bf16[2,256,128]{2,1,0:T(8,128)(2,1)S(1)} %get-tuple-element.40.near), channel_id=1, source_target_pairs={{0,24},{2,26},{4,28},{6,30},{8,0},{10,2},{12,4},{14,6},{16,8},{18,... | collective-permute-start | bytes 393224 | tf_op jit(solution)/shard_map/ppermute | solution.py:25
  7.5 9.6 %collective-permute-start.2 = (bf16[2,256,128]{2,1,0:T(8,128)(2,1)S(1)}, bf16[2,256,128]{2,1,0:T(8,128)(2,1)S(1)}, u32[]{:S(2)}, u32[]{:S(2)}) collective-permute-start(bf16[2,256,128]{2,1,0:T(8,128)(2,1)S(1)} %get-tuple-element.40.near), channel_id=1, source_target_pairs={{0,16},{2,18},{4,20},{6,22},{8,24},{10,26},{12,28},{14,30},{16,0},... | collective-permute-start | bytes 393224 | tf_op jit(solution)/shard_map/ppermute | solution.py:25
  13.5 10.4 %collective-permute-start.3 = (bf16[4,256,128]{2,1,0:T(8,128)(2,1)S(1)}, bf16[4,256,128]{2,1,0:T(8,128)(2,1)S(1)}, u32[]{:S(2)}, u32[]{:S(2)}) collective-permute-start(bf16[4,256,128]{2,1,0:T(8,128)(2,1)S(1)} %get-tuple-element.38), channel_id=1, source_target_pairs={{0,4},{2,6},{4,0},{6,2},{8,12},{10,14},{12,8},{14,10},{16,20},{18,... | collective-permute-start | bytes 786440 | tf_op jit(solution)/shard_map/ppermute | solution.py:30
  15.1 10.9 %collective-permute-start.7 = (bf16[4,256,128]{2,1,0:T(8,128)(2,1)S(1)}, bf16[4,256,128]{2,1,0:T(8,128)(2,1)S(1)}, u32[]{:S(2)}, u32[]{:S(2)}) collective-permute-start(bf16[4,256,128]{2,1,0:T(8,128)(2,1)S(1)} %get-tuple-element.43), channel_id=1, source_target_pairs={{0,2},{2,0},{4,6},{6,4},{8,10},{10,8},{12,14},{14,12},{16,18},{18,... | collective-permute-start | bytes 786440 | tf_op jit(solution)/shard_map/ppermute | solution.py:30
  16.6 13.3 %collective-permute-start.8 = (bf16[4,256,128]{2,1,0:T(8,128)(2,1)S(1)}, bf16[4,256,128]{2,1,0:T(8,128)(2,1)S(1)}, u32[]{:S(2)}, u32[]{:S(2)}) collective-permute-start(bf16[4,256,128]{2,1,0:T(8,128)(2,1)S(1)} %get-tuple-element.44), channel_id=1, source_target_pairs={{0,6},{2,4},{4,2},{6,0},{8,14},{10,12},{12,10},{14,8},{16,22},{18,... | collective-permute-start | bytes 786440 | tf_op jit(solution)/shard_map/ppermute | solution.py:30
  17.3 18.3 %collective-permute-start.4 = (bf16[4,256,128]{2,1,0:T(8,128)(2,1)S(1)}, bf16[4,256,128]{2,1,0:T(8,128)(2,1)S(1)}, u32[]{:S(2)}, u32[]{:S(2)}) collective-permute-start(bf16[4,256,128]{2,1,0:T(8,128)(2,1)S(1)} %get-tuple-element.57), channel_id=1, source_target_pairs={{0,2},{2,0},{4,6},{6,4},{8,10},{10,8},{12,14},{14,12},{16,18},{18,... | collective-permute-start | bytes 786440 | tf_op jit(solution)/shard_map/ppermute | solution.py:30
  18.8 16.8 %collective-permute-start.5 = (bf16[4,256,128]{2,1,0:T(8,128)(2,1)S(1)}, bf16[4,256,128]{2,1,0:T(8,128)(2,1)S(1)}, u32[]{:S(2)}, u32[]{:S(2)}) collective-permute-start(bf16[4,256,128]{2,1,0:T(8,128)(2,1)S(1)} %get-tuple-element.56), channel_id=1, source_target_pairs={{0,4},{2,6},{4,0},{6,2},{8,12},{10,14},{12,8},{14,10},{16,20},{18,... | collective-permute-start | bytes 786440 | tf_op jit(solution)/shard_map/ppermute | solution.py:30
  20.3 21.1 %copy-start.1 = (f32[2,256,128]{2,1,0:T(8,128)S(1)}, f32[2,256,128]{2,1,0:T(8,128)}, u32[]{:S(2)}) copy-start(f32[2,256,128]{2,1,0:T(8,128)} %panels.3) | copy-start | bytes 786436
  24.0 17.4 %collective-permute-start.6 = (bf16[4,256,128]{2,1,0:T(8,128)(2,1)S(1)}, bf16[4,256,128]{2,1,0:T(8,128)(2,1)S(1)}, u32[]{:S(2)}, u32[]{:S(2)}) collective-permute-start(bf16[4,256,128]{2,1,0:T(8,128)(2,1)S(1)} %maximum_select_fusion), channel_id=1, source_target_pairs={{0,6},{2,4},{4,2},{6,0},{8,14},{10,12},{12,10},{14,8},{16,22},{18,... | collective-permute-start | bytes 786440 | tf_op jit(solution)/shard_map/ppermute | solution.py:30
  30.2 11.2 %collective-permute-start.10 = (bf16[2,256,128]{2,1,0:T(8,128)(2,1)S(1)}, bf16[2,256,128]{2,1,0:T(8,128)(2,1)S(1)}, u32[]{:S(2)}, u32[]{:S(2)}) collective-permute-start(bf16[2,256,128]{2,1,0:T(8,128)(2,1)S(1)} %get-tuple-element.53), channel_id=1, source_target_pairs={{0,16},{2,18},{4,20},{6,22},{8,24},{10,26},{12,28},{14,30},{16,0},... | collective-permute-start | bytes 393224 | tf_op jit(solution)/shard_map/ppermute | solution.py:25
  33.2 8.2 %collective-permute-start.9 = (bf16[2,256,128]{2,1,0:T(8,128)(2,1)S(1)}, bf16[2,256,128]{2,1,0:T(8,128)(2,1)S(1)}, u32[]{:S(2)}, u32[]{:S(2)}) collective-permute-start(bf16[2,256,128]{2,1,0:T(8,128)(2,1)S(1)} %get-tuple-element.54), channel_id=1, source_target_pairs={{0,8},{2,10},{4,12},{6,14},{8,16},{10,18},{12,20},{14,22},{16,24},... | collective-permute-start | bytes 393224 | tf_op jit(solution)/shard_map/ppermute | solution.py:25
  45.1 1.6 %collective-permute-start.11 = (f32[2,256,128]{2,1,0:T(8,128)S(1)}, f32[2,256,128]{2,1,0:T(8,128)S(1)}, u32[]{:S(2)}, u32[]{:S(2)}) collective-permute-start(f32[2,256,128]{2,1,0:T(8,128)S(1)} %get-tuple-element.47), channel_id=1, source_target_pairs={{0,1},{1,0},{2,3},{3,2},{4,5},{5,4},{6,7},{7,6},{8,9},{9,8},{10,11... | collective-permute-start | bytes 786440 | tf_op jit(solution)/shard_map/ppermute | solution.py:30
  47.1 1.2 %collective-permute-start.12 = (f32[72,128]{1,0:T(8,128)S(1)}, f32[72,128]{1,0:T(8,128)S(1)}, u32[]{:S(2)}, u32[]{:S(2)}) collective-permute-start(f32[72,128]{1,0:T(8,128)S(1)} %get-tuple-element.51), channel_id=1, source_target_pairs={{0,1},{1,0},{2,3},{3,2},{4,5},{5,4},{6,7},{7,6},{8,9},{9,8},{10,11... | collective-permute-start | bytes 110600 | tf_op jit(solution)/shard_map/ppermute | solution.py:30
  48.4 4.2 %collective-permute-start.13 = (f32[72,128]{1,0:T(8,128)S(1)}, f32[72,128]{1,0:T(8,128)S(1)}, u32[]{:S(2)}, u32[]{:S(2)}) collective-permute-start(f32[72,128]{1,0:T(8,128)S(1)} %add.50), channel_id=1, source_target_pairs={{0,2},{2,0},{4,6},{6,4},{8,10},{10,8},{12,14},{14,12},{16,18},{18,... | collective-permute-start | bytes 110600 | tf_op jit(solution)/shard_map/ppermute | solution.py:30
  50.6 4.2 %collective-permute-start.14 = (f32[72,128]{1,0:T(8,128)S(1)}, f32[72,128]{1,0:T(8,128)S(1)}, u32[]{:S(2)}, u32[]{:S(2)}) collective-permute-start(f32[72,128]{1,0:T(8,128)S(1)} %add.50), channel_id=1, source_target_pairs={{0,4},{2,6},{4,0},{6,2},{8,12},{10,14},{12,8},{14,10},{16,20},{18,... | collective-permute-start | bytes 110600 | tf_op jit(solution)/shard_map/ppermute | solution.py:30
  50.6 4.9 %collective-permute-start.15 = (f32[72,128]{1,0:T(8,128)S(1)}, f32[72,128]{1,0:T(8,128)S(1)}, u32[]{:S(2)}, u32[]{:S(2)}) collective-permute-start(f32[72,128]{1,0:T(8,128)S(1)} %add.50), channel_id=1, source_target_pairs={{0,6},{2,4},{4,2},{6,0},{8,14},{10,12},{12,10},{14,8},{16,22},{18,... | collective-permute-start | bytes 110600 | tf_op jit(solution)/shard_map/ppermute | solution.py:30
  55.5 4.5 %collective-permute-start.16 = (f32[72,128]{1,0:T(8,128)S(1)}, f32[72,128]{1,0:T(8,128)S(1)}, u32[]{:S(2)}, u32[]{:S(2)}) collective-permute-start(f32[72,128]{1,0:T(8,128)S(1)} %add_add_fusion.rest_0_), channel_id=1, source_target_pairs={{0,8},{2,10},{4,12},{6,14},{8,0},{10,2},{12,4},{14,6},{16,24},{18,... | collective-permute-start | bytes 110600 | tf_op jit(solution)/shard_map/ppermute | solution.py:30
  57.1 5.1 %collective-permute-start.17 = (f32[72,128]{1,0:T(8,128)S(1)}, f32[72,128]{1,0:T(8,128)S(1)}, u32[]{:S(2)}, u32[]{:S(2)}) collective-permute-start(f32[72,128]{1,0:T(8,128)S(1)} %add_add_fusion.rest_0_), channel_id=1, source_target_pairs={{0,16},{2,18},{4,20},{6,22},{8,24},{10,26},{12,28},{14,30},{16,0},... | collective-permute-start | bytes 110600 | tf_op jit(solution)/shard_map/ppermute | solution.py:30
  57.4 5.8 %collective-permute-start.18 = (f32[72,128]{1,0:T(8,128)S(1)}, f32[72,128]{1,0:T(8,128)S(1)}, u32[]{:S(2)}, u32[]{:S(2)}) collective-permute-start(f32[72,128]{1,0:T(8,128)S(1)} %add_add_fusion.rest_0_), channel_id=1, source_target_pairs={{0,24},{2,26},{4,28},{6,30},{8,16},{10,18},{12,20},{14,22},{16,8},... | collective-permute-start | bytes 110600 | tf_op jit(solution)/shard_map/ppermute | solution.py:30
